TPU v7x, 128 devices: a whole 4x4x4 slice. The times are simulated.
128 devices in a mesh: seq: 32 (over y, x, core), head: 4 (over z).
Axes of the slice: x: 4, y: 4, z: 4, core: 2. Of those that a mesh axis runs over, the one named last changes fastest.
Arguments:
- queries: bfloat16 [32768, 2048], P('seq', 'head'), may hold values from -6 to 6
- keys: bfloat16 [32768, 2048], P('seq', 'head'), may hold values from -100 to 100
- values: bfloat16 [32768, 2048], P('seq', 'head'), may hold values from -16 to 16
- gates: float32 [32768, 16], P('seq', 'head'), may hold values from 0.05 to 1
- ridge: float32 [16], P('head'), may hold values from 0.25 to 4
- out_weight: bfloat16 [2048, 2048], P(None, 'head'), may hold values from -0.125 to 0.125
Outputs:
- partial_out: bfloat16 [4, 32768, 2048], P('head', 'seq')
All inputs are finite; a program needn't handle non-finite values.
Results may differ from a plain program's by a relative error of at most 0.0049.
Values may be sent and summed in bfloat16 or wider, within the bound.
No kernel may reach another device: no remote copies, remote signals or barrier semaphores. Data moves between devices by JAX's collectives and lax.ppermute only.
A program may use at most 128 MiB of HBM per device.

v0:
```python
import functools
import jax
import jax.numpy as jnp
from jax import lax
from jax.experimental import pallas as pl
from jax.experimental.pallas import tpu as pltpu
from jax.sharding import PartitionSpec as P

HD = 128
SPAN = 128
ITERS = 8
EPS = 1e-06
F32 = jnp.float32
BF16 = jnp.bfloat16
F16 = jnp.float16
VMEM_LIMIT = 56 * 1024 * 1024


def two_terms(value):
    high = value.astype(BF16)
    return high, (value - high.astype(F32)).astype(BF16)


def dot(left, right):
    return jnp.dot(left, right, preferred_element_type=F32)


def dot_rows(left, right):
    return lax.dot_general(left, right, (((0,), (0,)), ((), ())), preferred_element_type=F32)


def key_norms(keys):
    return jnp.sum(keys * keys, axis=1, keepdims=True) + EPS


def head_cols(head):
    return slice(head * HD, (head + 1) * HD)


def totals_kernel(heads, core_ref, keys_ref, gates_ref, mine_ref, theirs_ref):
    core = core_ref[0]
    half = heads // 2
    for head in range(heads):
        block = keys_ref[:, head_cols(head)]
        keys = block.astype(F32)
        scaled = keys * (gates_ref[:, head : head + 1] / key_norms(keys))
        high, low = two_terms(scaled)
        product = dot_rows(block, jnp.concatenate([high, low], axis=1))
        gram = product[:, :HD] + product[:, HD:]

        @pl.when(core == head // half)
        def _():
            mine_ref[head % half] = gram

        @pl.when(core != head // half)
        def _():
            theirs_ref[head % half] = gram


def local_kernel(
    heads, blocks, keys_ref, values_ref, gates_ref, gram_ref, moment_ref, total_ref, gram_sum, moment_sum
):
    step = pl.program_id(0)

    @pl.when(step == 0)
    def _():
        gram_sum[...] = jnp.zeros_like(gram_sum)
        moment_sum[...] = jnp.zeros_like(moment_sum)

    for head in range(heads):
        block = keys_ref[:, head_cols(head)]
        keys = block.astype(F32)
        inverse = lax.rsqrt(key_norms(keys))
        gated = keys * (gates_ref[:, head : head + 1] * inverse)
        gram_high, gram_low = two_terms(gated * inverse)
        high, low = two_terms(gated)
        product = dot_rows(block, jnp.concatenate([gram_high, gram_low], axis=1))
        gram_ref[head, 0] = gram_sum[head]
        gram_sum[head] += product[:, :HD] + product[:, HD:]
        product = dot_rows(values_ref[:, head_cols(head)], jnp.concatenate([high, low], axis=1))
        moment_ref[head, 0] = moment_sum[head]
        moment_sum[head] += product[:, :HD] + product[:, HD:]

    @pl.when(step == blocks - 1)
    def _():
        total_ref[...] = moment_sum[...].astype(BF16)


def solve_kernel(
    heads,
    blocks,
    core_ref,
    ridge_ref,
    queries_ref,
    keys_ref,
    gates_ref,
    local_ref,
    keep_ref,
    got_ref,
    high_ref,
    low_ref,
    corr_ref,
    first,
    second,
    weights,
    xs,
    rs,
    ds,
    norms,
):
    core = core_ref[0]
    half = heads // 2
    row = lax.broadcasted_iota(jnp.int32, (SPAN, SPAN), 0)
    column = lax.broadcasted_iota(jnp.int32, (SPAN, SPAN), 1)
    causal = row <= column
    units = [(head, block) for block in range(blocks) for head in range(heads)]
    for unit, (head, block) in enumerate(units):
        rows = slice(block * SPAN, (block + 1) * SPAN)
        own = keys_ref[rows, head_cols(head)]
        keys = own.astype(F32)
        norm = key_norms(keys)
        weights[unit] = jnp.where(causal, gates_ref[rows, head : head + 1] / norm, 0.0)
        prior = jnp.where(core == head // half, keep_ref[head % half], got_ref[head % half])
        gram = prior + local_ref[head, block] + jnp.where(row == column, ridge_ref[head], 0.0)
        high, low = two_terms(gram)
        first[unit, :HD, :HD] = high
        first[unit, :HD, HD:] = high
        first[unit, HD:, :HD] = own
        first[unit, HD:, HD:] = own
        second[unit, :, :HD] = low
        second[unit, :, HD:] = keys.T.astype(BF16)
        query = queries_ref[rows, head_cols(head)].astype(F32).T
        query = query * lax.rsqrt(jnp.sum(query * query, axis=0, keepdims=True) + EPS)
        xs[unit] = jnp.zeros((HD, SPAN), F32)
        rs[unit] = query
        ds[unit] = query
        norms[unit] = jnp.broadcast_to(jnp.sum(query * query, axis=0, keepdims=True), (8, SPAN))

    def sweep_once(sweep, carry):
        for unit in range(len(units)):
            direction = ds[unit]
            now = norms[unit, :1]
            high, low = two_terms(direction)
            product = dot(first[unit], jnp.concatenate([high, low], axis=0))
            corr = (product[HD:] * weights[unit]).astype(BF16)
            image = product[:HD] + dot(second[unit], jnp.concatenate([high, corr], axis=0))
            step = now / (jnp.sum(direction * image, axis=0, keepdims=True) + EPS)
            xs[unit] += step * direction
            residual = rs[unit] - step * image
            rs[unit] = residual
            after = jnp.sum(residual * residual, axis=0, keepdims=True)
            ds[unit] = residual + (after / (now + EPS)) * direction
            norms[unit] = jnp.broadcast_to(after, (8, SPAN))
        return carry

    lax.fori_loop(0, ITERS, sweep_once, 0)
    for unit, (head, block) in enumerate(units):
        rows = slice(block * SPAN, (block + 1) * SPAN)
        high, low = two_terms(xs[unit])
        norm = key_norms(keys_ref[rows, head_cols(head)].astype(F32))
        corr = dot(first[unit, HD:], jnp.concatenate([high, low], axis=0))
        scale = jnp.where(causal, gates_ref[rows, head : head + 1] * lax.rsqrt(norm), 0.0)
        high_ref[head, :, rows] = high
        low_ref[head, :, rows] = low
        corr_ref[head, :, rows] = (corr * scale).astype(BF16)


def project_kernel(
    heads,
    blocks,
    groups,
    group_ref,
    values_ref,
    high_ref,
    low_ref,
    corr_ref,
    local_ref,
    prior_ref,
    own_ref,
    *rest,
):
    others, out_ref = rest[: groups - 1], rest[groups - 1]
    readout = rest[groups]
    for block in range(blocks):
        rows = slice(block * SPAN, (block + 1) * SPAN)
        for head in range(heads):
            moment_high, moment_low = two_terms(prior_ref[head] + local_ref[head, block])
            values = values_ref[rows, head_cols(head)].astype(F32).T.astype(BF16)
            left = jnp.concatenate([moment_high, moment_high, moment_low, values], axis=1)
            high = high_ref[head, :, rows]
            right = jnp.concatenate([high, low_ref[head, :, rows], high, corr_ref[head, :, rows]], axis=0)
            readout[rows, head_cols(head)] = dot(left, right).T.astype(BF16)
    group = group_ref[0]
    width = own_ref.shape[1]
    for shift, part in enumerate((own_ref,) + tuple(others)):
        source = lax.rem(group + groups - shift, groups)
        columns = pl.ds(pl.multiple_of(source * width, width), width)
        out_ref[0, :, columns] = dot(readout[...], part[...]).astype(BF16)


def params():
    return pltpu.CompilerParams(vmem_limit_bytes=VMEM_LIMIT)


def whole(shape):
    return pl.BlockSpec(shape, lambda *a: (0,) * len(shape))


def shards(mesh, queries, keys, values, gates, ridge, out_weight):
    tokens, width = queries.shape
    heads = width // HD
    half = heads // 2
    blocks = tokens // SPAN
    seq, groups = mesh.shape["seq"], mesh.shape["head"]
    columns = out_weight.shape[1]
    side = 4
    place = lax.axis_index("seq")
    core = lax.rem(place, 2)
    x_at = lax.rem(place // 2, side)
    y_at = place // (2 * side)
    group = lax.axis_index("head")
    core_arg = core.reshape(1).astype(jnp.int32)
    group_arg = group.reshape(1).astype(jnp.int32)
    smem = pl.BlockSpec(memory_space=pltpu.SMEM)

    def perm_core():
        return [(p, p ^ 1) for p in range(seq)]

    def perm_x(shift):
        return [(p, (p // 8) * 8 + ((p // 2 + shift) % side) * 2 + p % 2) for p in range(seq)]

    def perm_y(shift):
        return [(p, (p + 8 * shift) % seq) for p in range(seq)]

    def send(array, perm):
        return lax.ppermute(array, "seq", perm)

    parts = []
    for shift in range(1, groups):
        to = lax.rem(group + shift, groups)
        piece = lax.dynamic_slice_in_dim(out_weight, to * width, width, 0)
        parts.append(
            lax.ppermute(piece, "head", [(i, (i + shift) % groups) for i in range(groups)])
        )

    square = (half, HD, HD)
    mine, theirs = pl.pallas_call(
        functools.partial(totals_kernel, heads),
        in_specs=[smem, pl.BlockSpec(memory_space=pltpu.VMEM), pl.BlockSpec(memory_space=pltpu.VMEM)],
        out_specs=[pl.BlockSpec(memory_space=pltpu.VMEM)] * 2,
        out_shape=[jax.ShapeDtypeStruct(square, F32)] * 2,
        compiler_params=params(),
        cost_estimate=pl.CostEstimate(
            flops=4 * tokens * width * HD, bytes_accessed=2 * tokens * width, transcendentals=0
        ),
        name="totals",
    )(core_arg, keys, gates)

    local_gram, local_moment, moment_total = pl.pallas_call(
        functools.partial(local_kernel, heads, blocks),
        grid=(blocks,),
        in_specs=[
            pl.BlockSpec((SPAN, width), lambda b: (b, 0)),
            pl.BlockSpec((SPAN, width), lambda b: (b, 0)),
            pl.BlockSpec((SPAN, heads), lambda b: (b, 0)),
        ],
        out_specs=[
            pl.BlockSpec((heads, 1, HD, HD), lambda b: (0, b, 0, 0)),
            pl.BlockSpec((heads, 1, HD, HD), lambda b: (0, b, 0, 0)),
            whole((heads, HD, HD)),
        ],
        out_shape=[
            jax.ShapeDtypeStruct((heads, blocks, HD, HD), F32),
            jax.ShapeDtypeStruct((heads, blocks, HD, HD), F32),
            jax.ShapeDtypeStruct((heads, HD, HD), BF16),
        ],
        scratch_shapes=[pltpu.VMEM((heads, HD, HD), F32)] * 2,
        compiler_params=params(),
        cost_estimate=pl.CostEstimate(
            flops=8 * tokens * width * HD, bytes_accessed=12 * tokens * width, transcendentals=0
        ),
        name="local",
    )(keys, values, gates)

    received = send(theirs, perm_core())
    chip = (mine + received).astype(F16)
    along = [send(chip, perm_x(shift)) for shift in range(1, side)]
    wide = [part.astype(F32) for part in along]
    row_total = (chip.astype(F32) + wide[0] + wide[1] + wide[2]).astype(F16)
    row_before = sum(jnp.where(x_at >= shift, part, 0.0) for shift, part in enumerate(wide, 1))
    above = [send(row_total, perm_y(shift)).astype(F32) for shift in range(1, side)]
    before = row_before + sum(jnp.where(y_at >= shift, part, 0.0) for shift, part in enumerate(above, 1))
    keep = before + jnp.where(core == 1, received, 0.0)
    give = before + jnp.where(core == 0, mine, 0.0)
    got = send(give, perm_core())

    other = send(moment_total, perm_core())
    moment_core = jnp.where(core == 1, other, jnp.zeros_like(other)).astype(F32)
    moment_chip = (moment_total.astype(F32) + other.astype(F32)).astype(BF16)
    wide = [send(moment_chip, perm_x(shift)).astype(F32) for shift in range(1, side)]
    row_total = (moment_chip.astype(F32) + wide[0] + wide[1] + wide[2]).astype(BF16)
    row_before = sum(jnp.where(x_at >= shift, part, 0.0) for shift, part in enumerate(wide, 1))
    above = [send(row_total, perm_y(shift)).astype(F32) for shift in range(1, side)]
    moment_prior = (
        moment_core
        + row_before
        + sum(jnp.where(y_at >= shift, part, 0.0) for shift, part in enumerate(above, 1))
    )

    step_blocks = 2
    step = step_blocks * SPAN
    units = heads * step_blocks
    calls = 2
    solved = []
    for call in range(calls):
        grid = blocks // step_blocks // calls
        base = call * grid
        solved.append(
            pl.pallas_call(
                functools.partial(solve_kernel, heads, step_blocks),
                grid=(grid,),
                in_specs=[
                    smem,
                    smem,
                    pl.BlockSpec((step, width), lambda b, base=base: (b + base, 0)),
                    pl.BlockSpec((step, width), lambda b, base=base: (b + base, 0)),
                    pl.BlockSpec((step, heads), lambda b, base=base: (b + base, 0)),
                    pl.BlockSpec((heads, step_blocks, HD, HD), lambda b, base=base: (0, b + base, 0, 0)),
                    whole(square),
                    whole(square),
                ],
                out_specs=[pl.BlockSpec((heads, HD, step), lambda b: (0, 0, b))] * 3,
                out_shape=[jax.ShapeDtypeStruct((heads, HD, tokens // calls), BF16)] * 3,
                scratch_shapes=[
                    pltpu.VMEM((units, 2 * HD, 2 * HD), BF16),
                    pltpu.VMEM((units, HD, 2 * HD), BF16),
                    pltpu.VMEM((units, SPAN, SPAN), F32),
                    pltpu.VMEM((units, HD, SPAN), F32),
                    pltpu.VMEM((units, HD, SPAN), F32),
                    pltpu.VMEM((units, HD, SPAN), F32),
                    pltpu.VMEM((units, 8, SPAN), F32),
                ],
                compiler_params=params(),
                cost_estimate=pl.CostEstimate(
                    flops=48 * ITERS * tokens * width * HD // calls,
                    bytes_accessed=20 * tokens * width // calls,
                    transcendentals=0,
                ),
                name="solve",
            )(core_arg, ridge, queries, keys, gates, local_gram, keep, got)
        )
    high, low, corr = (jnp.concatenate(group_of, axis=2) for group_of in zip(*solved))

    out = pl.pallas_call(
        functools.partial(project_kernel, heads, step_blocks, groups),
        grid_spec=pltpu.PrefetchScalarGridSpec(
            num_scalar_prefetch=1,
            grid=(blocks // step_blocks,),
            in_specs=[
                pl.BlockSpec((step, width), lambda b, g: (b, 0)),
                pl.BlockSpec((heads, HD, step), lambda b, g: (0, 0, b)),
                pl.BlockSpec((heads, HD, step), lambda b, g: (0, 0, b)),
                pl.BlockSpec((heads, HD, step), lambda b, g: (0, 0, b)),
                pl.BlockSpec((heads, step_blocks, HD, HD), lambda b, g: (0, b, 0, 0)),
                whole((heads, HD, HD)),
                pl.BlockSpec((width, columns), lambda b, g: (g[0], 0)),
            ]
            + [whole((width, columns))] * (groups - 1),
            out_specs=pl.BlockSpec((1, step, columns * groups), lambda b, g: (0, b, 0)),
            scratch_shapes=[pltpu.VMEM((step, width), BF16)],
        ),
        out_shape=jax.ShapeDtypeStruct((1, tokens, columns * groups), BF16),
        compiler_params=params(),
        cost_estimate=pl.CostEstimate(
            flops=2 * tokens * width * columns * groups,
            bytes_accessed=24 * tokens * width,
            transcendentals=0,
        ),
        name="project",
    )(group_arg, values, high, low, corr, local_moment, moment_prior, out_weight, *parts)
    return out


def solution(mesh):
    return jax.shard_map(
        functools.partial(shards, mesh),
        mesh=mesh,
        in_specs=(
            P("seq", "head"),
            P("seq", "head"),
            P("seq", "head"),
            P("seq", "head"),
            P("head"),
            P(None, "head"),
        ),
        out_specs=P("head", "seq", None),
        check_vma=False,
    )
```

profile of v0, /device:TPU:1, one launch (start us, length us, event | category | flops | bytes accessed | tf_op | source)
XLA Modules:
  0.0 142.0 jit_solution(13066486826305482144)
XLA Ops:
  0.0 1.9 %copy.9.gates_ref = f32[1024,4]{1,0:T(8,128)} copy(f32[1024,4]{0,1:T(4,128)} %param.9) | data formatting | bytes 32768 | tf_op args[3]
  1.9 4.4 %totals.1 = (f32[2,128,128]{2,1,0:T(8,128)}, f32[2,128,128]{2,1,0:T(8,128)}) custom-call(s32[1]{0:T(128)} %bitcast.1.core_ref, bf16[1024,512]{1,0:T(8,128)(2,1)} %keys_ref.7, f32[1024,4]{1,0:T(8,128)} %copy.9.gates_ref), custom_call_target="tpu_custom_call" | custom-call | flops 268435456 | bytes 1048576 | tf_op jit(solution)/shard_map/totals/pallas_call | solution.py:247
  6.3 1.4 %collective-permute-start = (f32[2,128,128]{2,1,0:T(8,128)}, f32[2,128,128]{2,1,0:T(8,128)S(1)}, u32[]{:S(2)}, u32[]{:S(2)}) collective-permute-start(f32[2,128,128]{2,1,0:T(8,128)} %get-tuple-element.18), channel_id=1, source_target_pairs={{0,4},{4,0},{8,12},{12,8},{16,20},{20,16},{24,28},{28,24},{32,36},... | collective-permute-start | bytes 393224 | tf_op jit(solution)/shard_map/ppermute | solution.py:236
  7.8 1.2 collective-permute-done
  9.0 0.9 add_convert_fusion.1
  9.9 2.6 %collective-permute-start.3 = (f16[2,128,128]{2,1,0:T(8,128)(2,1)S(1)}, f16[2,128,128]{2,1,0:T(8,128)(2,1)S(1)}, u32[]{:S(2)}, u32[]{:S(2)}) collective-permute-start(f16[2,128,128]{2,1,0:T(8,128)(2,1)S(1)} %add_convert_fusion.1), channel_id=1, source_target_pairs={{0,24},{4,28},{8,0},{12,4},{16,8},{20,12},{24,16},{28,20},{32,56},... | collective-permute-start | bytes 196616 | tf_op jit(solution)/shard_map/ppermute | solution.py:236
  12.5 0.5 collective-permute-start.2
  13.0 0.6 collective-permute-start.1
  13.6 0.9 constant_dynamic-slice_fusion
  14.5 3.8 %collective-permute-start.17 = (bf16[512,512]{1,0:T(8,128)(2,1)}, bf16[512,512]{1,0:T(8,128)(2,1)S(1)}, u32[]{:S(2)}, u32[]{:S(2)}) collective-permute-start(bf16[512,512]{1,0:T(8,128)(2,1)} %get-tuple-element.29), channel_id=1, source_target_pairs={{0,3},{1,0},{2,1},{3,2},{4,7},{5,4},{6,5},{7,6},{8,11},{9,8},{10,9... | collective-permute-start | bytes 1572872 | tf_op jit(solution)/shard_map/ppermute | solution.py:243
  18.3 8.6 %local.1 = (f32[4,8,128,128]{3,2,1,0:T(8,128)}, f32[4,8,128,128]{3,2,1,0:T(8,128)}, bf16[4,128,128]{2,1,0:T(8,128)(2,1)}) custom-call(bf16[1024,512]{1,0:T(8,128)(2,1)} %keys_ref.7, bf16[1024,512]{1,0:T(8,128)(2,1)} %values_ref.3, f32[1024,4]{1,0:T(8,128)} %copy.9.gates_ref), custom_call_target="tpu_custom_call" | custom-call | flops 536870912 | bytes 6291456 | tf_op jit(solution)/shard_map/local/pallas_call | solution.py:259
  26.9 0.0 collective-permute-done.3
  27.0 1.6 %collective-permute-start.8 = (bf16[4,128,128]{2,1,0:T(8,128)(2,1)}, bf16[4,128,128]{2,1,0:T(8,128)(2,1)S(1)}, u32[]{:S(2)}, u32[]{:S(2)}) collective-permute-start(bf16[4,128,128]{2,1,0:T(8,128)(2,1)} %get-tuple-element.26), channel_id=1, source_target_pairs={{0,4},{4,0},{8,12},{12,8},{16,20},{20,16},{24,28},{28,24},{32,36},... | collective-permute-start | bytes 393224 | tf_op jit(solution)/shard_map/ppermute | solution.py:236
  28.6 2.8 %collective-permute-start.6 = (f16[2,128,128]{2,1,0:T(8,128)(2,1)S(1)}, f16[2,128,128]{2,1,0:T(8,128)(2,1)S(1)}, u32[]{:S(2)}, u32[]{:S(2)}) collective-permute-start(f16[2,128,128]{2,1,0:T(8,128)(2,1)S(1)} %fusion.8), channel_id=1, source_target_pairs={{0,96},{4,100},{8,104},{12,108},{16,112},{20,116},{24,120},{28,124... | collective-permute-start | bytes 196616 | tf_op jit(solution)/shard_map/ppermute | solution.py:236
  31.4 0.3 collective-permute-start.5
  31.7 0.7 collective-permute-start.4
  32.4 0.9 add_convert_fusion
  33.4 2.1 %collective-permute-start.11 = (bf16[4,128,128]{2,1,0:T(8,128)(2,1)S(1)}, bf16[4,128,128]{2,1,0:T(8,128)(2,1)S(1)}, u32[]{:S(2)}, u32[]{:S(2)}) collective-permute-start(bf16[4,128,128]{2,1,0:T(8,128)(2,1)S(1)} %add_convert_fusion), channel_id=1, source_target_pairs={{0,24},{4,28},{8,0},{12,4},{16,8},{20,12},{24,16},{28,20},{32,56},... | collective-permute-start | bytes 393224 | tf_op jit(solution)/shard_map/ppermute | solution.py:236
  35.5 0.6 collective-permute-done.5
  36.1 1.6 %collective-permute-start.10 = (bf16[4,128,128]{2,1,0:T(8,128)(2,1)S(1)}, bf16[4,128,128]{2,1,0:T(8,128)(2,1)S(1)}, u32[]{:S(2)}, u32[]{:S(2)}) collective-permute-start(bf16[4,128,128]{2,1,0:T(8,128)(2,1)S(1)} %add_convert_fusion), channel_id=1, source_target_pairs={{0,16},{4,20},{8,24},{12,28},{16,0},{20,4},{24,8},{28,12},{32,48},... | collective-permute-start | bytes 393224 | tf_op jit(solution)/shard_map/ppermute | solution.py:236
  37.6 0.6 collective-permute-done.4
  38.2 1.5 %collective-permute-start.9 = (bf16[4,128,128]{2,1,0:T(8,128)(2,1)S(1)}, bf16[4,128,128]{2,1,0:T(8,128)(2,1)S(1)}, u32[]{:S(2)}, u32[]{:S(2)}) collective-permute-start(bf16[4,128,128]{2,1,0:T(8,128)(2,1)S(1)} %add_convert_fusion), channel_id=1, source_target_pairs={{0,8},{4,12},{8,16},{12,20},{16,24},{20,28},{24,0},{28,4},{32,40},... | collective-permute-start | bytes 393224 | tf_op jit(solution)/shard_map/ppermute | solution.py:236
  39.7 0.1 select_add_fusion
  39.8 0.0 collective-permute-done.11
  39.8 1.0 collective-permute-start.15
  40.8 0.6 collective-permute-done.10
  41.4 4.6 %collective-permute-start.7 = (f32[2,128,128]{2,1,0:T(8,128)S(1)}, f32[2,128,128]{2,1,0:T(8,128)S(1)}, u32[]{:S(2)}, u32[]{:S(2)}) collective-permute-start(f32[2,128,128]{2,1,0:T(8,128)S(1)} %get-tuple-element.27), channel_id=1, source_target_pairs={{0,4},{4,0},{8,12},{12,8},{16,20},{20,16},{24,28},{28,24},{32,36},... | collective-permute-start | bytes 393224 | tf_op jit(solution)/shard_map/ppermute | solution.py:236
  46.0 0.0 collective-permute-done.9
  46.0 0.1 fusion.4
  46.1 2.8 %collective-permute-start.14 = (bf16[4,128,128]{2,1,0:T(8,128)(2,1)S(1)}, bf16[4,128,128]{2,1,0:T(8,128)(2,1)S(1)}, u32[]{:S(2)}, u32[]{:S(2)}) collective-permute-start(bf16[4,128,128]{2,1,0:T(8,128)(2,1)S(1)} %fusion.4), channel_id=1, source_target_pairs={{0,96},{4,100},{8,104},{12,108},{16,112},{20,116},{24,120},{28,124... | collective-permute-start | bytes 393224 | tf_op jit(solution)/shard_map/ppermute | solution.py:236
  48.9 0.7 select_add_fusion.1.keep_ref
  49.5 0.0 collective-permute-start.13
  49.5 0.6 copy-done.9
  50.2 36.6 %solve.3 = (bf16[4,128,512]{2,1,0:T(8,128)(2,1)}, bf16[4,128,512]{2,1,0:T(8,128)(2,1)}, bf16[4,128,512]{2,1,0:T(8,128)(2,1)}) custom-call(s32[1]{0:T(128)} %bitcast.1.core_ref, f32[4]{0:T(128)} %ridge_ref.3, bf16[1024,512]{1,0:T(8,128)(2,1)} %queries_ref.3, bf16[1024,512]{1,0:T(8,128)(2,1)} %keys_ref.7, f32[1024,4]{1,0:T(8,128)} %copy.9.gates_ref, ...), custom_call_target="tpu_custom_call" | custom-call | flops 12884901888 | bytes 5242880 | tf_op jit(solution)/shard_map/solve/pallas_call | solution.py:319
  86.8 36.8 %solve.2 = (bf16[4,128,512]{2,1,0:T(8,128)(2,1)}, bf16[4,128,512]{2,1,0:T(8,128)(2,1)}, bf16[4,128,512]{2,1,0:T(8,128)(2,1)}) custom-call(s32[1]{0:T(128)} %bitcast.1.core_ref, f32[4]{0:T(128)} %ridge_ref.3, bf16[1024,512]{1,0:T(8,128)(2,1)} %queries_ref.3, bf16[1024,512]{1,0:T(8,128)(2,1)} %keys_ref.7, f32[1024,4]{1,0:T(8,128)} %copy.9.gates_ref, ...), custom_call_target="tpu_custom_call" | custom-call | flops 12884901888 | bytes 5242880 | tf_op jit(solution)/shard_map/solve/pallas_call | solution.py:319
  123.6 2.9 %pad_maximum_fusion = (bf16[4,128,1024]{2,1,0:T(8,128)(2,1)}, bf16[4,128,1024]{2,1,0:T(8,128)(2,1)}) fusion(bf16[4,128,512]{2,1,0:T(8,128)(2,1)S(1)} %copy-done.7, bf16[4,128,512]{2,1,0:T(8,128)(2,1)} %get-tuple-element.19, bf16[4,128,512]{2,1,0:T(8,128)(2,1)S(1)} %copy-done.8, bf16[4,128,512]{2,1,0:T(8,128)(2,1)} %get-tuple-element.21), kind=kLoop, calls=%fused_computation | loop fusion | flops 4194304 | bytes 4194304 | tf_op jit(solution)/shard_map/concatenate | solution.py:352
  126.5 0.0 collective-permute-done.14
  126.5 0.0 collective-permute-start.12
  126.5 1.2 pad_maximum_fusion.2.corr_ref
  127.7 0.0 collective-permute-done.13
  127.7 3.8 %collective-permute-done.12 = bf16[4,128,128]{2,1,0:T(8,128)(2,1)S(1)} collective-permute-done((bf16[4,128,128]{2,1,0:T(8,128)(2,1)S(1)}, bf16[4,128,128]{2,1,0:T(8,128)(2,1)S(1)}, u32[]{:S(2)}, u32[]{:S(2)}) %collective-permute-start.12) | collective-permute-done | bytes 131104 | tf_op jit(solution)/shard_map/ppermute | solution.py:236
  131.6 0.9 fusion.3.prior_ref
  132.4 0.0 collective-permute-done.17.rest_2_
  132.5 0.0 collective-permute-done.15.rest_0_
  132.5 0.8 copy-done.1
  133.2 0.2 copy-done.2
  133.4 0.2 copy-done.3
  133.6 8.3 %project.1 = bf16[1,1024,2048]{2,1,0:T(8,128)(2,1)} custom-call(s32[1]{0:T(128)} %bitcast.group_ref, bf16[1024,512]{1,0:T(8,128)(2,1)} %values_ref.3, bf16[4,128,1024]{2,1,0:T(8,128)(2,1)} %get-tuple-element.32.high_ref, bf16[4,128,1024]{2,1,0:T(8,128)(2,1)} %get-tuple-element.33.low_ref, bf16[4,128,1024]{2,1,0:T(8,128)(2,1)} %pad_maximum_fusion.2.corr_ref, ...), custom_call_target="tpu_custom_call" | custom-call | flops 2147483648 | bytes 12582912 | tf_op jit(solution)/shard_map/project/pallas_call | solution.py:354
  (24 shorter events, 0.1 us)
Async XLA Ops:
  0.0 13.6 %copy-start = (bf16[2048,512]{1,0:T(8,128)(2,1)S(1)}, bf16[2048,512]{1,0:T(8,128)(2,1)}, u32[]{:S(2)}) copy-start(bf16[2048,512]{1,0:T(8,128)(2,1)} %own_ref.1) | copy-start | bytes 6291460
  6.3 2.6 %collective-permute-start = (f32[2,128,128]{2,1,0:T(8,128)}, f32[2,128,128]{2,1,0:T(8,128)S(1)}, u32[]{:S(2)}, u32[]{:S(2)}) collective-permute-start(f32[2,128,128]{2,1,0:T(8,128)} %get-tuple-element.18), channel_id=1, source_target_pairs={{0,4},{4,0},{8,12},{12,8},{16,20},{20,16},{24,28},{28,24},{32,36},... | collective-permute-start | bytes 393224 | tf_op jit(solution)/shard_map/ppermute | solution.py:236
  9.9 17.1 %collective-permute-start.3 = (f16[2,128,128]{2,1,0:T(8,128)(2,1)S(1)}, f16[2,128,128]{2,1,0:T(8,128)(2,1)S(1)}, u32[]{:S(2)}, u32[]{:S(2)}) collective-permute-start(f16[2,128,128]{2,1,0:T(8,128)(2,1)S(1)} %add_convert_fusion.1), channel_id=1, source_target_pairs={{0,24},{4,28},{8,0},{12,4},{16,8},{20,12},{24,16},{28,20},{32,56},... | collective-permute-start | bytes 196616 | tf_op jit(solution)/shard_map/ppermute | solution.py:236
  12.5 16.0 %collective-permute-start.2 = (f16[2,128,128]{2,1,0:T(8,128)(2,1)S(1)}, f16[2,128,128]{2,1,0:T(8,128)(2,1)S(1)}, u32[]{:S(2)}, u32[]{:S(2)}) collective-permute-start(f16[2,128,128]{2,1,0:T(8,128)(2,1)S(1)} %add_convert_fusion.1), channel_id=1, source_target_pairs={{0,16},{4,20},{8,24},{12,28},{16,0},{20,4},{24,8},{28,12},{32,48},... | collective-permute-start | bytes 196616 | tf_op jit(solution)/shard_map/ppermute | solution.py:236
  13.0 15.5 %collective-permute-start.1 = (f16[2,128,128]{2,1,0:T(8,128)(2,1)S(1)}, f16[2,128,128]{2,1,0:T(8,128)(2,1)S(1)}, u32[]{:S(2)}, u32[]{:S(2)}) collective-permute-start(f16[2,128,128]{2,1,0:T(8,128)(2,1)S(1)} %add_convert_fusion.1), channel_id=1, source_target_pairs={{0,8},{4,12},{8,16},{12,20},{16,24},{20,28},{24,0},{28,4},{32,40},... | collective-permute-start | bytes 196616 | tf_op jit(solution)/shard_map/ppermute | solution.py:236
  14.5 25.1 %copy-start.4 = (f32[2,128,128]{2,1,0:T(8,128)S(1)}, f32[2,128,128]{2,1,0:T(8,128)}, u32[]{:S(2)}) copy-start(f32[2,128,128]{2,1,0:T(8,128)} %get-tuple-element.17) | copy-start | bytes 393220
  14.5 117.9 %collective-permute-start.17 = (bf16[512,512]{1,0:T(8,128)(2,1)}, bf16[512,512]{1,0:T(8,128)(2,1)S(1)}, u32[]{:S(2)}, u32[]{:S(2)}) collective-permute-start(bf16[512,512]{1,0:T(8,128)(2,1)} %get-tuple-element.29), channel_id=1, source_target_pairs={{0,3},{1,0},{2,1},{3,2},{4,7},{5,4},{6,5},{7,6},{8,11},{9,8},{10,9... | collective-permute-start | bytes 1572872 | tf_op jit(solution)/shard_map/ppermute | solution.py:243
  18.3 114.1 %collective-permute-start.16 = (bf16[512,512]{1,0:T(8,128)(2,1)S(1)}, bf16[512,512]{1,0:T(8,128)(2,1)S(1)}, u32[]{:S(2)}, u32[]{:S(2)}) collective-permute-start(bf16[512,512]{1,0:T(8,128)(2,1)S(1)} %get-tuple-element.30), channel_id=1, source_target_pairs={{0,2},{1,3},{2,0},{3,1},{4,6},{5,7},{6,4},{7,5},{8,10},{9,11},{10,... | collective-permute-start | bytes 1572872 | tf_op jit(solution)/shard_map/ppermute | solution.py:243
  27.0 4.8 %collective-permute-start.8 = (bf16[4,128,128]{2,1,0:T(8,128)(2,1)}, bf16[4,128,128]{2,1,0:T(8,128)(2,1)S(1)}, u32[]{:S(2)}, u32[]{:S(2)}) collective-permute-start(bf16[4,128,128]{2,1,0:T(8,128)(2,1)} %get-tuple-element.26), channel_id=1, source_target_pairs={{0,4},{4,0},{8,12},{12,8},{16,20},{20,16},{24,28},{28,24},{32,36},... | collective-permute-start | bytes 393224 | tf_op jit(solution)/shard_map/ppermute | solution.py:236
  28.6 4.8 %collective-permute-start.6 = (f16[2,128,128]{2,1,0:T(8,128)(2,1)S(1)}, f16[2,128,128]{2,1,0:T(8,128)(2,1)S(1)}, u32[]{:S(2)}, u32[]{:S(2)}) collective-permute-start(f16[2,128,128]{2,1,0:T(8,128)(2,1)S(1)} %fusion.8), channel_id=1, source_target_pairs={{0,96},{4,100},{8,104},{12,108},{16,112},{20,116},{24,120},{28,124... | collective-permute-start | bytes 196616 | tf_op jit(solution)/shard_map/ppermute | solution.py:236
  31.4 4.7 %collective-permute-start.5 = (f16[2,128,128]{2,1,0:T(8,128)(2,1)S(1)}, f16[2,128,128]{2,1,0:T(8,128)(2,1)S(1)}, u32[]{:S(2)}, u32[]{:S(2)}) collective-permute-start(f16[2,128,128]{2,1,0:T(8,128)(2,1)S(1)} %fusion.8), channel_id=1, source_target_pairs={{0,64},{4,68},{8,72},{12,76},{16,80},{20,84},{24,88},{28,92},{32,9... | collective-permute-start | bytes 196616 | tf_op jit(solution)/shard_map/ppermute | solution.py:236
  31.7 6.4 %collective-permute-start.4 = (f16[2,128,128]{2,1,0:T(8,128)(2,1)S(1)}, f16[2,128,128]{2,1,0:T(8,128)(2,1)S(1)}, u32[]{:S(2)}, u32[]{:S(2)}) collective-permute-start(f16[2,128,128]{2,1,0:T(8,128)(2,1)S(1)} %fusion.8), channel_id=1, source_target_pairs={{0,32},{4,36},{8,40},{12,44},{16,48},{20,52},{24,56},{28,60},{32,6... | collective-permute-start | bytes 196616 | tf_op jit(solution)/shard_map/ppermute | solution.py:236
  33.4 6.4 %collective-permute-start.11 = (bf16[4,128,128]{2,1,0:T(8,128)(2,1)S(1)}, bf16[4,128,128]{2,1,0:T(8,128)(2,1)S(1)}, u32[]{:S(2)}, u32[]{:S(2)}) collective-permute-start(bf16[4,128,128]{2,1,0:T(8,128)(2,1)S(1)} %add_convert_fusion), channel_id=1, source_target_pairs={{0,24},{4,28},{8,0},{12,4},{16,8},{20,12},{24,16},{28,20},{32,56},... | collective-permute-start | bytes 393224 | tf_op jit(solution)/shard_map/ppermute | solution.py:236
  36.1 5.3 %collective-permute-start.10 = (bf16[4,128,128]{2,1,0:T(8,128)(2,1)S(1)}, bf16[4,128,128]{2,1,0:T(8,128)(2,1)S(1)}, u32[]{:S(2)}, u32[]{:S(2)}) collective-permute-start(bf16[4,128,128]{2,1,0:T(8,128)(2,1)S(1)} %add_convert_fusion), channel_id=1, source_target_pairs={{0,16},{4,20},{8,24},{12,28},{16,0},{20,4},{24,8},{28,12},{32,48},... | collective-permute-start | bytes 393224 | tf_op jit(solution)/shard_map/ppermute | solution.py:236
  38.2 7.8 %collective-permute-start.9 = (bf16[4,128,128]{2,1,0:T(8,128)(2,1)S(1)}, bf16[4,128,128]{2,1,0:T(8,128)(2,1)S(1)}, u32[]{:S(2)}, u32[]{:S(2)}) collective-permute-start(bf16[4,128,128]{2,1,0:T(8,128)(2,1)S(1)} %add_convert_fusion), channel_id=1, source_target_pairs={{0,8},{4,12},{8,16},{12,20},{16,24},{20,28},{24,0},{28,4},{32,40},... | collective-permute-start | bytes 393224 | tf_op jit(solution)/shard_map/ppermute | solution.py:236
  39.8 92.7 %collective-permute-start.15 = (bf16[512,512]{1,0:T(8,128)(2,1)S(1)}, bf16[512,512]{1,0:T(8,128)(2,1)S(1)}, u32[]{:S(2)}, u32[]{:S(2)}) collective-permute-start(bf16[512,512]{1,0:T(8,128)(2,1)S(1)} %get-tuple-element.31), channel_id=1, source_target_pairs={{0,1},{1,2},{2,3},{3,0},{4,5},{5,6},{6,7},{7,4},{8,9},{9,10},{10,1... | collective-permute-start | bytes 1572872 | tf_op jit(solution)/shard_map/ppermute | solution.py:243
  41.4 8.2 %collective-permute-start.7 = (f32[2,128,128]{2,1,0:T(8,128)S(1)}, f32[2,128,128]{2,1,0:T(8,128)S(1)}, u32[]{:S(2)}, u32[]{:S(2)}) collective-permute-start(f32[2,128,128]{2,1,0:T(8,128)S(1)} %get-tuple-element.27), channel_id=1, source_target_pairs={{0,4},{4,0},{8,12},{12,8},{16,20},{20,16},{24,28},{28,24},{32,36},... | collective-permute-start | bytes 393224 | tf_op jit(solution)/shard_map/ppermute | solution.py:236
  46.1 80.5 %collective-permute-start.14 = (bf16[4,128,128]{2,1,0:T(8,128)(2,1)S(1)}, bf16[4,128,128]{2,1,0:T(8,128)(2,1)S(1)}, u32[]{:S(2)}, u32[]{:S(2)}) collective-permute-start(bf16[4,128,128]{2,1,0:T(8,128)(2,1)S(1)} %fusion.4), channel_id=1, source_target_pairs={{0,96},{4,100},{8,104},{12,108},{16,112},{20,116},{24,120},{28,124... | collective-permute-start | bytes 393224 | tf_op jit(solution)/shard_map/ppermute | solution.py:236
  49.5 0.6 copy-start.9
  49.5 78.2 %collective-permute-start.13 = (bf16[4,128,128]{2,1,0:T(8,128)(2,1)S(1)}, bf16[4,128,128]{2,1,0:T(8,128)(2,1)S(1)}, u32[]{:S(2)}, u32[]{:S(2)}) collective-permute-start(bf16[4,128,128]{2,1,0:T(8,128)(2,1)S(1)} %fusion.4), channel_id=1, source_target_pairs={{0,64},{4,68},{8,72},{12,76},{16,80},{20,84},{24,88},{28,92},{32,9... | collective-permute-start | bytes 393224 | tf_op jit(solution)/shard_map/ppermute | solution.py:236
  86.8 36.8 %copy-start.7 = (bf16[4,128,512]{2,1,0:T(8,128)(2,1)S(1)}, bf16[4,128,512]{2,1,0:T(8,128)(2,1)}, u32[]{:S(2)}) copy-start(bf16[4,128,512]{2,1,0:T(8,128)(2,1)} %get-tuple-element.20) | copy-start | bytes 1572868
  86.8 36.8 %copy-start.8 = (bf16[4,128,512]{2,1,0:T(8,128)(2,1)S(1)}, bf16[4,128,512]{2,1,0:T(8,128)(2,1)}, u32[]{:S(2)}) copy-start(bf16[4,128,512]{2,1,0:T(8,128)(2,1)} %get-tuple-element.22) | copy-start | bytes 1572868
  123.6 2.9 %copy-start.5 = (bf16[4,128,512]{2,1,0:T(8,128)(2,1)S(1)}, bf16[4,128,512]{2,1,0:T(8,128)(2,1)}, u32[]{:S(2)}) copy-start(bf16[4,128,512]{2,1,0:T(8,128)(2,1)} %get-tuple-element.24) | copy-start | bytes 1572868
  123.6 2.9 %copy-start.6 = (bf16[4,128,512]{2,1,0:T(8,128)(2,1)S(1)}, bf16[4,128,512]{2,1,0:T(8,128)(2,1)}, u32[]{:S(2)}) copy-start(bf16[4,128,512]{2,1,0:T(8,128)(2,1)} %get-tuple-element.23) | copy-start | bytes 1572868
  126.5 5.0 %collective-permute-start.12 = (bf16[4,128,128]{2,1,0:T(8,128)(2,1)S(1)}, bf16[4,128,128]{2,1,0:T(8,128)(2,1)S(1)}, u32[]{:S(2)}, u32[]{:S(2)}) collective-permute-start(bf16[4,128,128]{2,1,0:T(8,128)(2,1)S(1)} %fusion.4), channel_id=1, source_target_pairs={{0,32},{4,36},{8,40},{12,44},{16,48},{20,52},{24,56},{28,60},{32,6... | collective-permute-start | bytes 393224 | tf_op jit(solution)/shard_map/ppermute | solution.py:236
  132.4 0.8 copy-start.1
  132.4 1.0 copy-start.2
  132.5 1.1 copy-start.3
where the time goes:
time: 144 us; the launch traced here: 142 us
  Pallas kernels  94.8 us (66%)
  starting transfers between devices  28 us (19%)
  other arithmetic  7.7 us (5%)
  waiting for transfers between devices  6.7 us (5%)
  local copies, waits for them, and re-layouts  4.59 us (3%)
    pallas_call x2, Pallas kernels, shards(): pl.pallas_call(functools.partial(solve_kernel, heads, step_blocks), grid=...  73.4 us
    ppermute x15, starting transfers between devices, send(): return lax.ppermute(array, 'seq', perm)  23.2 us
    pallas_call x1, Pallas kernels, shards(): pl.pallas_call(functools.partial(local_kernel, heads, blocks), grid=(bloc...  8.63 us
    pallas_call x1, Pallas kernels, shards(): pl.pallas_call(functools.partial(project_kernel, heads, step_blocks, grou...  8.34 us
    ppermute x15, waiting for transfers between devices, send(): return lax.ppermute(array, 'seq', perm)  6.69 us
    ppermute x3, starting transfers between devices, shards(): lax.ppermute(piece, 'head', [(i, (i + shift) % groups) for i in range(gro...  4.8 us
    pallas_call x1, Pallas kernels, shards(): pl.pallas_call(functools.partial(totals_kernel, heads), in_specs=[smem, p...  4.44 us
    concatenate x2, other arithmetic, shards(): jnp.concatenate(group_of, axis=2)  4.09 us
  transfers between devices with their start and end apart: 18, of which 5 were waited for; matrix products, arithmetic and copies ran while one was open for 5% of the time, Pallas kernels for 58%

commit v1 on v0

v1 whole, which is shorter than its diff:
```python
import functools
import jax
import jax.numpy as jnp
from jax import lax
from jax.experimental import pallas as pl
from jax.experimental.pallas import tpu as pltpu
from jax.sharding import PartitionSpec as P

HD = 128
SPAN = 128
ITERS = 8
EPS = 1e-06
F32 = jnp.float32
BF16 = jnp.bfloat16
F16 = jnp.float16
VMEM_LIMIT = 56 * 1024 * 1024


def two_terms(value):
    high = value.astype(BF16)
    return high, (value - high.astype(F32)).astype(BF16)


def dot(left, right):
    return jnp.dot(left, right, preferred_element_type=F32)


def head_cols(head):
    return slice(head * HD, (head + 1) * HD)


def totals_kernel(half, core_ref, keys_ref, gates_ref, mine_ref, theirs_ref, turned_ref, scale_ref, gated_ref):
    head = pl.program_id(0)
    block = keys_ref[...]
    turned = block.T
    turned_ref[0] = turned
    wide = turned.astype(F32)
    norm = jnp.sum(wide * wide, axis=0, keepdims=True) + EPS
    gate = gates_ref[pl.ds(head, 1), :]
    scale = gate / norm
    scale_ref[0] = scale
    gated_ref[0] = gate * lax.rsqrt(norm)
    high, low = two_terms(wide * scale)
    product = dot(jnp.concatenate([high, low], axis=0), block)
    gram = product[:HD] + product[HD:]
    own = core_ref[0] == head // half

    @pl.when(own)
    def _():
        mine_ref[lax.rem(head, half)] = gram

    @pl.when(jnp.logical_not(own))
    def _():
        theirs_ref[lax.rem(head, half)] = gram


def moment_kernel(turned_ref, gated_ref, values_ref, total_ref):
    high, low = two_terms(turned_ref[0].astype(F32) * gated_ref[0])
    product = dot(jnp.concatenate([high, low], axis=0), values_ref[...])
    total_ref[0] = (product[:HD] + product[HD:]).astype(BF16)


def local_kernel(blocks, turned_ref, scale_ref, gated_ref, keys_ref, values_ref, gram_ref, moment_ref, values_turned_ref):
    values_turned_ref[0] = values_ref[...].T
    gram_ref[0, 0] = jnp.zeros((HD, HD), F32)
    moment_ref[0, 0] = jnp.zeros((HD, HD), F32)
    for block in range(blocks - 1):
        span = slice(block * SPAN, (block + 1) * SPAN)
        keys = turned_ref[0, :, span].astype(F32)
        high, low = two_terms(keys * scale_ref[0, :, span])
        product = dot(jnp.concatenate([high, low], axis=0), keys_ref[span, :])
        gram_ref[0, block + 1] = gram_ref[0, block] + (product[:HD] + product[HD:])
        high, low = two_terms(keys * gated_ref[0, :, span])
        product = dot(jnp.concatenate([high, low], axis=0), values_ref[span, :])
        moment_ref[0, block + 1] = moment_ref[0, block] + (product[:HD] + product[HD:]).T


def masks_kernel(blocks, queries_ref, scale_ref, gated_ref, turned_ref, gram_mask_ref, moment_mask_ref):
    row = lax.broadcasted_iota(jnp.int32, (SPAN, SPAN), 0)
    column = lax.broadcasted_iota(jnp.int32, (SPAN, SPAN), 1)
    turned_ref[0] = queries_ref[...].T
    for block in range(blocks):
        span = slice(block * SPAN, (block + 1) * SPAN)
        for out_ref, factors in ((gram_mask_ref, scale_ref), (moment_mask_ref, gated_ref)):
            factor = jnp.broadcast_to(factors[0, :, span], (SPAN, SPAN)).T
            out_ref[0, block] = jnp.where(row <= column, factor, 0.0)


def solve_kernel(
    heads,
    blocks,
    core_ref,
    ridge_ref,
    queries_ref,
    keys_ref,
    turned_ref,
    gram_mask_ref,
    moment_mask_ref,
    local_ref,
    keep_ref,
    got_ref,
    high_ref,
    low_ref,
    corr_ref,
    first,
    second,
    xs,
    rs,
    ds,
    norms,
):
    core = core_ref[0]
    half = heads // 2
    row = lax.broadcasted_iota(jnp.int32, (SPAN, SPAN), 0)
    column = lax.broadcasted_iota(jnp.int32, (SPAN, SPAN), 1)
    units = [(head, block) for block in range(blocks) for head in range(heads)]
    count = len(units)
    for head in range(heads):
        prior = jnp.where(core == head // half, keep_ref[head % half], got_ref[head % half])
        prior = prior + jnp.where(row == column, ridge_ref[head], 0.0)
        for block in range(blocks):
            unit = block * heads + head
            rows = slice(block * SPAN, (block + 1) * SPAN)
            own = keys_ref[rows, head_cols(head)]
            high, low = two_terms(prior + local_ref[head, block])
            first[unit, :HD, :HD] = high
            first[unit, :HD, HD:] = high
            first[unit, HD:, :HD] = own
            first[unit, HD:, HD:] = own
            second[unit, :, :HD] = low
            second[unit, :, HD:] = turned_ref[head, :, rows]
            query = queries_ref[head, :, rows].astype(F32)
            query = query * lax.rsqrt(jnp.sum(query * query, axis=0, keepdims=True) + EPS)
            xs[unit] = jnp.zeros((HD, SPAN), F32)
            rs[unit] = query
            ds[unit] = query
            norms[unit] = jnp.sum(query * query, axis=0, keepdims=True)

    def product_of(unit):
        high, low = two_terms(ds[unit])
        return high, dot(first[unit], jnp.concatenate([high, low], axis=0))

    def image_of(unit, high, product):
        head, block = units[unit]
        corr = (product[HD:] * gram_mask_ref[head, block]).astype(BF16)
        return product[:HD] + dot(second[unit], jnp.concatenate([high, corr], axis=0))

    def update(unit, image):
        direction = ds[unit]
        now = norms[unit]
        step = now / (jnp.sum(direction * image, axis=0, keepdims=True) + EPS)
        xs[unit] += step * direction
        residual = rs[unit] - step * image
        rs[unit] = residual
        after = jnp.sum(residual * residual, axis=0, keepdims=True)
        ds[unit] = residual + (after / (now + EPS)) * direction
        norms[unit] = after

    lag = 4

    def sweep_once(sweep, carry):
        products, images = {}, {}
        for at in range(count + 2 * lag):
            if at < count:
                products[at] = product_of(at)
            if 0 <= at - lag < count:
                images[at - lag] = image_of(at - lag, *products.pop(at - lag))
            if 0 <= at - 2 * lag < count:
                update(at - 2 * lag, images.pop(at - 2 * lag))
        return carry

    lax.fori_loop(0, ITERS, sweep_once, 0)
    for unit, (head, block) in enumerate(units):
        rows = slice(block * SPAN, (block + 1) * SPAN)
        high, low = two_terms(xs[unit])
        corr = dot(first[unit, HD:], jnp.concatenate([high, low], axis=0))
        high_ref[head, :, rows] = high
        low_ref[head, :, rows] = low
        corr_ref[head, :, rows] = (corr * moment_mask_ref[head, block]).astype(BF16)


def project_kernel(
    heads,
    blocks,
    groups,
    group_ref,
    values_ref,
    high_ref,
    low_ref,
    corr_ref,
    local_ref,
    prior_ref,
    own_ref,
    *rest,
):
    others, out_ref = rest[: groups - 1], rest[groups - 1]
    readout = rest[groups]
    for head in range(heads):
        prior = prior_ref[head].T
        for block in range(blocks):
            rows = slice(block * SPAN, (block + 1) * SPAN)
            moment_high, moment_low = two_terms(prior + local_ref[head, block])
            left = jnp.concatenate([moment_high, moment_high, moment_low, values_ref[head, :, rows]], axis=1)
            high = high_ref[head, :, rows]
            right = jnp.concatenate([high, low_ref[head, :, rows], high, corr_ref[head, :, rows]], axis=0)
            readout[rows, head_cols(head)] = dot(left, right).T.astype(BF16)
    group = group_ref[0]
    width = own_ref.shape[1]
    for shift, part in enumerate((own_ref,) + tuple(others)):
        source = lax.rem(group + groups - shift, groups)
        columns = pl.ds(pl.multiple_of(source * width, width), width)
        out_ref[0, :, columns] = dot(readout[...], part[...]).astype(BF16)


def params():
    return pltpu.CompilerParams(vmem_limit_bytes=VMEM_LIMIT)


def cost(us):
    return pl.CostEstimate(flops=int(us * 1.1e9), bytes_accessed=int(us * 1e6), transcendentals=0)


def whole(shape):
    return pl.BlockSpec(shape, lambda *a: (0,) * len(shape))


def shards(mesh, queries, keys, values, gates, ridge, out_weight):
    tokens, width = queries.shape
    heads = width // HD
    half = heads // 2
    blocks = tokens // SPAN
    seq, groups = mesh.shape["seq"], mesh.shape["head"]
    columns = out_weight.shape[1]
    side = 4
    place = lax.axis_index("seq")
    core = lax.rem(place, 2)
    x_at = lax.rem(place // 2, side)
    y_at = place // (2 * side)
    group = lax.axis_index("head")
    core_arg = core.reshape(1).astype(jnp.int32)
    group_arg = group.reshape(1).astype(jnp.int32)
    smem = pl.BlockSpec(memory_space=pltpu.SMEM)

    def perm_core():
        return [(p, p ^ 1) for p in range(seq)]

    def perm_x(shift):
        return [(p, (p // 8) * 8 + ((p // 2 + shift) % side) * 2 + p % 2) for p in range(seq)]

    def perm_y(shift):
        return [(p, (p + 8 * shift) % seq) for p in range(seq)]

    def send(array, perm):
        return lax.ppermute(array, "seq", perm)

    parts = []
    for shift in range(1, groups):
        to = lax.rem(group + shift, groups)
        piece = lax.dynamic_slice_in_dim(out_weight, to * width, width, 0)
        parts.append(
            lax.ppermute(piece, "head", [(i, (i + shift) % groups) for i in range(groups)])
        )

    square = (half, HD, HD)
    by_head = pl.BlockSpec((tokens, HD), lambda h: (0, h))
    head_turned = pl.BlockSpec((1, HD, tokens), lambda h: (h, 0, 0))
    head_blocks = pl.BlockSpec((1, blocks, HD, HD), lambda h: (h, 0, 0, 0))
    turned_shape = jax.ShapeDtypeStruct((heads, HD, tokens), BF16)
    block_shape = jax.ShapeDtypeStruct((heads, blocks, HD, HD), F32)
    row = pl.BlockSpec((1, 1, tokens), lambda h: (h, 0, 0))
    row_shape = jax.ShapeDtypeStruct((heads, 1, tokens), F32)
    mine, theirs, keys_turned, scale, gated = pl.pallas_call(
        functools.partial(totals_kernel, half),
        grid=(heads,),
        in_specs=[smem, by_head, whole((heads, tokens))],
        out_specs=[whole(square), whole(square), head_turned, row, row],
        out_shape=[jax.ShapeDtypeStruct(square, F32)] * 2
        + [turned_shape, row_shape, row_shape],
        compiler_params=params(),
        cost_estimate=cost(3),
        name="totals",
    )(core_arg, keys, gates.T)

    moment_total = pl.pallas_call(
        moment_kernel,
        grid=(heads,),
        in_specs=[head_turned, row, by_head],
        out_specs=pl.BlockSpec((1, HD, HD), lambda h: (h, 0, 0)),
        out_shape=jax.ShapeDtypeStruct((heads, HD, HD), BF16),
        compiler_params=params(),
        cost_estimate=cost(3),
        name="moments",
    )(keys_turned, gated, values)

    def before_of(parts, at):
        return sum(jnp.where(at >= shift, part.astype(F32), 0.0) for shift, part in enumerate(parts, 1))

    def total_of(own, parts):
        return (own.astype(F32) + sum(part.astype(F32) for part in parts)).astype(own.dtype)

    received = send(theirs, perm_core())
    other = send(moment_total, perm_core())
    chip = (mine + received).astype(F16)
    chip, keys_turned_later = lax.optimization_barrier((chip, keys_turned))
    along = [send(chip, perm_x(shift)) for shift in range(1, side)]
    local_gram, local_moment, values_turned = pl.pallas_call(
        functools.partial(local_kernel, blocks),
        grid=(heads,),
        in_specs=[head_turned, row, row, by_head, by_head],
        out_specs=[head_blocks, head_blocks, head_turned],
        out_shape=[block_shape, block_shape, turned_shape],
        compiler_params=params(),
        cost_estimate=cost(5),
        name="local",
    )(keys_turned_later, scale, gated, keys, values)

    row_total = total_of(chip, along)
    moment_chip = (moment_total.astype(F32) + other.astype(F32)).astype(BF16)
    row_total, moment_chip, queries_later = lax.optimization_barrier((row_total, moment_chip, queries))
    above = [send(row_total, perm_y(shift)) for shift in range(1, side)]
    moment_along = [send(moment_chip, perm_x(shift)) for shift in range(1, side)]
    queries_turned, gram_mask, moment_mask = pl.pallas_call(
        functools.partial(masks_kernel, blocks),
        grid=(heads,),
        in_specs=[by_head, row, row],
        out_specs=[head_turned, head_blocks, head_blocks],
        out_shape=[turned_shape, block_shape, block_shape],
        compiler_params=params(),
        cost_estimate=cost(4),
        name="masks",
    )(queries_later, scale, gated)

    before = before_of(along, x_at) + before_of(above, y_at)
    keep = before + jnp.where(core == 1, received, 0.0)
    give = before + jnp.where(core == 0, mine, 0.0)
    got = send(give, perm_core())
    moment_row = total_of(moment_chip, moment_along)
    keep, got, moment_row, parts = lax.optimization_barrier((keep, got, moment_row, parts))
    moment_above = [send(moment_row, perm_y(shift)) for shift in range(1, side)]
    moment_before = before_of(moment_along, x_at) + jnp.where(core == 1, other, jnp.zeros_like(other)).astype(F32)

    step_blocks = 4
    step = step_blocks * SPAN
    units = heads * step_blocks
    tall = pl.BlockSpec((heads, HD, step), lambda b: (0, 0, b))
    some_blocks = pl.BlockSpec((heads, step_blocks, HD, HD), lambda b: (0, b, 0, 0))
    high, low, corr = pl.pallas_call(
        functools.partial(solve_kernel, heads, step_blocks),
        grid=(blocks // step_blocks,),
        in_specs=[
            smem,
            smem,
            tall,
            pl.BlockSpec((step, width), lambda b: (b, 0)),
            tall,
            some_blocks,
            some_blocks,
            some_blocks,
            whole(square),
            whole(square),
        ],
        out_specs=[tall] * 3,
        out_shape=[turned_shape] * 3,
        scratch_shapes=[
            pltpu.VMEM((units, 2 * HD, 2 * HD), BF16),
            pltpu.VMEM((units, HD, 2 * HD), BF16),
            pltpu.VMEM((units, HD, SPAN), F32),
            pltpu.VMEM((units, HD, SPAN), F32),
            pltpu.VMEM((units, HD, SPAN), F32),
            pltpu.VMEM((units, 1, SPAN), F32),
        ],
        compiler_params=params(),
        cost_estimate=cost(30),
        name="solve",
    )(core_arg, ridge, queries_turned, keys, keys_turned, gram_mask, moment_mask, local_gram, keep, got)

    moment_prior = moment_before + before_of(moment_above, y_at)
    out_blocks = 2
    step = out_blocks * SPAN
    tall = pl.BlockSpec((heads, HD, step), lambda b, g: (0, 0, b))
    out = pl.pallas_call(
        functools.partial(project_kernel, heads, out_blocks, groups),
        grid_spec=pltpu.PrefetchScalarGridSpec(
            num_scalar_prefetch=1,
            grid=(blocks // out_blocks,),
            in_specs=[
                tall,
                tall,
                tall,
                tall,
                pl.BlockSpec((heads, out_blocks, HD, HD), lambda b, g: (0, b, 0, 0)),
                whole((heads, HD, HD)),
                pl.BlockSpec((width, columns), lambda b, g: (g[0], 0)),
            ]
            + [whole((width, columns))] * (groups - 1),
            out_specs=pl.BlockSpec((1, step, columns * groups), lambda b, g: (0, b, 0)),
            scratch_shapes=[pltpu.VMEM((step, width), BF16)],
        ),
        out_shape=jax.ShapeDtypeStruct((1, tokens, columns * groups), BF16),
        compiler_params=params(),
        cost_estimate=cost(7),
        name="project",
    )(group_arg, values_turned, high, low, corr, local_moment, moment_prior, out_weight, *parts)
    return out


def solution(mesh):
    return jax.shard_map(
        functools.partial(shards, mesh),
        mesh=mesh,
        in_specs=(
            P("seq", "head"),
            P("seq", "head"),
            P("seq", "head"),
            P("seq", "head"),
            P("head"),
            P(None, "head"),
        ),
        out_specs=P("head", "seq", None),
        check_vma=False,
    )
```

time: 144 us -> 90.9 us (0.63)
  the two profiles are of different devices: /device:TPU:1 before, /device:TPU:40 now
where the time goes in v1:
time: 90.9 us; the launch traced here: 90.4 us
  Pallas kernels  52.9 us (58%)
  starting transfers between devices  21.8 us (24%)
  waiting for transfers between devices  12.8 us (14%)
  other arithmetic  1.79 us (2%)
  local copies, waits for them, and re-layouts  1.01 us (1%)
    pallas_call x1, Pallas kernels, shards(): pl.pallas_call(functools.partial(solve_kernel, heads, step_blocks), grid=...  26 us
    ppermute x15, starting transfers between devices, send(): return lax.ppermute(array, 'seq', perm)  16.1 us
    ppermute x15, waiting for transfers between devices, send(): return lax.ppermute(array, 'seq', perm)  12.8 us
    pallas_call x1, Pallas kernels, shards(): pl.pallas_call(functools.partial(project_kernel, heads, out_blocks, group...  8.42 us
    ppermute x3, starting transfers between devices, shards(): lax.ppermute(piece, 'head', [(i, (i + shift) % groups) for i in range(gro...  5.61 us
    pallas_call x1, Pallas kernels, shards(): pl.pallas_call(functools.partial(local_kernel, blocks), grid=(heads,), in...  5.4 us
    pallas_call x1, Pallas kernels, shards(): pl.pallas_call(functools.partial(masks_kernel, blocks), grid=(heads,), in...  4.74 us
    pallas_call x1, Pallas kernels, shards(): pl.pallas_call(functools.partial(totals_kernel, half), grid=(heads,), in_...  4.31 us
  transfers between devices with their start and end apart: 18, of which 4 were waited for; matrix products, arithmetic and copies ran while one was open for 2% of the time, Pallas kernels for 40%

profile of v1, /device:TPU:40, one launch (start us, length us, event | category | flops | bytes accessed | tf_op | source)
XLA Modules:
  0.0 90.4 jit_solution(389300422754059036)
XLA Ops:
  0.0 4.3 %totals.1 = (f32[2,128,128]{2,1,0:T(8,128)}, f32[2,128,128]{2,1,0:T(8,128)}, bf16[4,128,1024]{2,1,0:T(8,128)(2,1)}, f32[4,1,1024]{2,1,0:T(1,128)}, f32[4,1,1024]{2,1,0:T(1,128)}) custom-call(s32[1]{0:T(128)} %bitcast.1.core_ref, bf16[1024,512]{1,0:T(8,128)(2,1)} %keys_ref.5, f32[4,1024]{1,0:T(4,128)} %bitcast.3), custom_call_target="tpu_custom_call" | custom-call | flops 3300000000 | bytes 3000000 | tf_op jit(solution)/shard_map/totals/pallas_call | solution.py:272
  4.3 4.1 %moments.1 = bf16[4,128,128]{2,1,0:T(8,128)(2,1)} custom-call(bf16[4,128,1024]{2,1,0:T(8,128)(2,1)} %get-tuple-element.33.turned_ref, f32[4,1,1024]{2,1,0:T(1,128)} %get-tuple-element.35.gated_ref, bf16[1024,512]{1,0:T(8,128)(2,1)} %values_ref.3), custom_call_target="tpu_custom_call" | custom-call | flops 3300000000 | bytes 3000000 | tf_op jit(solution)/shard_map/moments/pallas_call | solution.py:284
  8.4 0.0 collective-permute-start.4
  8.4 0.5 collective-permute-start
  8.9 1.0 %constant_dynamic-slice_fusion = (bf16[512,512]{1,0:T(8,128)(2,1)}, bf16[512,512]{1,0:T(8,128)(2,1)S(1)}, bf16[512,512]{1,0:T(8,128)(2,1)S(1)}) fusion(bf16[2048,512]{1,0:T(8,128)(2,1)S(1)} %copy-done, s32[]{:T(128)S(6)} %select_n.133, s32[]{:T(128)S(6)} %select_n.132, s32[]{:T(128)S(6)} %select_n.131), kind=kLoop, calls=%fused_computation.25 | loop fusion | bytes 3145740 | tf_op jit(solution)/shard_map/dynamic_slice | solution.py:259
  9.9 0.1 collective-permute-start.14
  10.0 3.3 %collective-permute-start.13 = (bf16[512,512]{1,0:T(8,128)(2,1)S(1)}, bf16[512,512]{1,0:T(8,128)(2,1)S(1)}, u32[]{:S(2)}, u32[]{:S(2)}) collective-permute-start(bf16[512,512]{1,0:T(8,128)(2,1)S(1)} %get-tuple-element.58), channel_id=1, source_target_pairs={{0,2},{1,3},{2,0},{3,1},{4,6},{5,7},{6,4},{7,5},{8,10},{9,11},{10,... | collective-permute-start | bytes 1572872 | tf_op jit(solution)/shard_map/ppermute | solution.py:261
  13.3 0.0 collective-permute-done
  13.3 2.8 %collective-permute-start.3 = (f16[2,128,128]{2,1,0:T(8,128)(2,1)S(1)}, f16[2,128,128]{2,1,0:T(8,128)(2,1)S(1)}, u32[]{:S(2)}, u32[]{:S(2)}) collective-permute-start(f16[2,128,128]{2,1,0:T(8,128)(2,1)S(1)} %add_convert_fusion.1), channel_id=1, source_target_pairs={{0,24},{4,28},{8,0},{12,4},{16,8},{20,12},{24,16},{28,20},{32,56},... | collective-permute-start | bytes 196616 | tf_op jit(solution)/shard_map/ppermute | solution.py:254
  16.1 0.8 collective-permute-start.2
  16.9 5.4 %local.1 = (f32[4,8,128,128]{3,2,1,0:T(8,128)}, f32[4,8,128,128]{3,2,1,0:T(8,128)}, bf16[4,128,1024]{2,1,0:T(8,128)(2,1)}) custom-call(bf16[4,128,1024]{2,1,0:T(8,128)(2,1)} %get-tuple-element.33.turned_ref, f32[4,1,1024]{2,1,0:T(1,128)} %get-tuple-element.34.scale_ref, f32[4,1,1024]{2,1,0:T(1,128)} %get-tuple-element.35.gated_ref, ...), custom_call_target="tpu_custom_call" | custom-call | flops 5500000256 | bytes 5000000 | tf_op jit(solution)/shard_map/local/pallas_call | solution.py:306
  22.3 0.0 collective-permute-done.4
  22.3 1.0 %collective-permute-start.1 = (f16[2,128,128]{2,1,0:T(8,128)(2,1)S(1)}, f16[2,128,128]{2,1,0:T(8,128)(2,1)S(1)}, u32[]{:S(2)}, u32[]{:S(2)}) collective-permute-start(f16[2,128,128]{2,1,0:T(8,128)(2,1)S(1)} %add_convert_fusion.1), channel_id=1, source_target_pairs={{0,8},{4,12},{8,16},{12,20},{16,24},{20,28},{24,0},{28,4},{32,40},... | collective-permute-start | bytes 196616 | tf_op jit(solution)/shard_map/ppermute | solution.py:254
  23.3 0.0 copy-done.2
  23.3 0.0 collective-permute-done.3
  23.3 0.0 collective-permute-done.2
  23.3 4.5 %collective-permute-done.1 = f16[2,128,128]{2,1,0:T(8,128)(2,1)S(1)} collective-permute-done((f16[2,128,128]{2,1,0:T(8,128)(2,1)S(1)}, f16[2,128,128]{2,1,0:T(8,128)(2,1)S(1)}, u32[]{:S(2)}, u32[]{:S(2)}) %collective-permute-start.1) | collective-permute-done | bytes 65568 | tf_op jit(solution)/shard_map/ppermute | solution.py:254
  27.9 0.5 collective-permute-start.7
  28.4 2.6 %collective-permute-start.6 = (f16[2,128,128]{2,1,0:T(8,128)(2,1)S(1)}, f16[2,128,128]{2,1,0:T(8,128)(2,1)S(1)}, u32[]{:S(2)}, u32[]{:S(2)}) collective-permute-start(f16[2,128,128]{2,1,0:T(8,128)(2,1)S(1)} %fusion.10), channel_id=1, source_target_pairs={{0,64},{4,68},{8,72},{12,76},{16,80},{20,84},{24,88},{28,92},{32,9... | collective-permute-start | bytes 196616 | tf_op jit(solution)/shard_map/ppermute | solution.py:254
  31.0 1.9 %collective-permute-start.5 = (f16[2,128,128]{2,1,0:T(8,128)(2,1)S(1)}, f16[2,128,128]{2,1,0:T(8,128)(2,1)S(1)}, u32[]{:S(2)}, u32[]{:S(2)}) collective-permute-start(f16[2,128,128]{2,1,0:T(8,128)(2,1)S(1)} %fusion.10), channel_id=1, source_target_pairs={{0,32},{4,36},{8,40},{12,44},{16,48},{20,52},{24,56},{28,60},{32,6... | collective-permute-start | bytes 196616 | tf_op jit(solution)/shard_map/ppermute | solution.py:254
  32.9 4.7 %masks.1 = (bf16[4,128,1024]{2,1,0:T(8,128)(2,1)}, f32[4,8,128,128]{3,2,1,0:T(8,128)}, f32[4,8,128,128]{3,2,1,0:T(8,128)}) custom-call(bf16[1024,512]{1,0:T(8,128)(2,1)} %queries_ref, f32[4,1,1024]{2,1,0:T(1,128)} %get-tuple-element.34.scale_ref, f32[4,1,1024]{2,1,0:T(1,128)} %get-tuple-element.35.gated_ref), custom_call_target="tpu_custom_call" | custom-call | flops 4400000000 | bytes 4000000 | tf_op jit(solution)/shard_map/masks/pallas_call | solution.py:322
  37.7 0.0 collective-permute-done.7
  37.7 2.2 %collective-permute-start.12 = (bf16[512,512]{1,0:T(8,128)(2,1)S(1)}, bf16[512,512]{1,0:T(8,128)(2,1)S(1)}, u32[]{:S(2)}, u32[]{:S(2)}) collective-permute-start(bf16[512,512]{1,0:T(8,128)(2,1)S(1)} %get-tuple-element.59), channel_id=1, source_target_pairs={{0,1},{1,2},{2,3},{3,0},{4,5},{5,6},{6,7},{7,4},{8,9},{9,10},{10,1... | collective-permute-start | bytes 1572872 | tf_op jit(solution)/shard_map/ppermute | solution.py:261
  39.9 0.0 collective-permute-done.6
  39.9 0.1 collective-permute-start.11
  40.0 0.0 collective-permute-done.5
  40.0 1.7 %collective-permute-start.10 = (bf16[4,128,128]{2,1,0:T(8,128)(2,1)S(1)}, bf16[4,128,128]{2,1,0:T(8,128)(2,1)S(1)}, u32[]{:S(2)}, u32[]{:S(2)}) collective-permute-start(bf16[4,128,128]{2,1,0:T(8,128)(2,1)S(1)} %add_convert_fusion), channel_id=1, source_target_pairs={{0,16},{4,20},{8,24},{12,28},{16,0},{20,4},{24,8},{28,12},{32,48},... | collective-permute-start | bytes 393224 | tf_op jit(solution)/shard_map/ppermute | solution.py:254
  41.6 0.1 select_add_fusion
  41.7 3.1 %collective-permute-done.11 = bf16[4,128,128]{2,1,0:T(8,128)(2,1)S(1)} collective-permute-done((bf16[4,128,128]{2,1,0:T(8,128)(2,1)S(1)}, bf16[4,128,128]{2,1,0:T(8,128)(2,1)S(1)}, u32[]{:S(2)}, u32[]{:S(2)}) %collective-permute-start.11) | collective-permute-done | bytes 131104 | tf_op jit(solution)/shard_map/ppermute | solution.py:254
  44.9 0.4 collective-permute-start.9
  45.2 0.7 select_add_fusion.1.keep_ref
  45.9 1.2 %collective-permute-done.10 = bf16[4,128,128]{2,1,0:T(8,128)(2,1)S(1)} collective-permute-done((bf16[4,128,128]{2,1,0:T(8,128)(2,1)S(1)}, bf16[4,128,128]{2,1,0:T(8,128)(2,1)S(1)}, u32[]{:S(2)}, u32[]{:S(2)}) %collective-permute-start.10) | collective-permute-done | bytes 131104 | tf_op jit(solution)/shard_map/ppermute | solution.py:254
  47.1 0.0 collective-permute-start.8
  47.1 4.0 %collective-permute-done.9 = bf16[4,128,128]{2,1,0:T(8,128)(2,1)S(1)} collective-permute-done((bf16[4,128,128]{2,1,0:T(8,128)(2,1)S(1)}, bf16[4,128,128]{2,1,0:T(8,128)(2,1)S(1)}, u32[]{:S(2)}, u32[]{:S(2)}) %collective-permute-start.9) | collective-permute-done | bytes 131104 | tf_op jit(solution)/shard_map/ppermute | solution.py:254
  51.0 0.1 fusion.5
  51.1 0.0 collective-permute-done.8.got_ref
  51.1 0.0 collective-permute-done.14.rest_2_
  51.2 0.0 collective-permute-done.13.rest_1_
  51.2 0.0 collective-permute-done.12.rest_0_
  51.2 0.2 collective-permute-start.17
  51.4 1.3 %collective-permute-start.16 = (bf16[4,128,128]{2,1,0:T(8,128)(2,1)S(1)}, bf16[4,128,128]{2,1,0:T(8,128)(2,1)S(1)}, u32[]{:S(2)}, u32[]{:S(2)}) collective-permute-start(bf16[4,128,128]{2,1,0:T(8,128)(2,1)S(1)} %fusion.5), channel_id=1, source_target_pairs={{0,64},{4,68},{8,72},{12,76},{16,80},{20,84},{24,88},{28,92},{32,9... | collective-permute-start | bytes 393224 | tf_op jit(solution)/shard_map/ppermute | solution.py:254
  52.7 2.4 %collective-permute-start.15 = (bf16[4,128,128]{2,1,0:T(8,128)(2,1)S(1)}, bf16[4,128,128]{2,1,0:T(8,128)(2,1)S(1)}, u32[]{:S(2)}, u32[]{:S(2)}) collective-permute-start(bf16[4,128,128]{2,1,0:T(8,128)(2,1)S(1)} %fusion.5), channel_id=1, source_target_pairs={{0,32},{4,36},{8,40},{12,44},{16,48},{20,52},{24,56},{28,60},{32,6... | collective-permute-start | bytes 393224 | tf_op jit(solution)/shard_map/ppermute | solution.py:254
  55.1 26.0 %solve.1 = (bf16[4,128,1024]{2,1,0:T(8,128)(2,1)}, bf16[4,128,1024]{2,1,0:T(8,128)(2,1)}, bf16[4,128,1024]{2,1,0:T(8,128)(2,1)}) custom-call(s32[1]{0:T(128)} %bitcast.1.core_ref, f32[4]{0:T(128)} %ridge_ref.1, bf16[4,128,1024]{2,1,0:T(8,128)(2,1)} %get-tuple-element.39.queries_ref, bf16[1024,512]{1,0:T(8,128)(2,1)} %keys_ref.5, ...), custom_call_target="tpu_custom_call" | custom-call | flops 32999999488 | bytes 30000000 | tf_op jit(solution)/shard_map/solve/pallas_call | solution.py:347
  81.1 0.0 collective-permute-done.17
  81.1 0.0 collective-permute-done.16
  81.1 0.0 collective-permute-done.15
  81.1 0.9 fusion.3.prior_ref
  82.0 8.4 %project.1 = bf16[1,1024,2048]{2,1,0:T(8,128)(2,1)} custom-call(s32[1]{0:T(128)} %bitcast.group_ref, bf16[4,128,1024]{2,1,0:T(8,128)(2,1)} %get-tuple-element.36.values_ref, bf16[4,128,1024]{2,1,0:T(8,128)(2,1)} %get-tuple-element.47.high_ref, bf16[4,128,1024]{2,1,0:T(8,128)(2,1)} %get-tuple-element.48.low_ref, ...), custom_call_target="tpu_custom_call" | custom-call | flops 7699999744 | bytes 7000000 | tf_op jit(solution)/shard_map/project/pallas_call | solution.py:381
  (16 shorter events, 0.1 us)
Async XLA Ops:
  4.3 4.6 %copy-start = (bf16[2048,512]{1,0:T(8,128)(2,1)S(1)}, bf16[2048,512]{1,0:T(8,128)(2,1)}, u32[]{:S(2)}) copy-start(bf16[2048,512]{1,0:T(8,128)(2,1)} %own_ref.1) | copy-start | bytes 6291460
  8.4 4.9 %copy-start.1 = (f32[2,128,128]{2,1,0:T(8,128)S(1)}, f32[2,128,128]{2,1,0:T(8,128)}, u32[]{:S(2)}) copy-start(f32[2,128,128]{2,1,0:T(8,128)} %get-tuple-element.30) | copy-start | bytes 393220
  8.4 13.9 %collective-permute-start.4 = (bf16[4,128,128]{2,1,0:T(8,128)(2,1)}, bf16[4,128,128]{2,1,0:T(8,128)(2,1)S(1)}, u32[]{:S(2)}, u32[]{:S(2)}) collective-permute-start(bf16[4,128,128]{2,1,0:T(8,128)(2,1)} %moments.1), channel_id=1, source_target_pairs={{0,4},{4,0},{8,12},{12,8},{16,20},{20,16},{24,28},{28,24},{32,36},... | collective-permute-start | bytes 393224 | tf_op jit(solution)/shard_map/ppermute | solution.py:254
  8.4 4.9 %collective-permute-start = (f32[2,128,128]{2,1,0:T(8,128)}, f32[2,128,128]{2,1,0:T(8,128)S(1)}, u32[]{:S(2)}, u32[]{:S(2)}) collective-permute-start(f32[2,128,128]{2,1,0:T(8,128)} %get-tuple-element.31), channel_id=1, source_target_pairs={{0,4},{4,0},{8,12},{12,8},{16,20},{20,16},{24,28},{28,24},{32,36},... | collective-permute-start | bytes 393224 | tf_op jit(solution)/shard_map/ppermute | solution.py:254
  9.9 41.3 %collective-permute-start.14 = (bf16[512,512]{1,0:T(8,128)(2,1)}, bf16[512,512]{1,0:T(8,128)(2,1)S(1)}, u32[]{:S(2)}, u32[]{:S(2)}) collective-permute-start(bf16[512,512]{1,0:T(8,128)(2,1)} %get-tuple-element.57), channel_id=1, source_target_pairs={{0,3},{1,0},{2,1},{3,2},{4,7},{5,4},{6,5},{7,6},{8,11},{9,8},{10,9... | collective-permute-start | bytes 1572872 | tf_op jit(solution)/shard_map/ppermute | solution.py:261
  10.0 41.2 %collective-permute-start.13 = (bf16[512,512]{1,0:T(8,128)(2,1)S(1)}, bf16[512,512]{1,0:T(8,128)(2,1)S(1)}, u32[]{:S(2)}, u32[]{:S(2)}) collective-permute-start(bf16[512,512]{1,0:T(8,128)(2,1)S(1)} %get-tuple-element.58), channel_id=1, source_target_pairs={{0,2},{1,3},{2,0},{3,1},{4,6},{5,7},{6,4},{7,5},{8,10},{9,11},{10,... | collective-permute-start | bytes 1572872 | tf_op jit(solution)/shard_map/ppermute | solution.py:261
  13.3 10.0 %collective-permute-start.3 = (f16[2,128,128]{2,1,0:T(8,128)(2,1)S(1)}, f16[2,128,128]{2,1,0:T(8,128)(2,1)S(1)}, u32[]{:S(2)}, u32[]{:S(2)}) collective-permute-start(f16[2,128,128]{2,1,0:T(8,128)(2,1)S(1)} %add_convert_fusion.1), channel_id=1, source_target_pairs={{0,24},{4,28},{8,0},{12,4},{16,8},{20,12},{24,16},{28,20},{32,56},... | collective-permute-start | bytes 196616 | tf_op jit(solution)/shard_map/ppermute | solution.py:254
  16.1 7.2 %collective-permute-start.2 = (f16[2,128,128]{2,1,0:T(8,128)(2,1)S(1)}, f16[2,128,128]{2,1,0:T(8,128)(2,1)S(1)}, u32[]{:S(2)}, u32[]{:S(2)}) collective-permute-start(f16[2,128,128]{2,1,0:T(8,128)(2,1)S(1)} %add_convert_fusion.1), channel_id=1, source_target_pairs={{0,16},{4,20},{8,24},{12,28},{16,0},{20,4},{24,8},{28,12},{32,48},... | collective-permute-start | bytes 196616 | tf_op jit(solution)/shard_map/ppermute | solution.py:254
  16.9 6.4 %copy-start.2 = (bf16[4,128,128]{2,1,0:T(8,128)(2,1)S(1)}, bf16[4,128,128]{2,1,0:T(8,128)(2,1)}, u32[]{:S(2)}) copy-start(bf16[4,128,128]{2,1,0:T(8,128)(2,1)} %moments.1) | copy-start | bytes 393220
  22.3 5.5 %collective-permute-start.1 = (f16[2,128,128]{2,1,0:T(8,128)(2,1)S(1)}, f16[2,128,128]{2,1,0:T(8,128)(2,1)S(1)}, u32[]{:S(2)}, u32[]{:S(2)}) collective-permute-start(f16[2,128,128]{2,1,0:T(8,128)(2,1)S(1)} %add_convert_fusion.1), channel_id=1, source_target_pairs={{0,8},{4,12},{8,16},{12,20},{16,24},{20,28},{24,0},{28,4},{32,40},... | collective-permute-start | bytes 196616 | tf_op jit(solution)/shard_map/ppermute | solution.py:254
  27.9 9.7 %collective-permute-start.7 = (f16[2,128,128]{2,1,0:T(8,128)(2,1)S(1)}, f16[2,128,128]{2,1,0:T(8,128)(2,1)S(1)}, u32[]{:S(2)}, u32[]{:S(2)}) collective-permute-start(f16[2,128,128]{2,1,0:T(8,128)(2,1)S(1)} %fusion.10), channel_id=1, source_target_pairs={{0,96},{4,100},{8,104},{12,108},{16,112},{20,116},{24,120},{28,124... | collective-permute-start | bytes 196616 | tf_op jit(solution)/shard_map/ppermute | solution.py:254
  28.4 11.5 %collective-permute-start.6 = (f16[2,128,128]{2,1,0:T(8,128)(2,1)S(1)}, f16[2,128,128]{2,1,0:T(8,128)(2,1)S(1)}, u32[]{:S(2)}, u32[]{:S(2)}) collective-permute-start(f16[2,128,128]{2,1,0:T(8,128)(2,1)S(1)} %fusion.10), channel_id=1, source_target_pairs={{0,64},{4,68},{8,72},{12,76},{16,80},{20,84},{24,88},{28,92},{32,9... | collective-permute-start | bytes 196616 | tf_op jit(solution)/shard_map/ppermute | solution.py:254
  31.0 8.9 %collective-permute-start.5 = (f16[2,128,128]{2,1,0:T(8,128)(2,1)S(1)}, f16[2,128,128]{2,1,0:T(8,128)(2,1)S(1)}, u32[]{:S(2)}, u32[]{:S(2)}) collective-permute-start(f16[2,128,128]{2,1,0:T(8,128)(2,1)S(1)} %fusion.10), channel_id=1, source_target_pairs={{0,32},{4,36},{8,40},{12,44},{16,48},{20,52},{24,56},{28,60},{32,6... | collective-permute-start | bytes 196616 | tf_op jit(solution)/shard_map/ppermute | solution.py:254
  37.7 13.5 %collective-permute-start.12 = (bf16[512,512]{1,0:T(8,128)(2,1)S(1)}, bf16[512,512]{1,0:T(8,128)(2,1)S(1)}, u32[]{:S(2)}, u32[]{:S(2)}) collective-permute-start(bf16[512,512]{1,0:T(8,128)(2,1)S(1)} %get-tuple-element.59), channel_id=1, source_target_pairs={{0,1},{1,2},{2,3},{3,0},{4,5},{5,6},{6,7},{7,4},{8,9},{9,10},{10,1... | collective-permute-start | bytes 1572872 | tf_op jit(solution)/shard_map/ppermute | solution.py:261
  39.9 5.0 %collective-permute-start.11 = (bf16[4,128,128]{2,1,0:T(8,128)(2,1)S(1)}, bf16[4,128,128]{2,1,0:T(8,128)(2,1)S(1)}, u32[]{:S(2)}, u32[]{:S(2)}) collective-permute-start(bf16[4,128,128]{2,1,0:T(8,128)(2,1)S(1)} %add_convert_fusion), channel_id=1, source_target_pairs={{0,24},{4,28},{8,0},{12,4},{16,8},{20,12},{24,16},{28,20},{32,56},... | collective-permute-start | bytes 393224 | tf_op jit(solution)/shard_map/ppermute | solution.py:254
  40.0 7.1 %collective-permute-start.10 = (bf16[4,128,128]{2,1,0:T(8,128)(2,1)S(1)}, bf16[4,128,128]{2,1,0:T(8,128)(2,1)S(1)}, u32[]{:S(2)}, u32[]{:S(2)}) collective-permute-start(bf16[4,128,128]{2,1,0:T(8,128)(2,1)S(1)} %add_convert_fusion), channel_id=1, source_target_pairs={{0,16},{4,20},{8,24},{12,28},{16,0},{20,4},{24,8},{28,12},{32,48},... | collective-permute-start | bytes 393224 | tf_op jit(solution)/shard_map/ppermute | solution.py:254
  44.9 6.2 %collective-permute-start.9 = (bf16[4,128,128]{2,1,0:T(8,128)(2,1)S(1)}, bf16[4,128,128]{2,1,0:T(8,128)(2,1)S(1)}, u32[]{:S(2)}, u32[]{:S(2)}) collective-permute-start(bf16[4,128,128]{2,1,0:T(8,128)(2,1)S(1)} %add_convert_fusion), channel_id=1, source_target_pairs={{0,8},{4,12},{8,16},{12,20},{16,24},{20,28},{24,0},{28,4},{32,40},... | collective-permute-start | bytes 393224 | tf_op jit(solution)/shard_map/ppermute | solution.py:254
  47.1 4.0 %collective-permute-start.8 = (f32[2,128,128]{2,1,0:T(8,128)S(1)}, f32[2,128,128]{2,1,0:T(8,128)S(1)}, u32[]{:S(2)}, u32[]{:S(2)}) collective-permute-start(f32[2,128,128]{2,1,0:T(8,128)S(1)} %get-tuple-element.55), channel_id=1, source_target_pairs={{0,4},{4,0},{8,12},{12,8},{16,20},{20,16},{24,28},{28,24},{32,36},... | collective-permute-start | bytes 393224 | tf_op jit(solution)/shard_map/ppermute | solution.py:254
  51.1 4.0 %copy-start.6 = (f32[2,128,128]{2,1,0:T(8,128)}, f32[2,128,128]{2,1,0:T(8,128)S(1)}, u32[]{:S(2)}) copy-start(f32[2,128,128]{2,1,0:T(8,128)S(1)} %collective-permute-done.8.got_ref) | copy-start | bytes 393220
  51.1 29.9 %copy-start.3 = (bf16[512,512]{1,0:T(8,128)(2,1)}, bf16[512,512]{1,0:T(8,128)(2,1)S(1)}, u32[]{:S(2)}) copy-start(bf16[512,512]{1,0:T(8,128)(2,1)S(1)} %collective-permute-done.14.rest_2_) | copy-start | bytes 1572868
  51.2 29.9 %copy-start.4 = (bf16[512,512]{1,0:T(8,128)(2,1)}, bf16[512,512]{1,0:T(8,128)(2,1)S(1)}, u32[]{:S(2)}) copy-start(bf16[512,512]{1,0:T(8,128)(2,1)S(1)} %collective-permute-done.13.rest_1_) | copy-start | bytes 1572868
  51.2 29.9 %copy-start.5 = (bf16[512,512]{1,0:T(8,128)(2,1)}, bf16[512,512]{1,0:T(8,128)(2,1)S(1)}, u32[]{:S(2)}) copy-start(bf16[512,512]{1,0:T(8,128)(2,1)S(1)} %collective-permute-done.12.rest_0_) | copy-start | bytes 1572868
  51.2 29.9 %collective-permute-start.17 = (bf16[4,128,128]{2,1,0:T(8,128)(2,1)S(1)}, bf16[4,128,128]{2,1,0:T(8,128)(2,1)S(1)}, u32[]{:S(2)}, u32[]{:S(2)}) collective-permute-start(bf16[4,128,128]{2,1,0:T(8,128)(2,1)S(1)} %fusion.5), channel_id=1, source_target_pairs={{0,96},{4,100},{8,104},{12,108},{16,112},{20,116},{24,120},{28,124... | collective-permute-start | bytes 393224 | tf_op jit(solution)/shard_map/ppermute | solution.py:254
  51.4 29.7 %collective-permute-start.16 = (bf16[4,128,128]{2,1,0:T(8,128)(2,1)S(1)}, bf16[4,128,128]{2,1,0:T(8,128)(2,1)S(1)}, u32[]{:S(2)}, u32[]{:S(2)}) collective-permute-start(bf16[4,128,128]{2,1,0:T(8,128)(2,1)S(1)} %fusion.5), channel_id=1, source_target_pairs={{0,64},{4,68},{8,72},{12,76},{16,80},{20,84},{24,88},{28,92},{32,9... | collective-permute-start | bytes 393224 | tf_op jit(solution)/shard_map/ppermute | solution.py:254
  52.7 28.4 %collective-permute-start.15 = (bf16[4,128,128]{2,1,0:T(8,128)(2,1)S(1)}, bf16[4,128,128]{2,1,0:T(8,128)(2,1)S(1)}, u32[]{:S(2)}, u32[]{:S(2)}) collective-permute-start(bf16[4,128,128]{2,1,0:T(8,128)(2,1)S(1)} %fusion.5), channel_id=1, source_target_pairs={{0,32},{4,36},{8,40},{12,44},{16,48},{20,52},{24,56},{28,60},{32,6... | collective-permute-start | bytes 393224 | tf_op jit(solution)/shard_map/ppermute | solution.py:254

commit v2 on v1

--- a/solution.py
+++ b/solution.py
@@ -13,6 +13,7 @@
 F32 = jnp.float32
 BF16 = jnp.bfloat16
 F16 = jnp.float16
+SHRINK = 16.0
 VMEM_LIMIT = 56 * 1024 * 1024
 
 
@@ -29,35 +30,38 @@
     return slice(head * HD, (head + 1) * HD)
 
 
-def totals_kernel(half, core_ref, keys_ref, gates_ref, mine_ref, theirs_ref, turned_ref, scale_ref, gated_ref):
-    head = pl.program_id(0)
-    block = keys_ref[...]
-    turned = block.T
-    turned_ref[0] = turned
-    wide = turned.astype(F32)
-    norm = jnp.sum(wide * wide, axis=0, keepdims=True) + EPS
-    gate = gates_ref[pl.ds(head, 1), :]
-    scale = gate / norm
-    scale_ref[0] = scale
-    gated_ref[0] = gate * lax.rsqrt(norm)
-    high, low = two_terms(wide * scale)
-    product = dot(jnp.concatenate([high, low], axis=0), block)
-    gram = product[:HD] + product[HD:]
-    own = core_ref[0] == head // half
+def totals_kernel(
+    half, core_ref, keys_ref, values_ref, gates_ref, mine_ref, theirs_ref, turned_ref, scale_ref, gated_ref
+):
+    step = pl.program_id(0)
+    gates = gates_ref[pl.ds(step, 1)][0]
+    lefts = []
+    for head in range(half):
+        turned = keys_ref[:, head_cols(head)].T
+        turned_ref[head] = turned
+        wide = turned.astype(F32)
+        norm = jnp.sum(wide * wide, axis=0, keepdims=True) + EPS
+        gate = gates[head : head + 1]
+        scale = gate / norm
+        gated = gate * lax.rsqrt(norm)
+        scale_ref[head] = scale
+        gated_ref[head] = gated
+        for factor in (scale, gated * (1.0 / SHRINK)):
+            lefts.append(jnp.concatenate(two_terms(wide * factor), axis=0))
+    grams = [dot(lefts[2 * head], keys_ref[:, head_cols(head)]) for head in range(half)]
+    moments = [dot(lefts[2 * head + 1], values_ref[:, head_cols(head)]) for head in range(half)]
+    sums = [product[:HD] + product[HD:] for product in grams + moments]
+    own = core_ref[0] == step
 
     @pl.when(own)
     def _():
-        mine_ref[lax.rem(head, half)] = gram
+        for at, value in enumerate(sums):
+            mine_ref[at] = value
 
     @pl.when(jnp.logical_not(own))
     def _():
-        theirs_ref[lax.rem(head, half)] = gram
-
-
-def moment_kernel(turned_ref, gated_ref, values_ref, total_ref):
-    high, low = two_terms(turned_ref[0].astype(F32) * gated_ref[0])
-    product = dot(jnp.concatenate([high, low], axis=0), values_ref[...])
-    total_ref[0] = (product[:HD] + product[HD:]).astype(BF16)
+        for at, value in enumerate(sums):
+            theirs_ref[at] = value
 
 
 def local_kernel(blocks, turned_ref, scale_ref, gated_ref, keys_ref, values_ref, gram_ref, moment_ref, values_turned_ref):
@@ -183,28 +187,38 @@
     heads,
     blocks,
     groups,
-    group_ref,
+    place_ref,
     values_ref,
     high_ref,
     low_ref,
     corr_ref,
     local_ref,
-    prior_ref,
+    keep_ref,
+    got_ref,
     own_ref,
     *rest,
 ):
     others, out_ref = rest[: groups - 1], rest[groups - 1]
-    readout = rest[groups]
-    for head in range(heads):
-        prior = prior_ref[head].T
-        for block in range(blocks):
-            rows = slice(block * SPAN, (block + 1) * SPAN)
-            moment_high, moment_low = two_terms(prior + local_ref[head, block])
-            left = jnp.concatenate([moment_high, moment_high, moment_low, values_ref[head, :, rows]], axis=1)
-            high = high_ref[head, :, rows]
-            right = jnp.concatenate([high, low_ref[head, :, rows], high, corr_ref[head, :, rows]], axis=0)
-            readout[rows, head_cols(head)] = dot(left, right).T.astype(BF16)
-    group = group_ref[0]
+    readout, prior = rest[groups], rest[groups + 1]
+    half = heads // 2
+
+    @pl.when(pl.program_id(0) == 0)
+    def _():
+        for head in range(heads):
+            at = half + head % half
+            prior[head] = jnp.where(place_ref[1] == head // half, keep_ref[at], got_ref[at]).T * SHRINK
+
+    units = [(head, slice(block * SPAN, (block + 1) * SPAN), block) for head in range(heads) for block in range(blocks)]
+    products = []
+    for head, rows, block in units:
+        moment_high, moment_low = two_terms(prior[head] + local_ref[head, block])
+        left = jnp.concatenate([moment_high, moment_high, moment_low, values_ref[head, :, rows]], axis=1)
+        high = high_ref[head, :, rows]
+        right = jnp.concatenate([high, low_ref[head, :, rows], high, corr_ref[head, :, rows]], axis=0)
+        products.append(dot(left, right))
+    for (head, rows, block), product in zip(units, products):
+        readout[rows, head_cols(head)] = product.T.astype(BF16)
+    group = place_ref[0]
     width = own_ref.shape[1]
     for shift, part in enumerate((own_ref,) + tuple(others)):
         source = lax.rem(group + groups - shift, groups)
@@ -238,7 +252,7 @@
     y_at = place // (2 * side)
     group = lax.axis_index("head")
     core_arg = core.reshape(1).astype(jnp.int32)
-    group_arg = group.reshape(1).astype(jnp.int32)
+    place_arg = jnp.stack([group, core]).astype(jnp.int32)
     smem = pl.BlockSpec(memory_space=pltpu.SMEM)
 
     def perm_core():
@@ -253,56 +267,45 @@
     def send(array, perm):
         return lax.ppermute(array, "seq", perm)
 
-    parts = []
-    for shift in range(1, groups):
-        to = lax.rem(group + shift, groups)
-        piece = lax.dynamic_slice_in_dim(out_weight, to * width, width, 0)
-        parts.append(
-            lax.ppermute(piece, "head", [(i, (i + shift) % groups) for i in range(groups)])
-        )
-
-    square = (half, HD, HD)
+    def rows_from(shift, weight):
+        piece = lax.dynamic_slice_in_dim(weight, lax.rem(group + shift, groups) * width, width, 0)
+        return lax.ppermute(piece, "head", [(i, (i + shift) % groups) for i in range(groups)])
+
+    sums = (2 * half, HD, HD)
     by_head = pl.BlockSpec((tokens, HD), lambda h: (0, h))
     head_turned = pl.BlockSpec((1, HD, tokens), lambda h: (h, 0, 0))
     head_blocks = pl.BlockSpec((1, blocks, HD, HD), lambda h: (h, 0, 0, 0))
+    row = pl.BlockSpec((1, 1, tokens), lambda h: (h, 0, 0))
+    row_shape = jax.ShapeDtypeStruct((heads, 1, tokens), F32)
     turned_shape = jax.ShapeDtypeStruct((heads, HD, tokens), BF16)
     block_shape = jax.ShapeDtypeStruct((heads, blocks, HD, HD), F32)
-    row = pl.BlockSpec((1, 1, tokens), lambda h: (h, 0, 0))
-    row_shape = jax.ShapeDtypeStruct((heads, 1, tokens), F32)
+    by_half = pl.BlockSpec((tokens, half * HD), lambda s: (0, s))
+    half_row = pl.BlockSpec((half, 1, tokens), lambda s: (s, 0, 0))
     mine, theirs, keys_turned, scale, gated = pl.pallas_call(
         functools.partial(totals_kernel, half),
-        grid=(heads,),
-        in_specs=[smem, by_head, whole((heads, tokens))],
-        out_specs=[whole(square), whole(square), head_turned, row, row],
-        out_shape=[jax.ShapeDtypeStruct(square, F32)] * 2
-        + [turned_shape, row_shape, row_shape],
+        grid=(2,),
+        in_specs=[smem, by_half, by_half, whole((2, half, tokens))],
+        out_specs=[
+            whole(sums),
+            whole(sums),
+            pl.BlockSpec((half, HD, tokens), lambda s: (s, 0, 0)),
+            half_row,
+            half_row,
+        ],
+        out_shape=[jax.ShapeDtypeStruct(sums, F32)] * 2 + [turned_shape, row_shape, row_shape],
         compiler_params=params(),
-        cost_estimate=cost(3),
+        cost_estimate=cost(5),
         name="totals",
-    )(core_arg, keys, gates.T)
-
-    moment_total = pl.pallas_call(
-        moment_kernel,
-        grid=(heads,),
-        in_specs=[head_turned, row, by_head],
-        out_specs=pl.BlockSpec((1, HD, HD), lambda h: (h, 0, 0)),
-        out_shape=jax.ShapeDtypeStruct((heads, HD, HD), BF16),
-        compiler_params=params(),
-        cost_estimate=cost(3),
-        name="moments",
-    )(keys_turned, gated, values)
+    )(core_arg, keys, values, gates.T.reshape(2, half, tokens))
 
     def before_of(parts, at):
         return sum(jnp.where(at >= shift, part.astype(F32), 0.0) for shift, part in enumerate(parts, 1))
 
-    def total_of(own, parts):
-        return (own.astype(F32) + sum(part.astype(F32) for part in parts)).astype(own.dtype)
-
     received = send(theirs, perm_core())
-    other = send(moment_total, perm_core())
     chip = (mine + received).astype(F16)
-    chip, keys_turned_later = lax.optimization_barrier((chip, keys_turned))
+    chip, keys_turned_later, weight = lax.optimization_barrier((chip, keys_turned, out_weight))
     along = [send(chip, perm_x(shift)) for shift in range(1, side)]
+    parts = [rows_from(shift, weight) for shift in range(1, groups - 1)]
     local_gram, local_moment, values_turned = pl.pallas_call(
         functools.partial(local_kernel, blocks),
         grid=(heads,),
@@ -314,11 +317,9 @@
         name="local",
     )(keys_turned_later, scale, gated, keys, values)
 
-    row_total = total_of(chip, along)
-    moment_chip = (moment_total.astype(F32) + other.astype(F32)).astype(BF16)
-    row_total, moment_chip, queries_later = lax.optimization_barrier((row_total, moment_chip, queries))
+    row_total = (chip.astype(F32) + sum(part.astype(F32) for part in along)).astype(F16)
+    row_total, queries_later = lax.optimization_barrier((row_total, queries))
     above = [send(row_total, perm_y(shift)) for shift in range(1, side)]
-    moment_along = [send(moment_chip, perm_x(shift)) for shift in range(1, side)]
     queries_turned, gram_mask, moment_mask = pl.pallas_call(
         functools.partial(masks_kernel, blocks),
         grid=(heads,),
@@ -330,14 +331,12 @@
         name="masks",
     )(queries_later, scale, gated)
 
+    above, weight = lax.optimization_barrier((above, weight))
+    parts.append(rows_from(groups - 1, weight))
     before = before_of(along, x_at) + before_of(above, y_at)
     keep = before + jnp.where(core == 1, received, 0.0)
     give = before + jnp.where(core == 0, mine, 0.0)
     got = send(give, perm_core())
-    moment_row = total_of(moment_chip, moment_along)
-    keep, got, moment_row, parts = lax.optimization_barrier((keep, got, moment_row, parts))
-    moment_above = [send(moment_row, perm_y(shift)) for shift in range(1, side)]
-    moment_before = before_of(moment_along, x_at) + jnp.where(core == 1, other, jnp.zeros_like(other)).astype(F32)
 
     step_blocks = 4
     step = step_blocks * SPAN
@@ -356,8 +355,8 @@
             some_blocks,
             some_blocks,
             some_blocks,
-            whole(square),
-            whole(square),
+            whole(sums),
+            whole(sums),
         ],
         out_specs=[tall] * 3,
         out_shape=[turned_shape] * 3,
@@ -374,7 +373,6 @@
         name="solve",
     )(core_arg, ridge, queries_turned, keys, keys_turned, gram_mask, moment_mask, local_gram, keep, got)
 
-    moment_prior = moment_before + before_of(moment_above, y_at)
     out_blocks = 2
     step = out_blocks * SPAN
     tall = pl.BlockSpec((heads, HD, step), lambda b, g: (0, 0, b))
@@ -389,18 +387,19 @@
                 tall,
                 tall,
                 pl.BlockSpec((heads, out_blocks, HD, HD), lambda b, g: (0, b, 0, 0)),
-                whole((heads, HD, HD)),
+                whole(sums),
+                whole(sums),
                 pl.BlockSpec((width, columns), lambda b, g: (g[0], 0)),
             ]
             + [whole((width, columns))] * (groups - 1),
             out_specs=pl.BlockSpec((1, step, columns * groups), lambda b, g: (0, b, 0)),
-            scratch_shapes=[pltpu.VMEM((step, width), BF16)],
+            scratch_shapes=[pltpu.VMEM((step, width), BF16), pltpu.VMEM((heads, HD, HD), F32)],
         ),
         out_shape=jax.ShapeDtypeStruct((1, tokens, columns * groups), BF16),
         compiler_params=params(),
         cost_estimate=cost(7),
         name="project",
-    )(group_arg, values_turned, high, low, corr, local_moment, moment_prior, out_weight, *parts)
+    )(place_arg, values_turned, high, low, corr, local_moment, keep, got, out_weight, *parts)
     return out
 
 

time: 90.9 us -> 76.7 us (0.84)
  the two profiles are of different devices: /device:TPU:40 before, /device:TPU:1 now
where the time goes in v2:
time: 76.7 us; the launch traced here: 76.3 us
  Pallas kernels  49.4 us (64%)
  starting transfers between devices  20 us (26%)
  local copies, waits for them, and re-layouts  3.34 us (4%)
  other arithmetic  2.65 us (3%)
    pallas_call x1, Pallas kernels, shards(): pl.pallas_call(functools.partial(solve_kernel, heads, step_blocks), grid=...  26.1 us
    ppermute x8, starting transfers between devices, send(): return lax.ppermute(array, 'seq', perm)  14.2 us
    pallas_call x1, Pallas kernels, shards(): pl.pallas_call(functools.partial(project_kernel, heads, out_blocks, group...  9.15 us
    ppermute x3, starting transfers between devices, rows_from(): lax.ppermute(piece, 'head', [(i, (i + shift) % groups) for i in range(gro...  5.8 us
    pallas_call x1, Pallas kernels, shards(): pl.pallas_call(functools.partial(local_kernel, blocks), grid=(heads,), in...  5.36 us
    pallas_call x1, Pallas kernels, shards(): pl.pallas_call(functools.partial(masks_kernel, blocks), grid=(heads,), in...  4.68 us
    pallas_call x1, Pallas kernels, shards(): pl.pallas_call(functools.partial(totals_kernel, half), grid=(2,), in_spec...  4.18 us
    unnamed x12, local copies, waits for them, and re-layouts  1.9 us
  transfers between devices with their start and end apart: 11, of which 1 were waited for; matrix products, arithmetic and copies ran while one was open for 2% of the time, Pallas kernels for 47%

profile of v2, /device:TPU:1, one launch (start us, length us, event | category | flops | bytes accessed | tf_op | source)
XLA Modules:
  0.0 76.3 jit_solution(13501572692081937957)
XLA Ops:
  0.0 1.3 %reshape.4.gates_ref = f32[2,2,1024]{2,1,0:T(2,128)} reshape(f32[4,1024]{1,0:T(4,128)} %bitcast.3) | data formatting | bytes 32768 | tf_op jit(solution)/shard_map/reshape | solution.py:299
  1.3 0.0 copy-start
  1.3 4.2 %totals.1 = (f32[4,128,128]{2,1,0:T(8,128)}, f32[4,128,128]{2,1,0:T(8,128)}, bf16[4,128,1024]{2,1,0:T(8,128)(2,1)}, f32[4,1,1024]{2,1,0:T(1,128)}, f32[4,1,1024]{2,1,0:T(1,128)}) custom-call(s32[1]{0:T(128)} %bitcast.1.core_ref, bf16[1024,512]{1,0:T(8,128)(2,1)} %keys_ref.5, bf16[1024,512]{1,0:T(8,128)(2,1)} %values_ref.3, f32[2,2,1024]{2,1,0:T(2,128)} %reshape.4.gates_ref), custom_call_target="tpu_custom_call" | custom-call | flops 5500000256 | bytes 5000000 | tf_op jit(solution)/shard_map/totals/pallas_call | solution.py:284
  5.5 1.4 %collective-permute-start = (f32[4,128,128]{2,1,0:T(8,128)}, f32[4,128,128]{2,1,0:T(8,128)S(1)}, u32[]{:S(2)}, u32[]{:S(2)}) collective-permute-start(f32[4,128,128]{2,1,0:T(8,128)} %get-tuple-element.29), channel_id=1, source_target_pairs={{0,4},{4,0},{8,12},{12,8},{16,20},{20,16},{24,28},{28,24},{32,36},... | collective-permute-start | bytes 786440 | tf_op jit(solution)/shard_map/ppermute | solution.py:268
  7.0 0.7 pad_add_fusion.place_ref
  7.6 0.7 collective-permute-done
  8.3 1.0 %add_convert_fusion = f16[4,128,128]{2,1,0:T(8,128)(2,1)S(1)} fusion(f32[4,128,128]{2,1,0:T(8,128)} %get-tuple-element.28, f32[4,128,128]{2,1,0:T(8,128)S(1)} %collective-permute-done), kind=kLoop, calls=%fused_computation.12 | loop fusion | flops 131072 | bytes 655360 | tf_op jit(solution)/shard_map/convert_element_type | solution.py:305
  9.3 1.4 %collective-permute-start.1 = (f16[4,128,128]{2,1,0:T(8,128)(2,1)S(1)}, f16[4,128,128]{2,1,0:T(8,128)(2,1)S(1)}, u32[]{:S(2)}, u32[]{:S(2)}) collective-permute-start(f16[4,128,128]{2,1,0:T(8,128)(2,1)S(1)} %add_convert_fusion), channel_id=1, source_target_pairs={{0,8},{4,12},{8,16},{12,20},{16,24},{20,28},{24,0},{28,4},{32,40},... | collective-permute-start | bytes 393224 | tf_op jit(solution)/shard_map/ppermute | solution.py:268
  10.7 2.5 %collective-permute-start.2 = (f16[4,128,128]{2,1,0:T(8,128)(2,1)S(1)}, f16[4,128,128]{2,1,0:T(8,128)(2,1)S(1)}, u32[]{:S(2)}, u32[]{:S(2)}) collective-permute-start(f16[4,128,128]{2,1,0:T(8,128)(2,1)S(1)} %add_convert_fusion), channel_id=1, source_target_pairs={{0,16},{4,20},{8,24},{12,28},{16,0},{20,4},{24,8},{28,12},{32,48},... | collective-permute-start | bytes 393224 | tf_op jit(solution)/shard_map/ppermute | solution.py:268
  13.1 1.2 %collective-permute-start.3 = (f16[4,128,128]{2,1,0:T(8,128)(2,1)S(1)}, f16[4,128,128]{2,1,0:T(8,128)(2,1)S(1)}, u32[]{:S(2)}, u32[]{:S(2)}) collective-permute-start(f16[4,128,128]{2,1,0:T(8,128)(2,1)S(1)} %add_convert_fusion), channel_id=1, source_target_pairs={{0,24},{4,28},{8,0},{12,4},{16,8},{20,12},{24,16},{28,20},{32,56},... | collective-permute-start | bytes 393224 | tf_op jit(solution)/shard_map/ppermute | solution.py:268
  14.3 0.0 copy-done
  14.3 0.1 constant_dynamic-slice_fusion.1
  14.4 1.7 %collective-permute-start.8 = (bf16[512,512]{1,0:T(8,128)(2,1)S(1)}, bf16[512,512]{1,0:T(8,128)(2,1)S(1)}, u32[]{:S(2)}, u32[]{:S(2)}) collective-permute-start(bf16[512,512]{1,0:T(8,128)(2,1)S(1)} %get-tuple-element.54), channel_id=1, source_target_pairs={{0,1},{1,2},{2,3},{3,0},{4,5},{5,6},{6,7},{7,4},{8,9},{9,10},{10,1... | collective-permute-start | bytes 1572872 | tf_op jit(solution)/shard_map/ppermute | solution.py:272
  16.1 3.3 %collective-permute-start.9 = (bf16[512,512]{1,0:T(8,128)(2,1)S(1)}, bf16[512,512]{1,0:T(8,128)(2,1)S(1)}, u32[]{:S(2)}, u32[]{:S(2)}) collective-permute-start(bf16[512,512]{1,0:T(8,128)(2,1)S(1)} %get-tuple-element.53), channel_id=1, source_target_pairs={{0,2},{1,3},{2,0},{3,1},{4,6},{5,7},{6,4},{7,5},{8,10},{9,11},{10,... | collective-permute-start | bytes 1572872 | tf_op jit(solution)/shard_map/ppermute | solution.py:272
  19.4 5.4 %local.1 = (f32[4,8,128,128]{3,2,1,0:T(8,128)}, f32[4,8,128,128]{3,2,1,0:T(8,128)}, bf16[4,128,1024]{2,1,0:T(8,128)(2,1)}) custom-call(bf16[4,128,1024]{2,1,0:T(8,128)(2,1)} %get-tuple-element.31.turned_ref, f32[4,1,1024]{2,1,0:T(1,128)} %get-tuple-element.32.scale_ref, f32[4,1,1024]{2,1,0:T(1,128)} %get-tuple-element.33.gated_ref, ...), custom_call_target="tpu_custom_call" | custom-call | flops 5500000256 | bytes 5000000 | tf_op jit(solution)/shard_map/local/pallas_call | solution.py:309
  24.7 0.0 collective-permute-done.1
  24.7 0.0 collective-permute-done.2
  24.7 0.0 collective-permute-done.3
  24.8 0.1 fusion.4
  24.8 0.0 copy-start.1
  24.9 1.4 %collective-permute-start.4 = (f16[4,128,128]{2,1,0:T(8,128)(2,1)S(1)}, f16[4,128,128]{2,1,0:T(8,128)(2,1)S(1)}, u32[]{:S(2)}, u32[]{:S(2)}) collective-permute-start(f16[4,128,128]{2,1,0:T(8,128)(2,1)S(1)} %fusion.4), channel_id=1, source_target_pairs={{0,32},{4,36},{8,40},{12,44},{16,48},{20,52},{24,56},{28,60},{32,6... | collective-permute-start | bytes 393224 | tf_op jit(solution)/shard_map/ppermute | solution.py:268
  26.2 2.6 %collective-permute-start.5 = (f16[4,128,128]{2,1,0:T(8,128)(2,1)S(1)}, f16[4,128,128]{2,1,0:T(8,128)(2,1)S(1)}, u32[]{:S(2)}, u32[]{:S(2)}) collective-permute-start(f16[4,128,128]{2,1,0:T(8,128)(2,1)S(1)} %fusion.4), channel_id=1, source_target_pairs={{0,64},{4,68},{8,72},{12,76},{16,80},{20,84},{24,88},{28,92},{32,9... | collective-permute-start | bytes 393224 | tf_op jit(solution)/shard_map/ppermute | solution.py:268
  28.8 1.1 %collective-permute-start.6 = (f16[4,128,128]{2,1,0:T(8,128)(2,1)S(1)}, f16[4,128,128]{2,1,0:T(8,128)(2,1)S(1)}, u32[]{:S(2)}, u32[]{:S(2)}) collective-permute-start(f16[4,128,128]{2,1,0:T(8,128)(2,1)S(1)} %fusion.4), channel_id=1, source_target_pairs={{0,96},{4,100},{8,104},{12,108},{16,112},{20,116},{24,120},{28,124... | collective-permute-start | bytes 393224 | tf_op jit(solution)/shard_map/ppermute | solution.py:268
  29.9 4.7 %masks.1 = (bf16[4,128,1024]{2,1,0:T(8,128)(2,1)}, f32[4,8,128,128]{3,2,1,0:T(8,128)}, f32[4,8,128,128]{3,2,1,0:T(8,128)}) custom-call(bf16[1024,512]{1,0:T(8,128)(2,1)} %queries_ref, f32[4,1,1024]{2,1,0:T(1,128)} %get-tuple-element.32.scale_ref, f32[4,1,1024]{2,1,0:T(1,128)} %get-tuple-element.33.gated_ref), custom_call_target="tpu_custom_call" | custom-call | flops 4400000000 | bytes 4000000 | tf_op jit(solution)/shard_map/masks/pallas_call | solution.py:323
  34.6 0.0 collective-permute-done.4
  34.6 0.0 collective-permute-done.5
  34.6 0.0 collective-permute-done.6
  34.6 0.0 copy-done.1
  34.6 0.2 select_add_fusion
  34.8 2.7 %collective-permute-start.7 = (f32[4,128,128]{2,1,0:T(8,128)S(1)}, f32[4,128,128]{2,1,0:T(8,128)S(1)}, u32[]{:S(2)}, u32[]{:S(2)}) collective-permute-start(f32[4,128,128]{2,1,0:T(8,128)S(1)} %get-tuple-element.51), channel_id=1, source_target_pairs={{0,4},{4,0},{8,12},{12,8},{16,20},{20,16},{24,28},{28,24},{32,36},... | collective-permute-start | bytes 786440 | tf_op jit(solution)/shard_map/ppermute | solution.py:268
  37.5 0.8 %collective-permute-start.10 = (bf16[512,512]{1,0:T(8,128)(2,1)S(1)}, bf16[512,512]{1,0:T(8,128)(2,1)S(1)}, u32[]{:S(2)}, u32[]{:S(2)}) collective-permute-start(bf16[512,512]{1,0:T(8,128)(2,1)S(1)} %constant_dynamic-slice_fusion), channel_id=1, source_target_pairs={{0,3},{1,0},{2,1},{3,2},{4,7},{5,4},{6,5},{7,6},{8,11},{9,8},{10,9... | collective-permute-start | bytes 1572872 | tf_op jit(solution)/shard_map/ppermute | solution.py:272
  38.3 0.8 select_add_fusion.1.keep_ref
  39.1 0.0 collective-permute-done.7.got_ref
  39.1 0.0 copy-start.5
  39.1 0.7 copy-done.5
  39.8 26.1 %solve.1 = (bf16[4,128,1024]{2,1,0:T(8,128)(2,1)}, bf16[4,128,1024]{2,1,0:T(8,128)(2,1)}, bf16[4,128,1024]{2,1,0:T(8,128)(2,1)}) custom-call(s32[1]{0:T(128)} %bitcast.1.core_ref, f32[4]{0:T(128)} %ridge_ref.1, bf16[4,128,1024]{2,1,0:T(8,128)(2,1)} %get-tuple-element.37.queries_ref, bf16[1024,512]{1,0:T(8,128)(2,1)} %keys_ref.5, ...), custom_call_target="tpu_custom_call" | custom-call | flops 32999999488 | bytes 30000000 | tf_op jit(solution)/shard_map/solve/pallas_call | solution.py:346
  65.9 0.0 collective-permute-done.8.rest_0_
  65.9 0.0 copy-start.2
  65.9 0.0 collective-permute-done.9.rest_1_
  65.9 0.0 copy-start.3
  65.9 0.0 collective-permute-done.10.rest_2_
  65.9 0.0 copy-start.4
  65.9 0.7 copy-done.2
  66.7 0.3 copy-done.3
  66.9 0.2 copy-done.4
  67.1 9.2 %project.1 = bf16[1,1024,2048]{2,1,0:T(8,128)(2,1)} custom-call(s32[2]{0:T(128)} %pad_add_fusion.place_ref, bf16[4,128,1024]{2,1,0:T(8,128)(2,1)} %get-tuple-element.34.values_ref, bf16[4,128,1024]{2,1,0:T(8,128)(2,1)} %get-tuple-element.46.high_ref, bf16[4,128,1024]{2,1,0:T(8,128)(2,1)} %get-tuple-element.47.low_ref, ...), custom_call_target="tpu_custom_call" | custom-call | flops 7699999744 | bytes 7000000 | tf_op jit(solution)/shard_map/project/pallas_call | solution.py:379
  (1 shorter events, 0.0 us)
Async XLA Ops:
  1.3 13.0 %copy-start = (bf16[2048,512]{1,0:T(8,128)(2,1)S(1)}, bf16[2048,512]{1,0:T(8,128)(2,1)}, u32[]{:S(2)}) copy-start(bf16[2048,512]{1,0:T(8,128)(2,1)} %own_ref.1) | copy-start | bytes 6291460
  5.5 2.8 %collective-permute-start = (f32[4,128,128]{2,1,0:T(8,128)}, f32[4,128,128]{2,1,0:T(8,128)S(1)}, u32[]{:S(2)}, u32[]{:S(2)}) collective-permute-start(f32[4,128,128]{2,1,0:T(8,128)} %get-tuple-element.29), channel_id=1, source_target_pairs={{0,4},{4,0},{8,12},{12,8},{16,20},{20,16},{24,28},{28,24},{32,36},... | collective-permute-start | bytes 786440 | tf_op jit(solution)/shard_map/ppermute | solution.py:268
  9.3 15.4 %collective-permute-start.1 = (f16[4,128,128]{2,1,0:T(8,128)(2,1)S(1)}, f16[4,128,128]{2,1,0:T(8,128)(2,1)S(1)}, u32[]{:S(2)}, u32[]{:S(2)}) collective-permute-start(f16[4,128,128]{2,1,0:T(8,128)(2,1)S(1)} %add_convert_fusion), channel_id=1, source_target_pairs={{0,8},{4,12},{8,16},{12,20},{16,24},{20,28},{24,0},{28,4},{32,40},... | collective-permute-start | bytes 393224 | tf_op jit(solution)/shard_map/ppermute | solution.py:268
  10.7 14.1 %collective-permute-start.2 = (f16[4,128,128]{2,1,0:T(8,128)(2,1)S(1)}, f16[4,128,128]{2,1,0:T(8,128)(2,1)S(1)}, u32[]{:S(2)}, u32[]{:S(2)}) collective-permute-start(f16[4,128,128]{2,1,0:T(8,128)(2,1)S(1)} %add_convert_fusion), channel_id=1, source_target_pairs={{0,16},{4,20},{8,24},{12,28},{16,0},{20,4},{24,8},{28,12},{32,48},... | collective-permute-start | bytes 393224 | tf_op jit(solution)/shard_map/ppermute | solution.py:268
  13.1 11.6 %collective-permute-start.3 = (f16[4,128,128]{2,1,0:T(8,128)(2,1)S(1)}, f16[4,128,128]{2,1,0:T(8,128)(2,1)S(1)}, u32[]{:S(2)}, u32[]{:S(2)}) collective-permute-start(f16[4,128,128]{2,1,0:T(8,128)(2,1)S(1)} %add_convert_fusion), channel_id=1, source_target_pairs={{0,24},{4,28},{8,0},{12,4},{16,8},{20,12},{24,16},{28,20},{32,56},... | collective-permute-start | bytes 393224 | tf_op jit(solution)/shard_map/ppermute | solution.py:268
  14.4 51.5 %collective-permute-start.8 = (bf16[512,512]{1,0:T(8,128)(2,1)S(1)}, bf16[512,512]{1,0:T(8,128)(2,1)S(1)}, u32[]{:S(2)}, u32[]{:S(2)}) collective-permute-start(bf16[512,512]{1,0:T(8,128)(2,1)S(1)} %get-tuple-element.54), channel_id=1, source_target_pairs={{0,1},{1,2},{2,3},{3,0},{4,5},{5,6},{6,7},{7,4},{8,9},{9,10},{10,1... | collective-permute-start | bytes 1572872 | tf_op jit(solution)/shard_map/ppermute | solution.py:272
  16.1 49.8 %collective-permute-start.9 = (bf16[512,512]{1,0:T(8,128)(2,1)S(1)}, bf16[512,512]{1,0:T(8,128)(2,1)S(1)}, u32[]{:S(2)}, u32[]{:S(2)}) collective-permute-start(bf16[512,512]{1,0:T(8,128)(2,1)S(1)} %get-tuple-element.53), channel_id=1, source_target_pairs={{0,2},{1,3},{2,0},{3,1},{4,6},{5,7},{6,4},{7,5},{8,10},{9,11},{10,... | collective-permute-start | bytes 1572872 | tf_op jit(solution)/shard_map/ppermute | solution.py:272
  24.8 9.8 %copy-start.1 = (f32[4,128,128]{2,1,0:T(8,128)S(1)}, f32[4,128,128]{2,1,0:T(8,128)}, u32[]{:S(2)}) copy-start(f32[4,128,128]{2,1,0:T(8,128)} %get-tuple-element.28) | copy-start | bytes 786436
  24.9 9.7 %collective-permute-start.4 = (f16[4,128,128]{2,1,0:T(8,128)(2,1)S(1)}, f16[4,128,128]{2,1,0:T(8,128)(2,1)S(1)}, u32[]{:S(2)}, u32[]{:S(2)}) collective-permute-start(f16[4,128,128]{2,1,0:T(8,128)(2,1)S(1)} %fusion.4), channel_id=1, source_target_pairs={{0,32},{4,36},{8,40},{12,44},{16,48},{20,52},{24,56},{28,60},{32,6... | collective-permute-start | bytes 393224 | tf_op jit(solution)/shard_map/ppermute | solution.py:268
  26.2 8.4 %collective-permute-start.5 = (f16[4,128,128]{2,1,0:T(8,128)(2,1)S(1)}, f16[4,128,128]{2,1,0:T(8,128)(2,1)S(1)}, u32[]{:S(2)}, u32[]{:S(2)}) collective-permute-start(f16[4,128,128]{2,1,0:T(8,128)(2,1)S(1)} %fusion.4), channel_id=1, source_target_pairs={{0,64},{4,68},{8,72},{12,76},{16,80},{20,84},{24,88},{28,92},{32,9... | collective-permute-start | bytes 393224 | tf_op jit(solution)/shard_map/ppermute | solution.py:268
  28.8 5.8 %collective-permute-start.6 = (f16[4,128,128]{2,1,0:T(8,128)(2,1)S(1)}, f16[4,128,128]{2,1,0:T(8,128)(2,1)S(1)}, u32[]{:S(2)}, u32[]{:S(2)}) collective-permute-start(f16[4,128,128]{2,1,0:T(8,128)(2,1)S(1)} %fusion.4), channel_id=1, source_target_pairs={{0,96},{4,100},{8,104},{12,108},{16,112},{20,116},{24,120},{28,124... | collective-permute-start | bytes 393224 | tf_op jit(solution)/shard_map/ppermute | solution.py:268
  34.8 4.3 %collective-permute-start.7 = (f32[4,128,128]{2,1,0:T(8,128)S(1)}, f32[4,128,128]{2,1,0:T(8,128)S(1)}, u32[]{:S(2)}, u32[]{:S(2)}) collective-permute-start(f32[4,128,128]{2,1,0:T(8,128)S(1)} %get-tuple-element.51), channel_id=1, source_target_pairs={{0,4},{4,0},{8,12},{12,8},{16,20},{20,16},{24,28},{28,24},{32,36},... | collective-permute-start | bytes 786440 | tf_op jit(solution)/shard_map/ppermute | solution.py:268
  37.5 28.4 %collective-permute-start.10 = (bf16[512,512]{1,0:T(8,128)(2,1)S(1)}, bf16[512,512]{1,0:T(8,128)(2,1)S(1)}, u32[]{:S(2)}, u32[]{:S(2)}) collective-permute-start(bf16[512,512]{1,0:T(8,128)(2,1)S(1)} %constant_dynamic-slice_fusion), channel_id=1, source_target_pairs={{0,3},{1,0},{2,1},{3,2},{4,7},{5,4},{6,5},{7,6},{8,11},{9,8},{10,9... | collective-permute-start | bytes 1572872 | tf_op jit(solution)/shard_map/ppermute | solution.py:272
  39.1 0.7 copy-start.5
  65.9 0.8 %copy-start.2 = (bf16[512,512]{1,0:T(8,128)(2,1)}, bf16[512,512]{1,0:T(8,128)(2,1)S(1)}, u32[]{:S(2)}) copy-start(bf16[512,512]{1,0:T(8,128)(2,1)S(1)} %collective-permute-done.8.rest_0_) | copy-start | bytes 1572868
  65.9 1.0 %copy-start.3 = (bf16[512,512]{1,0:T(8,128)(2,1)}, bf16[512,512]{1,0:T(8,128)(2,1)S(1)}, u32[]{:S(2)}) copy-start(bf16[512,512]{1,0:T(8,128)(2,1)S(1)} %collective-permute-done.9.rest_1_) | copy-start | bytes 1572868
  65.9 1.2 %copy-start.4 = (bf16[512,512]{1,0:T(8,128)(2,1)}, bf16[512,512]{1,0:T(8,128)(2,1)S(1)}, u32[]{:S(2)}) copy-start(bf16[512,512]{1,0:T(8,128)(2,1)S(1)} %collective-permute-done.10.rest_2_) | copy-start | bytes 1572868

commit v3 on v2

v3 whole, which is shorter than its diff:
```python
import functools
import jax
import jax.numpy as jnp
from jax import lax
from jax.experimental import pallas as pl
from jax.experimental.pallas import tpu as pltpu
from jax.sharding import PartitionSpec as P

HD = 128
SPAN = 128
ITERS = 8
EPS = 1e-06
F32 = jnp.float32
BF16 = jnp.bfloat16
F16 = jnp.float16
SHRINK = 16.0


def two_terms(value):
    high = value.astype(BF16)
    return high, (value - high.astype(F32)).astype(BF16)


def dot(left, right):
    return jnp.dot(left, right, preferred_element_type=F32)


def head_cols(head):
    return slice(head * HD, (head + 1) * HD)


def totals_kernel(
    half, core_ref, keys_ref, values_ref, gates_ref, mine_ref, theirs_ref, turned_ref, scale_ref, gated_ref
):
    step = pl.program_id(0)
    lefts = []
    for head in range(half):
        turned = keys_ref[:, head_cols(head)].T
        turned_ref[head] = turned
        wide = turned.astype(F32)
        norm = jnp.sum(wide * wide, axis=0, keepdims=True) + EPS
        gate = gates_ref[pl.ds(step * half + head, 1), :]
        scale = gate / norm
        gated = gate * lax.rsqrt(norm)
        scale_ref[head] = scale
        gated_ref[head] = gated
        for factor in (scale, gated * (1.0 / SHRINK)):
            lefts.append(jnp.concatenate(two_terms(wide * factor), axis=0))
    grams = [dot(lefts[2 * head], keys_ref[:, head_cols(head)]) for head in range(half)]
    moments = [dot(lefts[2 * head + 1], values_ref[:, head_cols(head)]) for head in range(half)]
    sums = [product[:HD] + product[HD:] for product in grams + moments]
    own = core_ref[0] == step

    @pl.when(own)
    def _():
        for at, value in enumerate(sums):
            mine_ref[at] = value

    @pl.when(jnp.logical_not(own))
    def _():
        for at, value in enumerate(sums):
            theirs_ref[at] = value


def local_kernel(blocks, turned_ref, scale_ref, gated_ref, keys_ref, values_ref, gram_ref, moment_ref, values_turned_ref):
    values_turned_ref[0] = values_ref[...].T
    gram_ref[0, 0] = jnp.zeros((HD, HD), F32)
    moment_ref[0, 0] = jnp.zeros((HD, HD), F32)
    grams, moments = [], []
    for block in range(blocks - 1):
        span = slice(block * SPAN, (block + 1) * SPAN)
        keys = turned_ref[0, :, span].astype(F32)
        left = jnp.concatenate(two_terms(keys * scale_ref[0, :, span]), axis=0)
        grams.append(dot(left, keys_ref[span, :]))
        left = jnp.concatenate(two_terms(keys * gated_ref[0, :, span]), axis=0)
        moments.append(dot(left, values_ref[span, :]))
    for block in range(blocks - 1):
        gram, moment = grams[block], moments[block]
        gram_ref[0, block + 1] = gram_ref[0, block] + (gram[:HD] + gram[HD:])
        moment_ref[0, block + 1] = moment_ref[0, block] + (moment[:HD] + moment[HD:]).T


def columns_kernel(blocks, queries_ref, scale_ref, gated_ref, turned_ref, scale_out_ref, gated_out_ref):
    turned_ref[0] = queries_ref[...].T
    for out_ref, factors in ((scale_out_ref, scale_ref), (gated_out_ref, gated_ref)):
        spans = [factors[0, :, block * SPAN : (block + 1) * SPAN] for block in range(blocks)]
        spans += [jnp.zeros((1, SPAN), F32)] * (SPAN - blocks)
        out_ref[0] = jnp.concatenate(spans, axis=0).T


def solve_kernel(
    heads,
    blocks,
    steps,
    core_ref,
    ridge_ref,
    queries_ref,
    keys_ref,
    turned_ref,
    scale_ref,
    gated_ref,
    local_ref,
    values_ref,
    local_moment_ref,
    keep_ref,
    got_ref,
    readout_ref,
    first,
    second,
    masks,
    xs,
    rs,
    ds,
    norms,
):
    core = core_ref[0]
    half = heads // 2
    row = lax.broadcasted_iota(jnp.int32, (SPAN, SPAN), 0)
    column = lax.broadcasted_iota(jnp.int32, (SPAN, SPAN), 1)
    causal = row <= column
    units = [(head, block) for block in range(blocks) for head in range(heads)]
    count = len(units)
    step = pl.program_id(0)

    def column_of(ref, head, block):
        options = [ref[head, :, at * blocks + block : at * blocks + block + 1] for at in range(steps)]
        value = options[0]
        for at in range(1, steps):
            value = jnp.where(step == at, options[at], value)
        return value

    for head in range(heads):
        prior = jnp.where(core == head // half, keep_ref[head % half], got_ref[head % half])
        prior = prior + jnp.where(row == column, ridge_ref[head], 0.0)
        for block in range(blocks):
            unit = block * heads + head
            rows = slice(block * SPAN, (block + 1) * SPAN)
            own = keys_ref[rows, head_cols(head)]
            masks[unit] = jnp.where(causal, column_of(scale_ref, head, block), 0.0)
            high, low = two_terms(prior + local_ref[head, block])
            first[unit, :HD, :HD] = high
            first[unit, :HD, HD:] = high
            first[unit, HD:, :HD] = own
            first[unit, HD:, HD:] = own
            second[unit, :, :HD] = low
            second[unit, :, HD:] = turned_ref[head, :, rows]
            query = queries_ref[head, :, rows].astype(F32)
            query = query * lax.rsqrt(jnp.sum(query * query, axis=0, keepdims=True) + EPS)
            xs[unit] = jnp.zeros((HD, SPAN), F32)
            rs[unit] = query
            ds[unit] = query
            norms[unit] = jnp.sum(query * query, axis=0, keepdims=True)

    def product_of(unit):
        high, low = two_terms(ds[unit])
        return high, dot(first[unit], jnp.concatenate([high, low], axis=0))

    def image_of(unit, high, product):
        corr = (product[HD:] * masks[unit]).astype(BF16)
        return product[:HD] + dot(second[unit], jnp.concatenate([high, corr], axis=0))

    def update(unit, image):
        direction = ds[unit]
        now = norms[unit]
        step = now / (jnp.sum(direction * image, axis=0, keepdims=True) + EPS)
        xs[unit] += step * direction
        residual = rs[unit] - step * image
        rs[unit] = residual
        after = jnp.sum(residual * residual, axis=0, keepdims=True)
        ds[unit] = residual + (after / (now + EPS)) * direction
        norms[unit] = after

    lag = 4

    def sweep_once(sweep, carry):
        products, images = {}, {}
        for at in range(count + 2 * lag):
            if at < count:
                products[at] = product_of(at)
            if 0 <= at - lag < count:
                images[at - lag] = image_of(at - lag, *products.pop(at - lag))
            if 0 <= at - 2 * lag < count:
                update(at - 2 * lag, images.pop(at - 2 * lag))
        return carry

    lax.fori_loop(0, ITERS, sweep_once, 0)

    priors = []
    for head in range(heads):
        at = half + head % half
        priors.append(jnp.where(core == head // half, keep_ref[at], got_ref[at]).T * SHRINK)

    def correlations_of(unit):
        high, low = two_terms(xs[unit])
        return high, low, dot(first[unit, HD:], jnp.concatenate([high, low], axis=0))

    def readout_of(unit, high, low, product):
        head, block = units[unit]
        corr = jnp.where(causal, product * column_of(gated_ref, head, block), 0.0).astype(BF16)
        moment_high, moment_low = two_terms(priors[head] + local_moment_ref[head, block])
        values = values_ref[head, :, block * SPAN : (block + 1) * SPAN]
        left = jnp.concatenate([moment_high, moment_high, moment_low, values], axis=1)
        return dot(left, jnp.concatenate([high, low, high, corr], axis=0))

    products, readouts = {}, {}
    for at in range(count + 2 * lag):
        if at < count:
            products[at] = correlations_of(at)
        if 0 <= at - lag < count:
            readouts[at - lag] = readout_of(at - lag, *products.pop(at - lag))
        if 0 <= at - 2 * lag < count:
            head, block = units[at - 2 * lag]
            rows = slice(block * SPAN, (block + 1) * SPAN)
            readout_ref[rows, head_cols(head)] = readouts.pop(at - 2 * lag).T.astype(BF16)


def project_kernel(groups, group_ref, readout_ref, own_ref, *rest):
    others, out_ref = rest[: groups - 1], rest[groups - 1]
    group = group_ref[0]
    width = own_ref.shape[1]
    for shift, part in enumerate((own_ref,) + tuple(others)):
        source = lax.rem(group + groups - shift, groups)
        columns = pl.ds(pl.multiple_of(source * width, width), width)
        out_ref[0, :, columns] = dot(readout_ref[...], part[...]).astype(BF16)


def params(mebibytes):
    return pltpu.CompilerParams(vmem_limit_bytes=mebibytes << 20)


def cost(us):
    return pl.CostEstimate(flops=int(us * 1.1e9), bytes_accessed=int(us * 1e6), transcendentals=0)


def whole(shape):
    return pl.BlockSpec(shape, lambda *a: (0,) * len(shape))


def shards(mesh, queries, keys, values, gates, ridge, out_weight):
    tokens, width = queries.shape
    heads = width // HD
    half = heads // 2
    blocks = tokens // SPAN
    seq, groups = mesh.shape["seq"], mesh.shape["head"]
    columns = out_weight.shape[1]
    side = 4
    place = lax.axis_index("seq")
    core = lax.rem(place, 2)
    x_at = lax.rem(place // 2, side)
    y_at = place // (2 * side)
    group = lax.axis_index("head")
    core_arg = core.reshape(1).astype(jnp.int32)
    group_arg = group.reshape(1).astype(jnp.int32)
    smem = pl.BlockSpec(memory_space=pltpu.SMEM)

    def perm_core():
        return [(p, p ^ 1) for p in range(seq)]

    def perm_x(shift):
        return [(p, (p // 8) * 8 + ((p // 2 + shift) % side) * 2 + p % 2) for p in range(seq)]

    def perm_y(shift):
        return [(p, (p + 8 * shift) % seq) for p in range(seq)]

    def send(array, perm):
        return lax.ppermute(array, "seq", perm)

    def rows_from(shift, weight):
        piece = lax.dynamic_slice_in_dim(weight, lax.rem(group + shift, groups) * width, width, 0)
        return lax.ppermute(piece, "head", [(i, (i + shift) % groups) for i in range(groups)])

    sums = (2 * half, HD, HD)
    by_head = pl.BlockSpec((tokens, HD), lambda h: (0, h))
    head_turned = pl.BlockSpec((1, HD, tokens), lambda h: (h, 0, 0))
    head_blocks = pl.BlockSpec((1, blocks, HD, HD), lambda h: (h, 0, 0, 0))
    row = pl.BlockSpec((1, 1, tokens), lambda h: (h, 0, 0))
    row_shape = jax.ShapeDtypeStruct((heads, 1, tokens), F32)
    turned_shape = jax.ShapeDtypeStruct((heads, HD, tokens), BF16)
    block_shape = jax.ShapeDtypeStruct((heads, blocks, HD, HD), F32)
    by_half = pl.BlockSpec((tokens, half * HD), lambda s: (0, s))
    half_row = pl.BlockSpec((half, 1, tokens), lambda s: (s, 0, 0))
    mine, theirs, keys_turned, scale, gated = pl.pallas_call(
        functools.partial(totals_kernel, half),
        grid=(2,),
        in_specs=[smem, by_half, by_half, whole((heads, tokens))],
        out_specs=[
            whole(sums),
            whole(sums),
            pl.BlockSpec((half, HD, tokens), lambda s: (s, 0, 0)),
            half_row,
            half_row,
        ],
        out_shape=[jax.ShapeDtypeStruct(sums, F32)] * 2 + [turned_shape, row_shape, row_shape],
        compiler_params=params(60),
        cost_estimate=cost(5),
        name="totals",
    )(core_arg, keys, values, gates.T)

    def before_of(parts, at):
        return sum(jnp.where(at >= shift, part.astype(F32), 0.0) for shift, part in enumerate(parts, 1))

    received = send(theirs, perm_core())
    chip = (mine + received).astype(F16)
    chip, keys_turned_later, weight = lax.optimization_barrier((chip, keys_turned, out_weight))
    along = [send(chip, perm_x(shift)) for shift in range(1, side)]
    parts = [rows_from(1, weight)]
    local_gram, local_moment, values_turned = pl.pallas_call(
        functools.partial(local_kernel, blocks),
        grid=(heads,),
        in_specs=[head_turned, row, row, by_head, by_head],
        out_specs=[head_blocks, head_blocks, head_turned],
        out_shape=[block_shape, block_shape, turned_shape],
        compiler_params=params(16),
        cost_estimate=cost(5),
        name="local",
    )(keys_turned_later, scale, gated, keys, values)

    row_total = (chip.astype(F32) + sum(part.astype(F32) for part in along)).astype(F16)
    row_total, queries_later, weight = lax.optimization_barrier((row_total, queries, weight))
    above = [send(row_total, perm_y(shift)) for shift in range(1, side)]
    parts += [rows_from(shift, weight) for shift in range(2, groups - 1)]
    columns_spec = pl.BlockSpec((1, SPAN, SPAN), lambda h: (h, 0, 0))
    columns_shape = jax.ShapeDtypeStruct((heads, SPAN, SPAN), F32)
    queries_turned, scale_columns, gated_columns = pl.pallas_call(
        functools.partial(columns_kernel, blocks),
        grid=(heads,),
        in_specs=[by_head, row, row],
        out_specs=[head_turned, columns_spec, columns_spec],
        out_shape=[turned_shape, columns_shape, columns_shape],
        compiler_params=params(16),
        cost_estimate=cost(3),
        name="columns",
    )(queries_later, scale, gated)

    above, weight = lax.optimization_barrier((above, weight))
    parts.append(rows_from(groups - 1, weight))
    before = before_of(along, x_at) + before_of(above, y_at)
    keep = before + jnp.where(core == 1, received, 0.0)
    give = before + jnp.where(core == 0, mine, 0.0)
    got = send(give, perm_core())

    step_blocks = 4
    step = step_blocks * SPAN
    units = heads * step_blocks
    tall = pl.BlockSpec((heads, HD, step), lambda b: (0, 0, b))
    some_blocks = pl.BlockSpec((heads, step_blocks, HD, HD), lambda b: (0, b, 0, 0))
    readout = pl.pallas_call(
        functools.partial(solve_kernel, heads, step_blocks, blocks // step_blocks),
        grid=(blocks // step_blocks,),
        in_specs=[
            smem,
            smem,
            tall,
            pl.BlockSpec((step, width), lambda b: (b, 0)),
            tall,
            whole((heads, SPAN, SPAN)),
            whole((heads, SPAN, SPAN)),
            some_blocks,
            tall,
            some_blocks,
            whole(sums),
            whole(sums),
        ],
        out_specs=pl.BlockSpec((step, width), lambda b: (b, 0)),
        out_shape=jax.ShapeDtypeStruct((tokens, width), BF16),
        scratch_shapes=[
            pltpu.VMEM((units, 2 * HD, 2 * HD), BF16),
            pltpu.VMEM((units, HD, 2 * HD), BF16),
            pltpu.VMEM((units, SPAN, SPAN), F32),
            pltpu.VMEM((units, HD, SPAN), F32),
            pltpu.VMEM((units, HD, SPAN), F32),
            pltpu.VMEM((units, HD, SPAN), F32),
            pltpu.VMEM((units, 1, SPAN), F32),
        ],
        compiler_params=params(32),
        cost_estimate=cost(30),
        name="solve",
    )(
        core_arg,
        ridge,
        queries_turned,
        keys,
        keys_turned,
        scale_columns,
        gated_columns,
        local_gram,
        values_turned,
        local_moment,
        keep,
        got,
    )

    step = 2 * SPAN
    out = pl.pallas_call(
        functools.partial(project_kernel, groups),
        grid_spec=pltpu.PrefetchScalarGridSpec(
            num_scalar_prefetch=1,
            grid=(tokens // step,),
            in_specs=[
                pl.BlockSpec((step, width), lambda b, g: (b, 0)),
                pl.BlockSpec((width, columns), lambda b, g: (g[0], 0)),
            ]
            + [pl.BlockSpec(memory_space=pltpu.VMEM)] * (groups - 1),
            out_specs=pl.BlockSpec((1, step, columns * groups), lambda b, g: (0, b, 0)),
        ),
        out_shape=jax.ShapeDtypeStruct((1, tokens, columns * groups), BF16),
        compiler_params=params(12),
        cost_estimate=cost(5),
        name="project",
    )(group_arg, readout, out_weight, *parts)
    return out


def solution(mesh):
    return jax.shard_map(
        functools.partial(shards, mesh),
        mesh=mesh,
        in_specs=(
            P("seq", "head"),
            P("seq", "head"),
            P("seq", "head"),
            P("seq", "head"),
            P("head"),
            P(None, "head"),
        ),
        out_specs=P("head", "seq", None),
        check_vma=False,
    )
```

time: 76.7 us -> 68.4 us (0.89)
  Pallas kernels: 49.4 us -> 40.6 us
  other arithmetic: 2.65 us -> 1.28 us
    pallas_call x3, Pallas kernels: 39.9 us -> 34.1 us  [the longest x1 29.1 us: shards(): pl.pallas_call(functools.partial(solve_kernel, heads, step_blocks, blocks...]
    pallas_call x1, Pallas kernels: 5.36 us -> 2.34 us  [shards(): pl.pallas_call(functools.partial(local_kernel, blocks), grid=(heads,), in...]
    unnamed x12 -> x22, local copies, waits for them, and re-layouts: 1.9 us -> 3.92 us
    reshape x1 -> x0, local copies, waits for them, and re-layouts: 1.33 us -> none  [shards(): gates.T.reshape(2, half, tokens)]
  transfers between devices with their start and end apart: 11 -> 11, of which waited for: 1 -> 1; matrix products, arithmetic and copies ran while one was open for 2% -> 1% of each run, Pallas kernels for 47% -> 47%
where the time goes in v3:
time: 68.4 us; the launch traced here: 68.1 us
  Pallas kernels  40.6 us (59%)
  starting transfers between devices  20.6 us (30%)
  local copies, waits for them, and re-layouts  4.03 us (6%)
  waiting for transfers between devices  1.4 us (2%)
  other arithmetic  1.28 us (2%)
    pallas_call x1, Pallas kernels, shards(): pl.pallas_call(functools.partial(solve_kernel, heads, step_blocks, blocks...  29.1 us
    ppermute x8, starting transfers between devices, send(): return lax.ppermute(array, 'seq', perm)  14.2 us
    ppermute x3, starting transfers between devices, rows_from(): lax.ppermute(piece, 'head', [(i, (i + shift) % groups) for i in range(gro...  6.45 us
    pallas_call x1, Pallas kernels, shards(): pl.pallas_call(functools.partial(totals_kernel, half), grid=(2,), in_spec...  4.13 us
    pallas_call x1, Pallas kernels, shards(): pl.pallas_call(functools.partial(project_kernel, groups), grid_spec=pltpu...  4.12 us
    unnamed x22, local copies, waits for them, and re-layouts  3.92 us
    pallas_call x1, Pallas kernels, shards(): pl.pallas_call(functools.partial(local_kernel, blocks), grid=(heads,), in...  2.34 us
    ppermute x8, waiting for transfers between devices, send(): return lax.ppermute(array, 'seq', perm)  1.39 us
  transfers between devices with their start and end apart: 11, of which 1 were waited for; matrix products, arithmetic and copies ran while one was open for 1% of the time, Pallas kernels for 47%

profile of v3, /device:TPU:1, one launch (start us, length us, event | category | flops | bytes accessed | tf_op | source)
XLA Modules:
  0.0 68.1 jit_solution(7336316980396311998)
XLA Ops:
  0.0 0.0 copy-start
  0.0 0.0 copy-start.1
  0.0 4.1 %totals.1 = (f32[4,128,128]{2,1,0:T(8,128)}, f32[4,128,128]{2,1,0:T(8,128)}, bf16[4,128,1024]{2,1,0:T(8,128)(2,1)}, f32[4,1,1024]{2,1,0:T(1,128)}, f32[4,1,1024]{2,1,0:T(1,128)}) custom-call(s32[1]{0:T(128)} %bitcast.1.core_ref, bf16[1024,512]{1,0:T(8,128)(2,1)} %keys_ref.5, bf16[1024,512]{1,0:T(8,128)(2,1)} %values_ref.3, f32[4,1024]{1,0:T(4,128)} %bitcast.3), custom_call_target="tpu_custom_call" | custom-call | flops 5500000256 | bytes 5000000 | tf_op jit(solution)/shard_map/totals/pallas_call | solution.py:282
  4.1 1.5 %collective-permute-start = (f32[4,128,128]{2,1,0:T(8,128)}, f32[4,128,128]{2,1,0:T(8,128)S(1)}, u32[]{:S(2)}, u32[]{:S(2)}) collective-permute-start(f32[4,128,128]{2,1,0:T(8,128)} %get-tuple-element.27), channel_id=1, source_target_pairs={{0,4},{4,0},{8,12},{12,8},{16,20},{20,16},{24,28},{28,24},{32,36},... | collective-permute-start | bytes 786440 | tf_op jit(solution)/shard_map/ppermute | solution.py:266
  5.6 1.4 %collective-permute-done = f32[4,128,128]{2,1,0:T(8,128)S(1)} collective-permute-done((f32[4,128,128]{2,1,0:T(8,128)}, f32[4,128,128]{2,1,0:T(8,128)S(1)}, u32[]{:S(2)}, u32[]{:S(2)}) %collective-permute-start) | collective-permute-done | bytes 262176 | tf_op jit(solution)/shard_map/ppermute | solution.py:266
  7.0 1.0 %add_convert_fusion = f16[4,128,128]{2,1,0:T(8,128)(2,1)S(1)} fusion(f32[4,128,128]{2,1,0:T(8,128)} %get-tuple-element.26, f32[4,128,128]{2,1,0:T(8,128)S(1)} %collective-permute-done), kind=kLoop, calls=%fused_computation.12 | loop fusion | flops 131072 | bytes 655360 | tf_op jit(solution)/shard_map/convert_element_type | solution.py:303
  8.0 1.4 %collective-permute-start.1 = (f16[4,128,128]{2,1,0:T(8,128)(2,1)S(1)}, f16[4,128,128]{2,1,0:T(8,128)(2,1)S(1)}, u32[]{:S(2)}, u32[]{:S(2)}) collective-permute-start(f16[4,128,128]{2,1,0:T(8,128)(2,1)S(1)} %add_convert_fusion), channel_id=1, source_target_pairs={{0,8},{4,12},{8,16},{12,20},{16,24},{20,28},{24,0},{28,4},{32,40},... | collective-permute-start | bytes 393224 | tf_op jit(solution)/shard_map/ppermute | solution.py:266
  9.3 2.4 %collective-permute-start.2 = (f16[4,128,128]{2,1,0:T(8,128)(2,1)S(1)}, f16[4,128,128]{2,1,0:T(8,128)(2,1)S(1)}, u32[]{:S(2)}, u32[]{:S(2)}) collective-permute-start(f16[4,128,128]{2,1,0:T(8,128)(2,1)S(1)} %add_convert_fusion), channel_id=1, source_target_pairs={{0,16},{4,20},{8,24},{12,28},{16,0},{20,4},{24,8},{28,12},{32,48},... | collective-permute-start | bytes 393224 | tf_op jit(solution)/shard_map/ppermute | solution.py:266
  11.8 1.2 %collective-permute-start.3 = (f16[4,128,128]{2,1,0:T(8,128)(2,1)S(1)}, f16[4,128,128]{2,1,0:T(8,128)(2,1)S(1)}, u32[]{:S(2)}, u32[]{:S(2)}) collective-permute-start(f16[4,128,128]{2,1,0:T(8,128)(2,1)S(1)} %add_convert_fusion), channel_id=1, source_target_pairs={{0,24},{4,28},{8,0},{12,4},{16,8},{20,12},{24,16},{28,20},{32,56},... | collective-permute-start | bytes 393224 | tf_op jit(solution)/shard_map/ppermute | solution.py:266
  12.9 0.0 copy-done
  13.0 1.7 %collective-permute-start.8 = (bf16[512,512]{1,0:T(8,128)(2,1)S(1)}, bf16[512,512]{1,0:T(8,128)(2,1)S(1)}, u32[]{:S(2)}, u32[]{:S(2)}) collective-permute-start(bf16[512,512]{1,0:T(8,128)(2,1)S(1)} %constant_dynamic-slice_fusion.2), channel_id=1, source_target_pairs={{0,1},{1,2},{2,3},{3,0},{4,5},{5,6},{6,7},{7,4},{8,9},{9,10},{10,1... | collective-permute-start | bytes 1572872 | tf_op jit(solution)/shard_map/ppermute | solution.py:270
  14.7 0.0 copy-done.1
  14.7 0.0 copy-start.3
  14.7 1.2 %copy-done.3 = bf16[1024,512]{1,0:T(8,128)(2,1)S(1)} copy-done((bf16[1024,512]{1,0:T(8,128)(2,1)S(1)}, bf16[1024,512]{1,0:T(8,128)(2,1)}, u32[]{:S(2)}) %copy-start.3) | copy-done | bytes 1048600
  15.9 1.2 %copy-done.6 = bf16[4,128,1024]{2,1,0:T(8,128)(2,1)S(1)} copy-done((bf16[4,128,1024]{2,1,0:T(8,128)(2,1)S(1)}, bf16[4,128,1024]{2,1,0:T(8,128)(2,1)}, u32[]{:S(2)}) %copy-start.6) | copy-done | bytes 1048600
  17.1 0.7 %copy-done.8 = f32[4,1,1024]{2,1,0:T(1,128)S(1)} copy-done((f32[4,1,1024]{2,1,0:T(1,128)S(1)}, f32[4,1,1024]{2,1,0:T(1,128)}, u32[]{:S(2)}) %copy-start.8) | copy-done | bytes 16408
  17.8 0.7 %copy-done.9 = f32[4,1,1024]{2,1,0:T(1,128)S(1)} copy-done((f32[4,1,1024]{2,1,0:T(1,128)S(1)}, f32[4,1,1024]{2,1,0:T(1,128)}, u32[]{:S(2)}) %copy-start.9) | copy-done | bytes 16408
  18.6 2.3 %local.1 = (f32[4,8,128,128]{3,2,1,0:T(8,128)S(1)}, f32[4,8,128,128]{3,2,1,0:T(8,128)S(1)}, bf16[4,128,1024]{2,1,0:T(8,128)(2,1)S(1)}) custom-call(bf16[4,128,1024]{2,1,0:T(8,128)(2,1)S(1)} %copy-done.6, f32[4,1,1024]{2,1,0:T(1,128)S(1)} %copy-done.8, f32[4,1,1024]{2,1,0:T(1,128)S(1)} %copy-done.9, bf16[1024,512]{1,0:T(8,128)(2,1)S(1)} %copy-done.3, ...), custom_call_target="tpu_custom_call" | custom-call | flops 5500000256 | bytes 5000000 | tf_op jit(solution)/shard_map/local/pallas_call | solution.py:307
  20.9 0.0 collective-permute-done.1
  20.9 0.0 collective-permute-done.2
  20.9 0.0 collective-permute-done.3
  20.9 0.1 fusion.4
  21.0 0.0 copy-start.10
  21.0 1.4 %collective-permute-start.4 = (f16[4,128,128]{2,1,0:T(8,128)(2,1)S(1)}, f16[4,128,128]{2,1,0:T(8,128)(2,1)S(1)}, u32[]{:S(2)}, u32[]{:S(2)}) collective-permute-start(f16[4,128,128]{2,1,0:T(8,128)(2,1)S(1)} %fusion.4), channel_id=1, source_target_pairs={{0,32},{4,36},{8,40},{12,44},{16,48},{20,52},{24,56},{28,60},{32,6... | collective-permute-start | bytes 393224 | tf_op jit(solution)/shard_map/ppermute | solution.py:266
  22.4 2.6 %collective-permute-start.5 = (f16[4,128,128]{2,1,0:T(8,128)(2,1)S(1)}, f16[4,128,128]{2,1,0:T(8,128)(2,1)S(1)}, u32[]{:S(2)}, u32[]{:S(2)}) collective-permute-start(f16[4,128,128]{2,1,0:T(8,128)(2,1)S(1)} %fusion.4), channel_id=1, source_target_pairs={{0,64},{4,68},{8,72},{12,76},{16,80},{20,84},{24,88},{28,92},{32,9... | collective-permute-start | bytes 393224 | tf_op jit(solution)/shard_map/ppermute | solution.py:266
  25.0 1.1 %collective-permute-start.6 = (f16[4,128,128]{2,1,0:T(8,128)(2,1)S(1)}, f16[4,128,128]{2,1,0:T(8,128)(2,1)S(1)}, u32[]{:S(2)}, u32[]{:S(2)}) collective-permute-start(f16[4,128,128]{2,1,0:T(8,128)(2,1)S(1)} %fusion.4), channel_id=1, source_target_pairs={{0,96},{4,100},{8,104},{12,108},{16,112},{20,116},{24,120},{28,124... | collective-permute-start | bytes 393224 | tf_op jit(solution)/shard_map/ppermute | solution.py:266
  26.1 0.0 copy-done.2
  26.1 0.9 %columns.1 = (bf16[4,128,1024]{2,1,0:T(8,128)(2,1)S(1)}, f32[4,128,128]{2,1,0:T(8,128)S(1)}, f32[4,128,128]{2,1,0:T(8,128)S(1)}) custom-call(bf16[1024,512]{1,0:T(8,128)(2,1)S(1)} %copy-done.2, f32[4,1,1024]{2,1,0:T(1,128)S(1)} %copy-done.8, f32[4,1,1024]{2,1,0:T(1,128)S(1)} %copy-done.9), custom_call_target="tpu_custom_call" | custom-call | flops 3300000000 | bytes 3000000 | tf_op jit(solution)/shard_map/columns/pallas_call | solution.py:324
  27.0 0.0 copy-start.4
  27.0 0.0 copy-start.5
  27.1 0.0 copy-start.7
  27.1 3.4 %collective-permute-start.9 = (bf16[512,512]{1,0:T(8,128)(2,1)S(1)}, bf16[512,512]{1,0:T(8,128)(2,1)S(1)}, u32[]{:S(2)}, u32[]{:S(2)}) collective-permute-start(bf16[512,512]{1,0:T(8,128)(2,1)S(1)} %constant_dynamic-slice_fusion.1), channel_id=1, source_target_pairs={{0,2},{1,3},{2,0},{3,1},{4,6},{5,7},{6,4},{7,5},{8,10},{9,11},{10,... | collective-permute-start | bytes 1572872 | tf_op jit(solution)/shard_map/ppermute | solution.py:270
  30.5 0.0 collective-permute-done.4
  30.5 0.0 collective-permute-done.5
  30.5 0.0 collective-permute-done.6
  30.5 0.0 copy-done.10
  30.5 0.2 select_add_fusion
  30.7 2.7 %collective-permute-start.7 = (f32[4,128,128]{2,1,0:T(8,128)S(1)}, f32[4,128,128]{2,1,0:T(8,128)S(1)}, u32[]{:S(2)}, u32[]{:S(2)}) collective-permute-start(f32[4,128,128]{2,1,0:T(8,128)S(1)} %get-tuple-element.47), channel_id=1, source_target_pairs={{0,4},{4,0},{8,12},{12,8},{16,20},{20,16},{24,28},{28,24},{32,36},... | collective-permute-start | bytes 786440 | tf_op jit(solution)/shard_map/ppermute | solution.py:266
  33.4 1.4 %collective-permute-start.10 = (bf16[512,512]{1,0:T(8,128)(2,1)S(1)}, bf16[512,512]{1,0:T(8,128)(2,1)S(1)}, u32[]{:S(2)}, u32[]{:S(2)}) collective-permute-start(bf16[512,512]{1,0:T(8,128)(2,1)S(1)} %constant_dynamic-slice_fusion), channel_id=1, source_target_pairs={{0,3},{1,0},{2,1},{3,2},{4,7},{5,4},{6,5},{7,6},{8,11},{9,8},{10,9... | collective-permute-start | bytes 1572872 | tf_op jit(solution)/shard_map/ppermute | solution.py:270
  34.8 0.0 collective-permute-done.7.got_ref
  34.8 0.0 copy-done.4
  34.9 0.0 copy-done.5
  34.9 0.0 copy-done.7
  34.9 29.1 %solve.1.readout_ref = bf16[1024,512]{1,0:T(8,128)(2,1)S(1)} custom-call(s32[1]{0:T(128)} %bitcast.1.core_ref, f32[4]{0:T(128)S(1)} %copy-done.5, bf16[4,128,1024]{2,1,0:T(8,128)(2,1)S(1)} %get-tuple-element.34.queries_ref, bf16[1024,512]{1,0:T(8,128)(2,1)S(1)} %copy-done.4, bf16[4,128,1024]{2,1,0:T(8,128)(2,1)S(1)} %copy-done.7, ...), custom_call_target="tpu_custom_call" | custom-call | flops 32999999488 | bytes 30000000 | tf_op jit(solution)/shard_map/solve/pallas_call | solution.py:347
  64.0 0.0 collective-permute-done.8.rest_0_
  64.0 0.0 collective-permute-done.9.rest_1_
  64.0 0.0 collective-permute-done.10.rest_2_
  64.0 4.1 %project.1 = bf16[1,1024,2048]{2,1,0:T(8,128)(2,1)} custom-call(s32[1]{0:T(128)} %bitcast.group_ref, bf16[1024,512]{1,0:T(8,128)(2,1)S(1)} %solve.1.readout_ref, bf16[2048,512]{1,0:T(8,128)(2,1)S(1)} %copy-done, bf16[512,512]{1,0:T(8,128)(2,1)S(1)} %collective-permute-done.8.rest_0_, bf16[512,512]{1,0:T(8,128)(2,1)S(1)} %collective-permute-done.9.rest_1_, ...), custom_call_target="tpu_custom_call" | custom-call | flops 5500000256 | bytes 5000000 | tf_op jit(solution)/shard_map/project/pallas_call | solution.py:394
  (8 shorter events, 0.2 us)
Async XLA Ops:
  0.0 12.9 %copy-start = (bf16[2048,512]{1,0:T(8,128)(2,1)S(1)}, bf16[2048,512]{1,0:T(8,128)(2,1)}, u32[]{:S(2)}) copy-start(bf16[2048,512]{1,0:T(8,128)(2,1)} %own_ref.1) | copy-start | bytes 6291460
  0.0 14.7 %copy-start.1 = (bf16[1024,512]{1,0:T(8,128)(2,1)S(1)}, bf16[1024,512]{1,0:T(8,128)(2,1)}, u32[]{:S(2)}) copy-start(bf16[1024,512]{1,0:T(8,128)(2,1)} %values_ref.3) | copy-start | bytes 3145732
  4.1 2.8 %collective-permute-start = (f32[4,128,128]{2,1,0:T(8,128)}, f32[4,128,128]{2,1,0:T(8,128)S(1)}, u32[]{:S(2)}, u32[]{:S(2)}) collective-permute-start(f32[4,128,128]{2,1,0:T(8,128)} %get-tuple-element.27), channel_id=1, source_target_pairs={{0,4},{4,0},{8,12},{12,8},{16,20},{20,16},{24,28},{28,24},{32,36},... | collective-permute-start | bytes 786440 | tf_op jit(solution)/shard_map/ppermute | solution.py:266
  8.0 13.0 %collective-permute-start.1 = (f16[4,128,128]{2,1,0:T(8,128)(2,1)S(1)}, f16[4,128,128]{2,1,0:T(8,128)(2,1)S(1)}, u32[]{:S(2)}, u32[]{:S(2)}) collective-permute-start(f16[4,128,128]{2,1,0:T(8,128)(2,1)S(1)} %add_convert_fusion), channel_id=1, source_target_pairs={{0,8},{4,12},{8,16},{12,20},{16,24},{20,28},{24,0},{28,4},{32,40},... | collective-permute-start | bytes 393224 | tf_op jit(solution)/shard_map/ppermute | solution.py:266
  9.3 11.6 %collective-permute-start.2 = (f16[4,128,128]{2,1,0:T(8,128)(2,1)S(1)}, f16[4,128,128]{2,1,0:T(8,128)(2,1)S(1)}, u32[]{:S(2)}, u32[]{:S(2)}) collective-permute-start(f16[4,128,128]{2,1,0:T(8,128)(2,1)S(1)} %add_convert_fusion), channel_id=1, source_target_pairs={{0,16},{4,20},{8,24},{12,28},{16,0},{20,4},{24,8},{28,12},{32,48},... | collective-permute-start | bytes 393224 | tf_op jit(solution)/shard_map/ppermute | solution.py:266
  11.8 9.2 %collective-permute-start.3 = (f16[4,128,128]{2,1,0:T(8,128)(2,1)S(1)}, f16[4,128,128]{2,1,0:T(8,128)(2,1)S(1)}, u32[]{:S(2)}, u32[]{:S(2)}) collective-permute-start(f16[4,128,128]{2,1,0:T(8,128)(2,1)S(1)} %add_convert_fusion), channel_id=1, source_target_pairs={{0,24},{4,28},{8,0},{12,4},{16,8},{20,12},{24,16},{28,20},{32,56},... | collective-permute-start | bytes 393224 | tf_op jit(solution)/shard_map/ppermute | solution.py:266
  13.0 51.0 %collective-permute-start.8 = (bf16[512,512]{1,0:T(8,128)(2,1)S(1)}, bf16[512,512]{1,0:T(8,128)(2,1)S(1)}, u32[]{:S(2)}, u32[]{:S(2)}) collective-permute-start(bf16[512,512]{1,0:T(8,128)(2,1)S(1)} %constant_dynamic-slice_fusion.2), channel_id=1, source_target_pairs={{0,1},{1,2},{2,3},{3,0},{4,5},{5,6},{6,7},{7,4},{8,9},{9,10},{10,1... | collective-permute-start | bytes 1572872 | tf_op jit(solution)/shard_map/ppermute | solution.py:270
  14.7 1.2 %copy-start.3 = (bf16[1024,512]{1,0:T(8,128)(2,1)S(1)}, bf16[1024,512]{1,0:T(8,128)(2,1)}, u32[]{:S(2)}) copy-start(bf16[1024,512]{1,0:T(8,128)(2,1)} %keys_ref.5) | copy-start | bytes 3145732
  15.9 1.2 %copy-start.6 = (bf16[4,128,1024]{2,1,0:T(8,128)(2,1)S(1)}, bf16[4,128,1024]{2,1,0:T(8,128)(2,1)}, u32[]{:S(2)}) copy-start(bf16[4,128,1024]{2,1,0:T(8,128)(2,1)} %get-tuple-element.37.turned_ref) | copy-start | bytes 3145732
  17.1 0.7 %copy-start.8 = (f32[4,1,1024]{2,1,0:T(1,128)S(1)}, f32[4,1,1024]{2,1,0:T(1,128)}, u32[]{:S(2)}) copy-start(f32[4,1,1024]{2,1,0:T(1,128)} %get-tuple-element.32.scale_ref) | copy-start | bytes 49156
  17.8 0.7 %copy-start.9 = (f32[4,1,1024]{2,1,0:T(1,128)S(1)}, f32[4,1,1024]{2,1,0:T(1,128)}, u32[]{:S(2)}) copy-start(f32[4,1,1024]{2,1,0:T(1,128)} %get-tuple-element.33.gated_ref) | copy-start | bytes 49156
  18.6 7.5 %copy-start.2 = (bf16[1024,512]{1,0:T(8,128)(2,1)S(1)}, bf16[1024,512]{1,0:T(8,128)(2,1)}, u32[]{:S(2)}) copy-start(bf16[1024,512]{1,0:T(8,128)(2,1)} %queries_ref) | copy-start | bytes 3145732
  21.0 9.5 %copy-start.10 = (f32[4,128,128]{2,1,0:T(8,128)S(1)}, f32[4,128,128]{2,1,0:T(8,128)}, u32[]{:S(2)}) copy-start(f32[4,128,128]{2,1,0:T(8,128)} %get-tuple-element.26) | copy-start | bytes 786436
  21.0 9.5 %collective-permute-start.4 = (f16[4,128,128]{2,1,0:T(8,128)(2,1)S(1)}, f16[4,128,128]{2,1,0:T(8,128)(2,1)S(1)}, u32[]{:S(2)}, u32[]{:S(2)}) collective-permute-start(f16[4,128,128]{2,1,0:T(8,128)(2,1)S(1)} %fusion.4), channel_id=1, source_target_pairs={{0,32},{4,36},{8,40},{12,44},{16,48},{20,52},{24,56},{28,60},{32,6... | collective-permute-start | bytes 393224 | tf_op jit(solution)/shard_map/ppermute | solution.py:266
  22.4 8.1 %collective-permute-start.5 = (f16[4,128,128]{2,1,0:T(8,128)(2,1)S(1)}, f16[4,128,128]{2,1,0:T(8,128)(2,1)S(1)}, u32[]{:S(2)}, u32[]{:S(2)}) collective-permute-start(f16[4,128,128]{2,1,0:T(8,128)(2,1)S(1)} %fusion.4), channel_id=1, source_target_pairs={{0,64},{4,68},{8,72},{12,76},{16,80},{20,84},{24,88},{28,92},{32,9... | collective-permute-start | bytes 393224 | tf_op jit(solution)/shard_map/ppermute | solution.py:266
  25.0 5.5 %collective-permute-start.6 = (f16[4,128,128]{2,1,0:T(8,128)(2,1)S(1)}, f16[4,128,128]{2,1,0:T(8,128)(2,1)S(1)}, u32[]{:S(2)}, u32[]{:S(2)}) collective-permute-start(f16[4,128,128]{2,1,0:T(8,128)(2,1)S(1)} %fusion.4), channel_id=1, source_target_pairs={{0,96},{4,100},{8,104},{12,108},{16,112},{20,116},{24,120},{28,124... | collective-permute-start | bytes 393224 | tf_op jit(solution)/shard_map/ppermute | solution.py:266
  27.0 7.8 %copy-start.4 = (bf16[1024,512]{1,0:T(8,128)(2,1)S(1)}, bf16[1024,512]{1,0:T(8,128)(2,1)}, u32[]{:S(2)}) copy-start(bf16[1024,512]{1,0:T(8,128)(2,1)} %keys_ref.5) | copy-start | bytes 3145732
  27.0 7.8 %copy-start.5 = (f32[4]{0:T(128)S(1)}, f32[4]{0:T(128)}, u32[]{:S(2)}) copy-start(f32[4]{0:T(128)} %ridge_ref.1) | copy-start | bytes 52
  27.1 7.8 %copy-start.7 = (bf16[4,128,1024]{2,1,0:T(8,128)(2,1)S(1)}, bf16[4,128,1024]{2,1,0:T(8,128)(2,1)}, u32[]{:S(2)}) copy-start(bf16[4,128,1024]{2,1,0:T(8,128)(2,1)} %get-tuple-element.37.turned_ref) | copy-start | bytes 3145732
  27.1 36.8 %collective-permute-start.9 = (bf16[512,512]{1,0:T(8,128)(2,1)S(1)}, bf16[512,512]{1,0:T(8,128)(2,1)S(1)}, u32[]{:S(2)}, u32[]{:S(2)}) collective-permute-start(bf16[512,512]{1,0:T(8,128)(2,1)S(1)} %constant_dynamic-slice_fusion.1), channel_id=1, source_target_pairs={{0,2},{1,3},{2,0},{3,1},{4,6},{5,7},{6,4},{7,5},{8,10},{9,11},{10,... | collective-permute-start | bytes 1572872 | tf_op jit(solution)/shard_map/ppermute | solution.py:270
  30.7 4.1 %collective-permute-start.7 = (f32[4,128,128]{2,1,0:T(8,128)S(1)}, f32[4,128,128]{2,1,0:T(8,128)S(1)}, u32[]{:S(2)}, u32[]{:S(2)}) collective-permute-start(f32[4,128,128]{2,1,0:T(8,128)S(1)} %get-tuple-element.47), channel_id=1, source_target_pairs={{0,4},{4,0},{8,12},{12,8},{16,20},{20,16},{24,28},{28,24},{32,36},... | collective-permute-start | bytes 786440 | tf_op jit(solution)/shard_map/ppermute | solution.py:266
  33.4 30.5 %collective-permute-start.10 = (bf16[512,512]{1,0:T(8,128)(2,1)S(1)}, bf16[512,512]{1,0:T(8,128)(2,1)S(1)}, u32[]{:S(2)}, u32[]{:S(2)}) collective-permute-start(bf16[512,512]{1,0:T(8,128)(2,1)S(1)} %constant_dynamic-slice_fusion), channel_id=1, source_target_pairs={{0,3},{1,0},{2,1},{3,2},{4,7},{5,4},{6,5},{7,6},{8,11},{9,8},{10,9... | collective-permute-start | bytes 1572872 | tf_op jit(solution)/shard_map/ppermute | solution.py:270

commit v4 on v3

--- a/solution.py
+++ b/solution.py
@@ -14,6 +14,7 @@
 BF16 = jnp.bfloat16
 F16 = jnp.float16
 SHRINK = 16.0
+LAG = 4
 
 
 def two_terms(value):
@@ -114,7 +115,6 @@
     norms,
 ):
     core = core_ref[0]
-    half = heads // 2
     row = lax.broadcasted_iota(jnp.int32, (SPAN, SPAN), 0)
     column = lax.broadcasted_iota(jnp.int32, (SPAN, SPAN), 1)
     causal = row <= column
@@ -123,33 +123,39 @@
     step = pl.program_id(0)
 
     def column_of(ref, head, block):
-        options = [ref[head, :, at * blocks + block : at * blocks + block + 1] for at in range(steps)]
-        value = options[0]
+        value = ref[head, :, block : block + 1]
         for at in range(1, steps):
-            value = jnp.where(step == at, options[at], value)
+            other = at * blocks + block
+            value = jnp.where(step == at, ref[head, :, other : other + 1], value)
         return value
 
+    start = pl.multiple_of(step * blocks * SPAN, blocks * SPAN)
+    half = heads // 2
+    grams, moments = [], []
     for head in range(heads):
-        prior = jnp.where(core == head // half, keep_ref[head % half], got_ref[head % half])
-        prior = prior + jnp.where(row == column, ridge_ref[head], 0.0)
-        for block in range(blocks):
-            unit = block * heads + head
-            rows = slice(block * SPAN, (block + 1) * SPAN)
-            own = keys_ref[rows, head_cols(head)]
-            masks[unit] = jnp.where(causal, column_of(scale_ref, head, block), 0.0)
-            high, low = two_terms(prior + local_ref[head, block])
-            first[unit, :HD, :HD] = high
-            first[unit, :HD, HD:] = high
-            first[unit, HD:, :HD] = own
-            first[unit, HD:, HD:] = own
-            second[unit, :, :HD] = low
-            second[unit, :, HD:] = turned_ref[head, :, rows]
-            query = queries_ref[head, :, rows].astype(F32)
-            query = query * lax.rsqrt(jnp.sum(query * query, axis=0, keepdims=True) + EPS)
-            xs[unit] = jnp.zeros((HD, SPAN), F32)
-            rs[unit] = query
-            ds[unit] = query
-            norms[unit] = jnp.sum(query * query, axis=0, keepdims=True)
+        own, at = core == head // half, head % half
+        gram = jnp.where(own, keep_ref[at], got_ref[at])
+        grams.append(gram + jnp.where(row == column, ridge_ref[head], 0.0))
+        moments.append(jnp.where(own, keep_ref[half + at], got_ref[half + at]).T * SHRINK)
+
+    def prepare(unit):
+        head, block = units[unit]
+        rows = pl.ds(start + block * SPAN, SPAN)
+        own = keys_ref[rows, head_cols(head)]
+        masks[unit] = jnp.where(causal, column_of(scale_ref, head, block), 0.0)
+        high, low = two_terms(grams[head] + local_ref[head, step * blocks + block])
+        first[unit, :HD, :HD] = high
+        first[unit, :HD, HD:] = high
+        first[unit, HD:, :HD] = own
+        first[unit, HD:, HD:] = own
+        second[unit, :, :HD] = low
+        second[unit, :, HD:] = turned_ref[head, :, rows]
+        query = queries_ref[head, :, rows].astype(F32)
+        query = query * lax.rsqrt(jnp.sum(query * query, axis=0, keepdims=True) + EPS)
+        xs[unit] = jnp.zeros((HD, SPAN), F32)
+        rs[unit] = query
+        ds[unit] = query
+        norms[unit] = jnp.sum(query * query, axis=0, keepdims=True)
 
     def product_of(unit):
         high, low = two_terms(ds[unit])
@@ -162,34 +168,14 @@
     def update(unit, image):
         direction = ds[unit]
         now = norms[unit]
-        step = now / (jnp.sum(direction * image, axis=0, keepdims=True) + EPS)
-        xs[unit] += step * direction
-        residual = rs[unit] - step * image
+        size = now / (jnp.sum(direction * image, axis=0, keepdims=True) + EPS)
+        xs[unit] += size * direction
+        residual = rs[unit] - size * image
         rs[unit] = residual
         after = jnp.sum(residual * residual, axis=0, keepdims=True)
         ds[unit] = residual + (after / (now + EPS)) * direction
         norms[unit] = after
 
-    lag = 4
-
-    def sweep_once(sweep, carry):
-        products, images = {}, {}
-        for at in range(count + 2 * lag):
-            if at < count:
-                products[at] = product_of(at)
-            if 0 <= at - lag < count:
-                images[at - lag] = image_of(at - lag, *products.pop(at - lag))
-            if 0 <= at - 2 * lag < count:
-                update(at - 2 * lag, images.pop(at - 2 * lag))
-        return carry
-
-    lax.fori_loop(0, ITERS, sweep_once, 0)
-
-    priors = []
-    for head in range(heads):
-        at = half + head % half
-        priors.append(jnp.where(core == head // half, keep_ref[at], got_ref[at]).T * SHRINK)
-
     def correlations_of(unit):
         high, low = two_terms(xs[unit])
         return high, low, dot(first[unit, HD:], jnp.concatenate([high, low], axis=0))
@@ -197,21 +183,30 @@
     def readout_of(unit, high, low, product):
         head, block = units[unit]
         corr = jnp.where(causal, product * column_of(gated_ref, head, block), 0.0).astype(BF16)
-        moment_high, moment_low = two_terms(priors[head] + local_moment_ref[head, block])
-        values = values_ref[head, :, block * SPAN : (block + 1) * SPAN]
+        moment_high, moment_low = two_terms(moments[head] + local_moment_ref[head, step * blocks + block])
+        values = values_ref[head, :, pl.ds(start + block * SPAN, SPAN)]
         left = jnp.concatenate([moment_high, moment_high, moment_low, values], axis=1)
         return dot(left, jnp.concatenate([high, low, high, corr], axis=0))
 
-    products, readouts = {}, {}
-    for at in range(count + 2 * lag):
+    def store(unit, readout):
+        head, block = units[unit]
+        readout_ref[block * SPAN : (block + 1) * SPAN, head_cols(head)] = readout.T.astype(BF16)
+
+    solved = ITERS * count
+    products, images = {}, {}
+    for at in range(solved + count + 2 * LAG):
         if at < count:
-            products[at] = correlations_of(at)
-        if 0 <= at - lag < count:
-            readouts[at - lag] = readout_of(at - lag, *products.pop(at - lag))
-        if 0 <= at - 2 * lag < count:
-            head, block = units[at - 2 * lag]
-            rows = slice(block * SPAN, (block + 1) * SPAN)
-            readout_ref[rows, head_cols(head)] = readouts.pop(at - 2 * lag).T.astype(BF16)
+            prepare(at)
+        if at < solved + count:
+            products[at] = product_of(at % count) if at < solved else correlations_of(at % count)
+        then = at - LAG
+        if 0 <= then < solved + count:
+            stage = image_of if then < solved else readout_of
+            images[then] = stage(then % count, *products.pop(then))
+        then = at - 2 * LAG
+        if 0 <= then < solved + count:
+            stage = update if then < solved else store
+            stage(then % count, images.pop(then))
 
 
 def project_kernel(groups, group_ref, readout_ref, own_ref, *rest):
@@ -342,25 +337,14 @@
     step_blocks = 4
     step = step_blocks * SPAN
     units = heads * step_blocks
-    tall = pl.BlockSpec((heads, HD, step), lambda b: (0, 0, b))
-    some_blocks = pl.BlockSpec((heads, step_blocks, HD, HD), lambda b: (0, b, 0, 0))
     readout = pl.pallas_call(
         functools.partial(solve_kernel, heads, step_blocks, blocks // step_blocks),
         grid=(blocks // step_blocks,),
         in_specs=[
             smem,
             smem,
-            tall,
-            pl.BlockSpec((step, width), lambda b: (b, 0)),
-            tall,
-            whole((heads, SPAN, SPAN)),
-            whole((heads, SPAN, SPAN)),
-            some_blocks,
-            tall,
-            some_blocks,
-            whole(sums),
-            whole(sums),
-        ],
+        ]
+        + [pl.BlockSpec(memory_space=pltpu.VMEM)] * 10,
         out_specs=pl.BlockSpec((step, width), lambda b: (b, 0)),
         out_shape=jax.ShapeDtypeStruct((tokens, width), BF16),
         scratch_shapes=[

time: 68.4 us -> 58.4 us (0.85)
  Pallas kernels: 40.6 us -> 30.4 us
    pallas_call x1, Pallas kernels: 29.1 us -> 18.8 us  [shards(): pl.pallas_call(functools.partial(solve_kernel, heads, step_blocks, blocks...]
  transfers between devices with their start and end apart: 11 -> 11, of which waited for: 1 -> 1; matrix products, arithmetic and copies ran while one was open for 1% -> 1% of each run, Pallas kernels for 47% -> 38%
where the time goes in v4:
time: 58.4 us; the launch traced here: 58.1 us
  Pallas kernels  30.4 us (52%)
  starting transfers between devices  20.8 us (36%)
  local copies, waits for them, and re-layouts  4.03 us (7%)
  waiting for transfers between devices  1.4 us (2%)
  other arithmetic  1.28 us (2%)
    pallas_call x1, Pallas kernels, shards(): pl.pallas_call(functools.partial(solve_kernel, heads, step_blocks, blocks...  18.8 us
    ppermute x8, starting transfers between devices, send(): return lax.ppermute(array, 'seq', perm)  14.2 us
    ppermute x3, starting transfers between devices, rows_from(): lax.ppermute(piece, 'head', [(i, (i + shift) % groups) for i in range(gro...  6.63 us
    pallas_call x1, Pallas kernels, shards(): pl.pallas_call(functools.partial(totals_kernel, half), grid=(2,), in_spec...  4.13 us
    pallas_call x1, Pallas kernels, shards(): pl.pallas_call(functools.partial(project_kernel, groups), grid_spec=pltpu...  4.12 us
    unnamed x22, local copies, waits for them, and re-layouts  3.92 us
    pallas_call x1, Pallas kernels, shards(): pl.pallas_call(functools.partial(local_kernel, blocks), grid=(heads,), in...  2.34 us
    ppermute x8, waiting for transfers between devices, send(): return lax.ppermute(array, 'seq', perm)  1.39 us
  transfers between devices with their start and end apart: 11, of which 1 were waited for; matrix products, arithmetic and copies ran while one was open for 1% of the time, Pallas kernels for 38%

profile of v4, /device:TPU:1, one launch (start us, length us, event | category | flops | bytes accessed | tf_op | source)
XLA Modules:
  0.0 58.1 jit_solution(17011850479835815707)
XLA Ops:
  0.0 0.0 copy-start
  0.0 0.0 copy-start.1
  0.0 4.1 %totals.1 = (f32[4,128,128]{2,1,0:T(8,128)}, f32[4,128,128]{2,1,0:T(8,128)}, bf16[4,128,1024]{2,1,0:T(8,128)(2,1)}, f32[4,1,1024]{2,1,0:T(1,128)}, f32[4,1,1024]{2,1,0:T(1,128)}) custom-call(s32[1]{0:T(128)} %bitcast.1.core_ref, bf16[1024,512]{1,0:T(8,128)(2,1)} %keys_ref.5, bf16[1024,512]{1,0:T(8,128)(2,1)} %values_ref.3, f32[4,1024]{1,0:T(4,128)} %bitcast.3), custom_call_target="tpu_custom_call" | custom-call | flops 5500000256 | bytes 5000000 | tf_op jit(solution)/shard_map/totals/pallas_call | solution.py:277
  4.1 1.5 %collective-permute-start = (f32[4,128,128]{2,1,0:T(8,128)}, f32[4,128,128]{2,1,0:T(8,128)S(1)}, u32[]{:S(2)}, u32[]{:S(2)}) collective-permute-start(f32[4,128,128]{2,1,0:T(8,128)} %get-tuple-element.27), channel_id=1, source_target_pairs={{0,4},{4,0},{8,12},{12,8},{16,20},{20,16},{24,28},{28,24},{32,36},... | collective-permute-start | bytes 786440 | tf_op jit(solution)/shard_map/ppermute | solution.py:261
  5.6 1.4 %collective-permute-done = f32[4,128,128]{2,1,0:T(8,128)S(1)} collective-permute-done((f32[4,128,128]{2,1,0:T(8,128)}, f32[4,128,128]{2,1,0:T(8,128)S(1)}, u32[]{:S(2)}, u32[]{:S(2)}) %collective-permute-start) | collective-permute-done | bytes 262176 | tf_op jit(solution)/shard_map/ppermute | solution.py:261
  7.0 1.0 %add_convert_fusion = f16[4,128,128]{2,1,0:T(8,128)(2,1)S(1)} fusion(f32[4,128,128]{2,1,0:T(8,128)} %get-tuple-element.26, f32[4,128,128]{2,1,0:T(8,128)S(1)} %collective-permute-done), kind=kLoop, calls=%fused_computation.12 | loop fusion | flops 131072 | bytes 655360 | tf_op jit(solution)/shard_map/convert_element_type | solution.py:298
  8.0 1.4 %collective-permute-start.1 = (f16[4,128,128]{2,1,0:T(8,128)(2,1)S(1)}, f16[4,128,128]{2,1,0:T(8,128)(2,1)S(1)}, u32[]{:S(2)}, u32[]{:S(2)}) collective-permute-start(f16[4,128,128]{2,1,0:T(8,128)(2,1)S(1)} %add_convert_fusion), channel_id=1, source_target_pairs={{0,8},{4,12},{8,16},{12,20},{16,24},{20,28},{24,0},{28,4},{32,40},... | collective-permute-start | bytes 393224 | tf_op jit(solution)/shard_map/ppermute | solution.py:261
  9.3 2.5 %collective-permute-start.2 = (f16[4,128,128]{2,1,0:T(8,128)(2,1)S(1)}, f16[4,128,128]{2,1,0:T(8,128)(2,1)S(1)}, u32[]{:S(2)}, u32[]{:S(2)}) collective-permute-start(f16[4,128,128]{2,1,0:T(8,128)(2,1)S(1)} %add_convert_fusion), channel_id=1, source_target_pairs={{0,16},{4,20},{8,24},{12,28},{16,0},{20,4},{24,8},{28,12},{32,48},... | collective-permute-start | bytes 393224 | tf_op jit(solution)/shard_map/ppermute | solution.py:261
  11.8 1.2 %collective-permute-start.3 = (f16[4,128,128]{2,1,0:T(8,128)(2,1)S(1)}, f16[4,128,128]{2,1,0:T(8,128)(2,1)S(1)}, u32[]{:S(2)}, u32[]{:S(2)}) collective-permute-start(f16[4,128,128]{2,1,0:T(8,128)(2,1)S(1)} %add_convert_fusion), channel_id=1, source_target_pairs={{0,24},{4,28},{8,0},{12,4},{16,8},{20,12},{24,16},{28,20},{32,56},... | collective-permute-start | bytes 393224 | tf_op jit(solution)/shard_map/ppermute | solution.py:261
  12.9 0.0 copy-done
  13.0 1.7 %collective-permute-start.8 = (bf16[512,512]{1,0:T(8,128)(2,1)S(1)}, bf16[512,512]{1,0:T(8,128)(2,1)S(1)}, u32[]{:S(2)}, u32[]{:S(2)}) collective-permute-start(bf16[512,512]{1,0:T(8,128)(2,1)S(1)} %constant_dynamic-slice_fusion.2), channel_id=1, source_target_pairs={{0,1},{1,2},{2,3},{3,0},{4,5},{5,6},{6,7},{7,4},{8,9},{9,10},{10,1... | collective-permute-start | bytes 1572872 | tf_op jit(solution)/shard_map/ppermute | solution.py:265
  14.7 0.0 copy-done.1
  14.7 0.0 copy-start.3
  14.7 1.2 %copy-done.3 = bf16[1024,512]{1,0:T(8,128)(2,1)S(1)} copy-done((bf16[1024,512]{1,0:T(8,128)(2,1)S(1)}, bf16[1024,512]{1,0:T(8,128)(2,1)}, u32[]{:S(2)}) %copy-start.3) | copy-done | bytes 1048600
  15.9 1.2 %copy-done.6 = bf16[4,128,1024]{2,1,0:T(8,128)(2,1)S(1)} copy-done((bf16[4,128,1024]{2,1,0:T(8,128)(2,1)S(1)}, bf16[4,128,1024]{2,1,0:T(8,128)(2,1)}, u32[]{:S(2)}) %copy-start.6) | copy-done | bytes 1048600
  17.1 0.7 %copy-done.8 = f32[4,1,1024]{2,1,0:T(1,128)S(1)} copy-done((f32[4,1,1024]{2,1,0:T(1,128)S(1)}, f32[4,1,1024]{2,1,0:T(1,128)}, u32[]{:S(2)}) %copy-start.8) | copy-done | bytes 16408
  17.8 0.7 %copy-done.9 = f32[4,1,1024]{2,1,0:T(1,128)S(1)} copy-done((f32[4,1,1024]{2,1,0:T(1,128)S(1)}, f32[4,1,1024]{2,1,0:T(1,128)}, u32[]{:S(2)}) %copy-start.9) | copy-done | bytes 16408
  18.6 2.3 %local.1 = (f32[4,8,128,128]{3,2,1,0:T(8,128)S(1)}, f32[4,8,128,128]{3,2,1,0:T(8,128)S(1)}, bf16[4,128,1024]{2,1,0:T(8,128)(2,1)S(1)}) custom-call(bf16[4,128,1024]{2,1,0:T(8,128)(2,1)S(1)} %copy-done.6, f32[4,1,1024]{2,1,0:T(1,128)S(1)} %copy-done.8, f32[4,1,1024]{2,1,0:T(1,128)S(1)} %copy-done.9, bf16[1024,512]{1,0:T(8,128)(2,1)S(1)} %copy-done.3, ...), custom_call_target="tpu_custom_call" | custom-call | flops 5500000256 | bytes 5000000 | tf_op jit(solution)/shard_map/local/pallas_call | solution.py:302
  20.9 0.0 collective-permute-done.1
  20.9 0.0 collective-permute-done.2
  20.9 0.0 collective-permute-done.3
  20.9 0.1 fusion.4
  21.0 0.0 copy-start.10
  21.0 1.4 %collective-permute-start.4 = (f16[4,128,128]{2,1,0:T(8,128)(2,1)S(1)}, f16[4,128,128]{2,1,0:T(8,128)(2,1)S(1)}, u32[]{:S(2)}, u32[]{:S(2)}) collective-permute-start(f16[4,128,128]{2,1,0:T(8,128)(2,1)S(1)} %fusion.4), channel_id=1, source_target_pairs={{0,32},{4,36},{8,40},{12,44},{16,48},{20,52},{24,56},{28,60},{32,6... | collective-permute-start | bytes 393224 | tf_op jit(solution)/shard_map/ppermute | solution.py:261
  22.4 2.6 %collective-permute-start.5 = (f16[4,128,128]{2,1,0:T(8,128)(2,1)S(1)}, f16[4,128,128]{2,1,0:T(8,128)(2,1)S(1)}, u32[]{:S(2)}, u32[]{:S(2)}) collective-permute-start(f16[4,128,128]{2,1,0:T(8,128)(2,1)S(1)} %fusion.4), channel_id=1, source_target_pairs={{0,64},{4,68},{8,72},{12,76},{16,80},{20,84},{24,88},{28,92},{32,9... | collective-permute-start | bytes 393224 | tf_op jit(solution)/shard_map/ppermute | solution.py:261
  25.0 1.1 %collective-permute-start.6 = (f16[4,128,128]{2,1,0:T(8,128)(2,1)S(1)}, f16[4,128,128]{2,1,0:T(8,128)(2,1)S(1)}, u32[]{:S(2)}, u32[]{:S(2)}) collective-permute-start(f16[4,128,128]{2,1,0:T(8,128)(2,1)S(1)} %fusion.4), channel_id=1, source_target_pairs={{0,96},{4,100},{8,104},{12,108},{16,112},{20,116},{24,120},{28,124... | collective-permute-start | bytes 393224 | tf_op jit(solution)/shard_map/ppermute | solution.py:261
  26.1 0.0 copy-done.2
  26.1 0.9 %columns.1 = (bf16[4,128,1024]{2,1,0:T(8,128)(2,1)S(1)}, f32[4,128,128]{2,1,0:T(8,128)S(1)}, f32[4,128,128]{2,1,0:T(8,128)S(1)}) custom-call(bf16[1024,512]{1,0:T(8,128)(2,1)S(1)} %copy-done.2, f32[4,1,1024]{2,1,0:T(1,128)S(1)} %copy-done.8, f32[4,1,1024]{2,1,0:T(1,128)S(1)} %copy-done.9), custom_call_target="tpu_custom_call" | custom-call | flops 3300000000 | bytes 3000000 | tf_op jit(solution)/shard_map/columns/pallas_call | solution.py:319
  27.0 0.0 copy-start.4
  27.0 0.0 copy-start.5
  27.1 0.0 copy-start.7
  27.1 3.4 %collective-permute-start.9 = (bf16[512,512]{1,0:T(8,128)(2,1)S(1)}, bf16[512,512]{1,0:T(8,128)(2,1)S(1)}, u32[]{:S(2)}, u32[]{:S(2)}) collective-permute-start(bf16[512,512]{1,0:T(8,128)(2,1)S(1)} %constant_dynamic-slice_fusion.1), channel_id=1, source_target_pairs={{0,2},{1,3},{2,0},{3,1},{4,6},{5,7},{6,4},{7,5},{8,10},{9,11},{10,... | collective-permute-start | bytes 1572872 | tf_op jit(solution)/shard_map/ppermute | solution.py:265
  30.5 0.0 collective-permute-done.4
  30.5 0.0 collective-permute-done.5
  30.5 0.0 collective-permute-done.6
  30.5 0.0 copy-done.10
  30.5 0.2 select_add_fusion
  30.7 2.7 %collective-permute-start.7 = (f32[4,128,128]{2,1,0:T(8,128)S(1)}, f32[4,128,128]{2,1,0:T(8,128)S(1)}, u32[]{:S(2)}, u32[]{:S(2)}) collective-permute-start(f32[4,128,128]{2,1,0:T(8,128)S(1)} %get-tuple-element.47), channel_id=1, source_target_pairs={{0,4},{4,0},{8,12},{12,8},{16,20},{20,16},{24,28},{28,24},{32,36},... | collective-permute-start | bytes 786440 | tf_op jit(solution)/shard_map/ppermute | solution.py:261
  33.4 1.5 %collective-permute-start.10 = (bf16[512,512]{1,0:T(8,128)(2,1)S(1)}, bf16[512,512]{1,0:T(8,128)(2,1)S(1)}, u32[]{:S(2)}, u32[]{:S(2)}) collective-permute-start(bf16[512,512]{1,0:T(8,128)(2,1)S(1)} %constant_dynamic-slice_fusion), channel_id=1, source_target_pairs={{0,3},{1,0},{2,1},{3,2},{4,7},{5,4},{6,5},{7,6},{8,11},{9,8},{10,9... | collective-permute-start | bytes 1572872 | tf_op jit(solution)/shard_map/ppermute | solution.py:265
  35.0 0.0 collective-permute-done.7.got_ref
  35.0 0.0 copy-done.4
  35.0 0.0 copy-done.5
  35.0 0.0 copy-done.7
  35.1 18.8 %solve.1.readout_ref = bf16[1024,512]{1,0:T(8,128)(2,1)S(1)} custom-call(s32[1]{0:T(128)} %bitcast.1.core_ref, f32[4]{0:T(128)S(1)} %copy-done.5, bf16[4,128,1024]{2,1,0:T(8,128)(2,1)S(1)} %get-tuple-element.34.queries_ref, bf16[1024,512]{1,0:T(8,128)(2,1)S(1)} %copy-done.4, bf16[4,128,1024]{2,1,0:T(8,128)(2,1)S(1)} %copy-done.7, ...), custom_call_target="tpu_custom_call" | custom-call | flops 32999999488 | bytes 30000000 | tf_op jit(solution)/shard_map/solve/pallas_call | solution.py:340
  53.9 0.0 collective-permute-done.8.rest_0_
  53.9 0.0 collective-permute-done.9.rest_1_
  53.9 0.0 collective-permute-done.10.rest_2_
  53.9 4.1 %project.1 = bf16[1,1024,2048]{2,1,0:T(8,128)(2,1)} custom-call(s32[1]{0:T(128)} %bitcast.group_ref, bf16[1024,512]{1,0:T(8,128)(2,1)S(1)} %solve.1.readout_ref, bf16[2048,512]{1,0:T(8,128)(2,1)S(1)} %copy-done, bf16[512,512]{1,0:T(8,128)(2,1)S(1)} %collective-permute-done.8.rest_0_, bf16[512,512]{1,0:T(8,128)(2,1)S(1)} %collective-permute-done.9.rest_1_, ...), custom_call_target="tpu_custom_call" | custom-call | flops 5500000256 | bytes 5000000 | tf_op jit(solution)/shard_map/project/pallas_call | solution.py:378
  (8 shorter events, 0.2 us)
Async XLA Ops:
  0.0 12.9 %copy-start = (bf16[2048,512]{1,0:T(8,128)(2,1)S(1)}, bf16[2048,512]{1,0:T(8,128)(2,1)}, u32[]{:S(2)}) copy-start(bf16[2048,512]{1,0:T(8,128)(2,1)} %own_ref.1) | copy-start | bytes 6291460
  0.0 14.7 %copy-start.1 = (bf16[1024,512]{1,0:T(8,128)(2,1)S(1)}, bf16[1024,512]{1,0:T(8,128)(2,1)}, u32[]{:S(2)}) copy-start(bf16[1024,512]{1,0:T(8,128)(2,1)} %values_ref.3) | copy-start | bytes 3145732
  4.1 2.8 %collective-permute-start = (f32[4,128,128]{2,1,0:T(8,128)}, f32[4,128,128]{2,1,0:T(8,128)S(1)}, u32[]{:S(2)}, u32[]{:S(2)}) collective-permute-start(f32[4,128,128]{2,1,0:T(8,128)} %get-tuple-element.27), channel_id=1, source_target_pairs={{0,4},{4,0},{8,12},{12,8},{16,20},{20,16},{24,28},{28,24},{32,36},... | collective-permute-start | bytes 786440 | tf_op jit(solution)/shard_map/ppermute | solution.py:261
  8.0 13.0 %collective-permute-start.1 = (f16[4,128,128]{2,1,0:T(8,128)(2,1)S(1)}, f16[4,128,128]{2,1,0:T(8,128)(2,1)S(1)}, u32[]{:S(2)}, u32[]{:S(2)}) collective-permute-start(f16[4,128,128]{2,1,0:T(8,128)(2,1)S(1)} %add_convert_fusion), channel_id=1, source_target_pairs={{0,8},{4,12},{8,16},{12,20},{16,24},{20,28},{24,0},{28,4},{32,40},... | collective-permute-start | bytes 393224 | tf_op jit(solution)/shard_map/ppermute | solution.py:261
  9.3 11.6 %collective-permute-start.2 = (f16[4,128,128]{2,1,0:T(8,128)(2,1)S(1)}, f16[4,128,128]{2,1,0:T(8,128)(2,1)S(1)}, u32[]{:S(2)}, u32[]{:S(2)}) collective-permute-start(f16[4,128,128]{2,1,0:T(8,128)(2,1)S(1)} %add_convert_fusion), channel_id=1, source_target_pairs={{0,16},{4,20},{8,24},{12,28},{16,0},{20,4},{24,8},{28,12},{32,48},... | collective-permute-start | bytes 393224 | tf_op jit(solution)/shard_map/ppermute | solution.py:261
  11.8 9.2 %collective-permute-start.3 = (f16[4,128,128]{2,1,0:T(8,128)(2,1)S(1)}, f16[4,128,128]{2,1,0:T(8,128)(2,1)S(1)}, u32[]{:S(2)}, u32[]{:S(2)}) collective-permute-start(f16[4,128,128]{2,1,0:T(8,128)(2,1)S(1)} %add_convert_fusion), channel_id=1, source_target_pairs={{0,24},{4,28},{8,0},{12,4},{16,8},{20,12},{24,16},{28,20},{32,56},... | collective-permute-start | bytes 393224 | tf_op jit(solution)/shard_map/ppermute | solution.py:261
  13.0 40.9 %collective-permute-start.8 = (bf16[512,512]{1,0:T(8,128)(2,1)S(1)}, bf16[512,512]{1,0:T(8,128)(2,1)S(1)}, u32[]{:S(2)}, u32[]{:S(2)}) collective-permute-start(bf16[512,512]{1,0:T(8,128)(2,1)S(1)} %constant_dynamic-slice_fusion.2), channel_id=1, source_target_pairs={{0,1},{1,2},{2,3},{3,0},{4,5},{5,6},{6,7},{7,4},{8,9},{9,10},{10,1... | collective-permute-start | bytes 1572872 | tf_op jit(solution)/shard_map/ppermute | solution.py:265
  14.7 1.2 %copy-start.3 = (bf16[1024,512]{1,0:T(8,128)(2,1)S(1)}, bf16[1024,512]{1,0:T(8,128)(2,1)}, u32[]{:S(2)}) copy-start(bf16[1024,512]{1,0:T(8,128)(2,1)} %keys_ref.5) | copy-start | bytes 3145732
  15.9 1.2 %copy-start.6 = (bf16[4,128,1024]{2,1,0:T(8,128)(2,1)S(1)}, bf16[4,128,1024]{2,1,0:T(8,128)(2,1)}, u32[]{:S(2)}) copy-start(bf16[4,128,1024]{2,1,0:T(8,128)(2,1)} %get-tuple-element.37.turned_ref) | copy-start | bytes 3145732
  17.1 0.7 %copy-start.8 = (f32[4,1,1024]{2,1,0:T(1,128)S(1)}, f32[4,1,1024]{2,1,0:T(1,128)}, u32[]{:S(2)}) copy-start(f32[4,1,1024]{2,1,0:T(1,128)} %get-tuple-element.32.scale_ref) | copy-start | bytes 49156
  17.8 0.7 %copy-start.9 = (f32[4,1,1024]{2,1,0:T(1,128)S(1)}, f32[4,1,1024]{2,1,0:T(1,128)}, u32[]{:S(2)}) copy-start(f32[4,1,1024]{2,1,0:T(1,128)} %get-tuple-element.33.gated_ref) | copy-start | bytes 49156
  18.6 7.5 %copy-start.2 = (bf16[1024,512]{1,0:T(8,128)(2,1)S(1)}, bf16[1024,512]{1,0:T(8,128)(2,1)}, u32[]{:S(2)}) copy-start(bf16[1024,512]{1,0:T(8,128)(2,1)} %queries_ref) | copy-start | bytes 3145732
  21.0 9.5 %copy-start.10 = (f32[4,128,128]{2,1,0:T(8,128)S(1)}, f32[4,128,128]{2,1,0:T(8,128)}, u32[]{:S(2)}) copy-start(f32[4,128,128]{2,1,0:T(8,128)} %get-tuple-element.26) | copy-start | bytes 786436
  21.0 9.5 %collective-permute-start.4 = (f16[4,128,128]{2,1,0:T(8,128)(2,1)S(1)}, f16[4,128,128]{2,1,0:T(8,128)(2,1)S(1)}, u32[]{:S(2)}, u32[]{:S(2)}) collective-permute-start(f16[4,128,128]{2,1,0:T(8,128)(2,1)S(1)} %fusion.4), channel_id=1, source_target_pairs={{0,32},{4,36},{8,40},{12,44},{16,48},{20,52},{24,56},{28,60},{32,6... | collective-permute-start | bytes 393224 | tf_op jit(solution)/shard_map/ppermute | solution.py:261
  22.4 8.1 %collective-permute-start.5 = (f16[4,128,128]{2,1,0:T(8,128)(2,1)S(1)}, f16[4,128,128]{2,1,0:T(8,128)(2,1)S(1)}, u32[]{:S(2)}, u32[]{:S(2)}) collective-permute-start(f16[4,128,128]{2,1,0:T(8,128)(2,1)S(1)} %fusion.4), channel_id=1, source_target_pairs={{0,64},{4,68},{8,72},{12,76},{16,80},{20,84},{24,88},{28,92},{32,9... | collective-permute-start | bytes 393224 | tf_op jit(solution)/shard_map/ppermute | solution.py:261
  25.0 5.5 %collective-permute-start.6 = (f16[4,128,128]{2,1,0:T(8,128)(2,1)S(1)}, f16[4,128,128]{2,1,0:T(8,128)(2,1)S(1)}, u32[]{:S(2)}, u32[]{:S(2)}) collective-permute-start(f16[4,128,128]{2,1,0:T(8,128)(2,1)S(1)} %fusion.4), channel_id=1, source_target_pairs={{0,96},{4,100},{8,104},{12,108},{16,112},{20,116},{24,120},{28,124... | collective-permute-start | bytes 393224 | tf_op jit(solution)/shard_map/ppermute | solution.py:261
  27.0 8.0 %copy-start.4 = (bf16[1024,512]{1,0:T(8,128)(2,1)S(1)}, bf16[1024,512]{1,0:T(8,128)(2,1)}, u32[]{:S(2)}) copy-start(bf16[1024,512]{1,0:T(8,128)(2,1)} %keys_ref.5) | copy-start | bytes 3145732
  27.0 8.0 %copy-start.5 = (f32[4]{0:T(128)S(1)}, f32[4]{0:T(128)}, u32[]{:S(2)}) copy-start(f32[4]{0:T(128)} %ridge_ref.1) | copy-start | bytes 52
  27.1 8.0 %copy-start.7 = (bf16[4,128,1024]{2,1,0:T(8,128)(2,1)S(1)}, bf16[4,128,1024]{2,1,0:T(8,128)(2,1)}, u32[]{:S(2)}) copy-start(bf16[4,128,1024]{2,1,0:T(8,128)(2,1)} %get-tuple-element.37.turned_ref) | copy-start | bytes 3145732
  27.1 26.8 %collective-permute-start.9 = (bf16[512,512]{1,0:T(8,128)(2,1)S(1)}, bf16[512,512]{1,0:T(8,128)(2,1)S(1)}, u32[]{:S(2)}, u32[]{:S(2)}) collective-permute-start(bf16[512,512]{1,0:T(8,128)(2,1)S(1)} %constant_dynamic-slice_fusion.1), channel_id=1, source_target_pairs={{0,2},{1,3},{2,0},{3,1},{4,6},{5,7},{6,4},{7,5},{8,10},{9,11},{10,... | collective-permute-start | bytes 1572872 | tf_op jit(solution)/shard_map/ppermute | solution.py:265
  30.7 4.3 %collective-permute-start.7 = (f32[4,128,128]{2,1,0:T(8,128)S(1)}, f32[4,128,128]{2,1,0:T(8,128)S(1)}, u32[]{:S(2)}, u32[]{:S(2)}) collective-permute-start(f32[4,128,128]{2,1,0:T(8,128)S(1)} %get-tuple-element.47), channel_id=1, source_target_pairs={{0,4},{4,0},{8,12},{12,8},{16,20},{20,16},{24,28},{28,24},{32,36},... | collective-permute-start | bytes 786440 | tf_op jit(solution)/shard_map/ppermute | solution.py:261
  33.4 20.5 %collective-permute-start.10 = (bf16[512,512]{1,0:T(8,128)(2,1)S(1)}, bf16[512,512]{1,0:T(8,128)(2,1)S(1)}, u32[]{:S(2)}, u32[]{:S(2)}) collective-permute-start(bf16[512,512]{1,0:T(8,128)(2,1)S(1)} %constant_dynamic-slice_fusion), channel_id=1, source_target_pairs={{0,3},{1,0},{2,1},{3,2},{4,7},{5,4},{6,5},{7,6},{8,11},{9,8},{10,9... | collective-permute-start | bytes 1572872 | tf_op jit(solution)/shard_map/ppermute | solution.py:265

commit v5 on v4

--- a/solution.py
+++ b/solution.py
@@ -31,7 +31,7 @@
 
 
 def totals_kernel(
-    half, core_ref, keys_ref, values_ref, gates_ref, mine_ref, theirs_ref, turned_ref, scale_ref, gated_ref
+    half, core_ref, keys_ref, values_ref, gates_ref, mine_ref, theirs_ref, turned_ref, factors_ref
 ):
     step = pl.program_id(0)
     lefts = []
@@ -43,8 +43,7 @@
         gate = gates_ref[pl.ds(step * half + head, 1), :]
         scale = gate / norm
         gated = gate * lax.rsqrt(norm)
-        scale_ref[head] = scale
-        gated_ref[head] = gated
+        factors_ref[head] = jnp.concatenate([scale, gated], axis=0)
         for factor in (scale, gated * (1.0 / SHRINK)):
             lefts.append(jnp.concatenate(two_terms(wide * factor), axis=0))
     grams = [dot(lefts[2 * head], keys_ref[:, head_cols(head)]) for head in range(half)]
@@ -63,7 +62,7 @@
             theirs_ref[at] = value
 
 
-def local_kernel(blocks, turned_ref, scale_ref, gated_ref, keys_ref, values_ref, gram_ref, moment_ref, values_turned_ref):
+def local_kernel(blocks, tag_ref, turned_ref, factors_ref, keys_ref, values_ref, gram_ref, moment_ref, values_turned_ref):
     values_turned_ref[0] = values_ref[...].T
     gram_ref[0, 0] = jnp.zeros((HD, HD), F32)
     moment_ref[0, 0] = jnp.zeros((HD, HD), F32)
@@ -71,9 +70,9 @@
     for block in range(blocks - 1):
         span = slice(block * SPAN, (block + 1) * SPAN)
         keys = turned_ref[0, :, span].astype(F32)
-        left = jnp.concatenate(two_terms(keys * scale_ref[0, :, span]), axis=0)
+        left = jnp.concatenate(two_terms(keys * factors_ref[0, :1, span]), axis=0)
         grams.append(dot(left, keys_ref[span, :]))
-        left = jnp.concatenate(two_terms(keys * gated_ref[0, :, span]), axis=0)
+        left = jnp.concatenate(two_terms(keys * factors_ref[0, 1:, span]), axis=0)
         moments.append(dot(left, values_ref[span, :]))
     for block in range(blocks - 1):
         gram, moment = grams[block], moments[block]
@@ -81,10 +80,10 @@
         moment_ref[0, block + 1] = moment_ref[0, block] + (moment[:HD] + moment[HD:]).T
 
 
-def columns_kernel(blocks, queries_ref, scale_ref, gated_ref, turned_ref, scale_out_ref, gated_out_ref):
+def columns_kernel(blocks, queries_ref, factors_ref, turned_ref, scale_ref, gated_ref):
     turned_ref[0] = queries_ref[...].T
-    for out_ref, factors in ((scale_out_ref, scale_ref), (gated_out_ref, gated_ref)):
-        spans = [factors[0, :, block * SPAN : (block + 1) * SPAN] for block in range(blocks)]
+    for at, out_ref in enumerate((scale_ref, gated_ref)):
+        spans = [factors_ref[0, at : at + 1, block * SPAN : (block + 1) * SPAN] for block in range(blocks)]
         spans += [jnp.zeros((1, SPAN), F32)] * (SPAN - blocks)
         out_ref[0] = jnp.concatenate(spans, axis=0).T
 
@@ -268,13 +267,12 @@
     by_head = pl.BlockSpec((tokens, HD), lambda h: (0, h))
     head_turned = pl.BlockSpec((1, HD, tokens), lambda h: (h, 0, 0))
     head_blocks = pl.BlockSpec((1, blocks, HD, HD), lambda h: (h, 0, 0, 0))
-    row = pl.BlockSpec((1, 1, tokens), lambda h: (h, 0, 0))
-    row_shape = jax.ShapeDtypeStruct((heads, 1, tokens), F32)
+    rows = pl.BlockSpec((1, 2, tokens), lambda h: (h, 0, 0))
+    rows_shape = jax.ShapeDtypeStruct((heads, 2, tokens), F32)
     turned_shape = jax.ShapeDtypeStruct((heads, HD, tokens), BF16)
     block_shape = jax.ShapeDtypeStruct((heads, blocks, HD, HD), F32)
     by_half = pl.BlockSpec((tokens, half * HD), lambda s: (0, s))
-    half_row = pl.BlockSpec((half, 1, tokens), lambda s: (s, 0, 0))
-    mine, theirs, keys_turned, scale, gated = pl.pallas_call(
+    mine, theirs, keys_turned, factors = pl.pallas_call(
         functools.partial(totals_kernel, half),
         grid=(2,),
         in_specs=[smem, by_half, by_half, whole((heads, tokens))],
@@ -282,10 +280,9 @@
             whole(sums),
             whole(sums),
             pl.BlockSpec((half, HD, tokens), lambda s: (s, 0, 0)),
-            half_row,
-            half_row,
+            pl.BlockSpec((half, 2, tokens), lambda s: (s, 0, 0)),
         ],
-        out_shape=[jax.ShapeDtypeStruct(sums, F32)] * 2 + [turned_shape, row_shape, row_shape],
+        out_shape=[jax.ShapeDtypeStruct(sums, F32)] * 2 + [turned_shape, rows_shape],
         compiler_params=params(60),
         cost_estimate=cost(5),
         name="totals",
@@ -296,19 +293,19 @@
 
     received = send(theirs, perm_core())
     chip = (mine + received).astype(F16)
-    chip, keys_turned_later, weight = lax.optimization_barrier((chip, keys_turned, out_weight))
+    chip, tag, weight = lax.optimization_barrier((chip, core_arg, out_weight))
     along = [send(chip, perm_x(shift)) for shift in range(1, side)]
     parts = [rows_from(1, weight)]
     local_gram, local_moment, values_turned = pl.pallas_call(
         functools.partial(local_kernel, blocks),
         grid=(heads,),
-        in_specs=[head_turned, row, row, by_head, by_head],
+        in_specs=[smem, head_turned, rows, by_head, by_head],
         out_specs=[head_blocks, head_blocks, head_turned],
         out_shape=[block_shape, block_shape, turned_shape],
         compiler_params=params(16),
         cost_estimate=cost(5),
         name="local",
-    )(keys_turned_later, scale, gated, keys, values)
+    )(tag, keys_turned, factors, keys, values)
 
     row_total = (chip.astype(F32) + sum(part.astype(F32) for part in along)).astype(F16)
     row_total, queries_later, weight = lax.optimization_barrier((row_total, queries, weight))
@@ -319,13 +316,13 @@
     queries_turned, scale_columns, gated_columns = pl.pallas_call(
         functools.partial(columns_kernel, blocks),
         grid=(heads,),
-        in_specs=[by_head, row, row],
+        in_specs=[by_head, rows],
         out_specs=[head_turned, columns_spec, columns_spec],
         out_shape=[turned_shape, columns_shape, columns_shape],
         compiler_params=params(16),
         cost_estimate=cost(3),
         name="columns",
-    )(queries_later, scale, gated)
+    )(queries_later, factors)
 
     above, weight = lax.optimization_barrier((above, weight))
     parts.append(rows_from(groups - 1, weight))

time: 58.4 us -> 57.6 us (0.986)
  local copies, waits for them, and re-layouts: 4.03 us -> 3.35 us
    unnamed x22 -> x20, local copies, waits for them, and re-layouts: 3.92 us -> 3.24 us
  transfers between devices with their start and end apart: 11 -> 11, of which waited for: 1 -> 1; matrix products, arithmetic and copies ran while one was open for 1% -> 1% of each run, Pallas kernels for 38% -> 39%
where the time goes in v5:
time: 57.6 us; the launch traced here: 57.4 us
  Pallas kernels  30.4 us (53%)
  starting transfers between devices  20.8 us (36%)
  local copies, waits for them, and re-layouts  3.35 us (6%)
  waiting for transfers between devices  1.4 us (2%)
  other arithmetic  1.28 us (2%)
    pallas_call x1, Pallas kernels, shards(): pl.pallas_call(functools.partial(solve_kernel, heads, step_blocks, blocks...  18.8 us
    ppermute x8, starting transfers between devices, send(): return lax.ppermute(array, 'seq', perm)  14.1 us
    ppermute x3, starting transfers between devices, rows_from(): lax.ppermute(piece, 'head', [(i, (i + shift) % groups) for i in range(gro...  6.64 us
    pallas_call x1, Pallas kernels, shards(): pl.pallas_call(functools.partial(totals_kernel, half), grid=(2,), in_spec...  4.13 us
    pallas_call x1, Pallas kernels, shards(): pl.pallas_call(functools.partial(project_kernel, groups), grid_spec=pltpu...  4.12 us
    unnamed x20, local copies, waits for them, and re-layouts  3.24 us
    pallas_call x1, Pallas kernels, shards(): pl.pallas_call(functools.partial(local_kernel, blocks), grid=(heads,), in...  2.35 us
    ppermute x8, waiting for transfers between devices, send(): return lax.ppermute(array, 'seq', perm)  1.39 us
  transfers between devices with their start and end apart: 11, of which 1 were waited for; matrix products, arithmetic and copies ran while one was open for 1% of the time, Pallas kernels for 39%

profile of v5, /device:TPU:1, one launch (start us, length us, event | category | flops | bytes accessed | tf_op | source)
XLA Modules:
  0.0 57.4 jit_solution(6024001846543507196)
XLA Ops:
  0.0 0.0 copy-start
  0.0 0.0 copy-start.1
  0.0 4.1 %totals.1 = (f32[4,128,128]{2,1,0:T(8,128)}, f32[4,128,128]{2,1,0:T(8,128)}, bf16[4,128,1024]{2,1,0:T(8,128)(2,1)}, f32[4,2,1024]{2,1,0:T(2,128)}) custom-call(s32[1]{0:T(128)} %bitcast.1.core_ref.tag_ref, bf16[1024,512]{1,0:T(8,128)(2,1)} %keys_ref.5, bf16[1024,512]{1,0:T(8,128)(2,1)} %values_ref.3, f32[4,1024]{1,0:T(4,128)} %bitcast.3), custom_call_target="tpu_custom_call" | custom-call | flops 5500000256 | bytes 5000000 | tf_op jit(solution)/shard_map/totals/pallas_call | solution.py:275
  4.1 1.4 %collective-permute-start = (f32[4,128,128]{2,1,0:T(8,128)}, f32[4,128,128]{2,1,0:T(8,128)S(1)}, u32[]{:S(2)}, u32[]{:S(2)}) collective-permute-start(f32[4,128,128]{2,1,0:T(8,128)} %get-tuple-element.26), channel_id=1, source_target_pairs={{0,4},{4,0},{8,12},{12,8},{16,20},{20,16},{24,28},{28,24},{32,36},... | collective-permute-start | bytes 786440 | tf_op jit(solution)/shard_map/ppermute | solution.py:260
  5.6 1.4 %collective-permute-done = f32[4,128,128]{2,1,0:T(8,128)S(1)} collective-permute-done((f32[4,128,128]{2,1,0:T(8,128)}, f32[4,128,128]{2,1,0:T(8,128)S(1)}, u32[]{:S(2)}, u32[]{:S(2)}) %collective-permute-start) | collective-permute-done | bytes 262176 | tf_op jit(solution)/shard_map/ppermute | solution.py:260
  6.9 1.0 %add_convert_fusion = f16[4,128,128]{2,1,0:T(8,128)(2,1)S(1)} fusion(f32[4,128,128]{2,1,0:T(8,128)} %get-tuple-element.25, f32[4,128,128]{2,1,0:T(8,128)S(1)} %collective-permute-done), kind=kLoop, calls=%fused_computation.12 | loop fusion | flops 131072 | bytes 655360 | tf_op jit(solution)/shard_map/convert_element_type | solution.py:295
  7.9 1.4 %collective-permute-start.1 = (f16[4,128,128]{2,1,0:T(8,128)(2,1)S(1)}, f16[4,128,128]{2,1,0:T(8,128)(2,1)S(1)}, u32[]{:S(2)}, u32[]{:S(2)}) collective-permute-start(f16[4,128,128]{2,1,0:T(8,128)(2,1)S(1)} %add_convert_fusion), channel_id=1, source_target_pairs={{0,8},{4,12},{8,16},{12,20},{16,24},{20,28},{24,0},{28,4},{32,40},... | collective-permute-start | bytes 393224 | tf_op jit(solution)/shard_map/ppermute | solution.py:260
  9.3 2.5 %collective-permute-start.2 = (f16[4,128,128]{2,1,0:T(8,128)(2,1)S(1)}, f16[4,128,128]{2,1,0:T(8,128)(2,1)S(1)}, u32[]{:S(2)}, u32[]{:S(2)}) collective-permute-start(f16[4,128,128]{2,1,0:T(8,128)(2,1)S(1)} %add_convert_fusion), channel_id=1, source_target_pairs={{0,16},{4,20},{8,24},{12,28},{16,0},{20,4},{24,8},{28,12},{32,48},... | collective-permute-start | bytes 393224 | tf_op jit(solution)/shard_map/ppermute | solution.py:260
  11.7 1.1 %collective-permute-start.3 = (f16[4,128,128]{2,1,0:T(8,128)(2,1)S(1)}, f16[4,128,128]{2,1,0:T(8,128)(2,1)S(1)}, u32[]{:S(2)}, u32[]{:S(2)}) collective-permute-start(f16[4,128,128]{2,1,0:T(8,128)(2,1)S(1)} %add_convert_fusion), channel_id=1, source_target_pairs={{0,24},{4,28},{8,0},{12,4},{16,8},{20,12},{24,16},{28,20},{32,56},... | collective-permute-start | bytes 393224 | tf_op jit(solution)/shard_map/ppermute | solution.py:260
  12.9 0.0 copy-done
  12.9 1.7 %collective-permute-start.8 = (bf16[512,512]{1,0:T(8,128)(2,1)S(1)}, bf16[512,512]{1,0:T(8,128)(2,1)S(1)}, u32[]{:S(2)}, u32[]{:S(2)}) collective-permute-start(bf16[512,512]{1,0:T(8,128)(2,1)S(1)} %constant_dynamic-slice_fusion.2), channel_id=1, source_target_pairs={{0,1},{1,2},{2,3},{3,0},{4,5},{5,6},{6,7},{7,4},{8,9},{9,10},{10,1... | collective-permute-start | bytes 1572872 | tf_op jit(solution)/shard_map/ppermute | solution.py:264
  14.6 0.0 copy-done.1
  14.6 1.2 %copy-done.3 = bf16[1024,512]{1,0:T(8,128)(2,1)S(1)} copy-done((bf16[1024,512]{1,0:T(8,128)(2,1)S(1)}, bf16[1024,512]{1,0:T(8,128)(2,1)}, u32[]{:S(2)}) %copy-start.3) | copy-done | bytes 1048600
  15.9 0.0 copy-start.6
  15.9 1.2 %copy-done.6 = bf16[4,128,1024]{2,1,0:T(8,128)(2,1)S(1)} copy-done((bf16[4,128,1024]{2,1,0:T(8,128)(2,1)S(1)}, bf16[4,128,1024]{2,1,0:T(8,128)(2,1)}, u32[]{:S(2)}) %copy-start.6) | copy-done | bytes 1048600
  17.1 0.0 copy-start.8
  17.1 0.8 %copy-done.8 = f32[4,2,1024]{2,1,0:T(2,128)S(1)} copy-done((f32[4,2,1024]{2,1,0:T(2,128)S(1)}, f32[4,2,1024]{2,1,0:T(2,128)}, u32[]{:S(2)}) %copy-start.8) | copy-done | bytes 32792
  17.9 2.4 %local.1 = (f32[4,8,128,128]{3,2,1,0:T(8,128)S(1)}, f32[4,8,128,128]{3,2,1,0:T(8,128)S(1)}, bf16[4,128,1024]{2,1,0:T(8,128)(2,1)S(1)}) custom-call(s32[1]{0:T(128)} %bitcast.1.core_ref.tag_ref, bf16[4,128,1024]{2,1,0:T(8,128)(2,1)S(1)} %copy-done.6, f32[4,2,1024]{2,1,0:T(2,128)S(1)} %copy-done.8, bf16[1024,512]{1,0:T(8,128)(2,1)S(1)} %copy-done.3, ...), custom_call_target="tpu_custom_call" | custom-call | flops 5500000256 | bytes 5000000 | tf_op jit(solution)/shard_map/local/pallas_call | solution.py:299
  20.2 0.0 collective-permute-done.1
  20.2 0.0 collective-permute-done.2
  20.2 0.0 collective-permute-done.3
  20.2 0.1 fusion.4
  20.3 0.0 copy-start.9
  20.3 1.4 %collective-permute-start.4 = (f16[4,128,128]{2,1,0:T(8,128)(2,1)S(1)}, f16[4,128,128]{2,1,0:T(8,128)(2,1)S(1)}, u32[]{:S(2)}, u32[]{:S(2)}) collective-permute-start(f16[4,128,128]{2,1,0:T(8,128)(2,1)S(1)} %fusion.4), channel_id=1, source_target_pairs={{0,32},{4,36},{8,40},{12,44},{16,48},{20,52},{24,56},{28,60},{32,6... | collective-permute-start | bytes 393224 | tf_op jit(solution)/shard_map/ppermute | solution.py:260
  21.7 2.6 %collective-permute-start.5 = (f16[4,128,128]{2,1,0:T(8,128)(2,1)S(1)}, f16[4,128,128]{2,1,0:T(8,128)(2,1)S(1)}, u32[]{:S(2)}, u32[]{:S(2)}) collective-permute-start(f16[4,128,128]{2,1,0:T(8,128)(2,1)S(1)} %fusion.4), channel_id=1, source_target_pairs={{0,64},{4,68},{8,72},{12,76},{16,80},{20,84},{24,88},{28,92},{32,9... | collective-permute-start | bytes 393224 | tf_op jit(solution)/shard_map/ppermute | solution.py:260
  24.3 1.1 %collective-permute-start.6 = (f16[4,128,128]{2,1,0:T(8,128)(2,1)S(1)}, f16[4,128,128]{2,1,0:T(8,128)(2,1)S(1)}, u32[]{:S(2)}, u32[]{:S(2)}) collective-permute-start(f16[4,128,128]{2,1,0:T(8,128)(2,1)S(1)} %fusion.4), channel_id=1, source_target_pairs={{0,96},{4,100},{8,104},{12,108},{16,112},{20,116},{24,120},{28,124... | collective-permute-start | bytes 393224 | tf_op jit(solution)/shard_map/ppermute | solution.py:260
  25.4 0.0 copy-done.2
  25.4 0.9 %columns.1 = (bf16[4,128,1024]{2,1,0:T(8,128)(2,1)S(1)}, f32[4,128,128]{2,1,0:T(8,128)S(1)}, f32[4,128,128]{2,1,0:T(8,128)S(1)}) custom-call(bf16[1024,512]{1,0:T(8,128)(2,1)S(1)} %copy-done.2, f32[4,2,1024]{2,1,0:T(2,128)S(1)} %copy-done.8), custom_call_target="tpu_custom_call" | custom-call | flops 3300000000 | bytes 3000000 | tf_op jit(solution)/shard_map/columns/pallas_call | solution.py:316
  26.3 0.0 copy-start.4
  26.3 0.0 copy-start.5
  26.4 0.0 copy-start.7
  26.4 3.4 %collective-permute-start.9 = (bf16[512,512]{1,0:T(8,128)(2,1)S(1)}, bf16[512,512]{1,0:T(8,128)(2,1)S(1)}, u32[]{:S(2)}, u32[]{:S(2)}) collective-permute-start(bf16[512,512]{1,0:T(8,128)(2,1)S(1)} %constant_dynamic-slice_fusion.1), channel_id=1, source_target_pairs={{0,2},{1,3},{2,0},{3,1},{4,6},{5,7},{6,4},{7,5},{8,10},{9,11},{10,... | collective-permute-start | bytes 1572872 | tf_op jit(solution)/shard_map/ppermute | solution.py:264
  29.8 0.0 collective-permute-done.4
  29.8 0.0 collective-permute-done.5
  29.8 0.0 collective-permute-done.6
  29.8 0.0 copy-done.9
  29.8 0.2 select_add_fusion
  30.0 2.7 %collective-permute-start.7 = (f32[4,128,128]{2,1,0:T(8,128)S(1)}, f32[4,128,128]{2,1,0:T(8,128)S(1)}, u32[]{:S(2)}, u32[]{:S(2)}) collective-permute-start(f32[4,128,128]{2,1,0:T(8,128)S(1)} %get-tuple-element.45), channel_id=1, source_target_pairs={{0,4},{4,0},{8,12},{12,8},{16,20},{20,16},{24,28},{28,24},{32,36},... | collective-permute-start | bytes 786440 | tf_op jit(solution)/shard_map/ppermute | solution.py:260
  32.7 1.5 %collective-permute-start.10 = (bf16[512,512]{1,0:T(8,128)(2,1)S(1)}, bf16[512,512]{1,0:T(8,128)(2,1)S(1)}, u32[]{:S(2)}, u32[]{:S(2)}) collective-permute-start(bf16[512,512]{1,0:T(8,128)(2,1)S(1)} %constant_dynamic-slice_fusion), channel_id=1, source_target_pairs={{0,3},{1,0},{2,1},{3,2},{4,7},{5,4},{6,5},{7,6},{8,11},{9,8},{10,9... | collective-permute-start | bytes 1572872 | tf_op jit(solution)/shard_map/ppermute | solution.py:264
  34.3 0.0 collective-permute-done.7.got_ref
  34.3 0.0 copy-done.4
  34.3 0.0 copy-done.5
  34.3 0.0 copy-done.7
  34.4 18.8 %solve.1.readout_ref = bf16[1024,512]{1,0:T(8,128)(2,1)S(1)} custom-call(s32[1]{0:T(128)} %bitcast.1.core_ref.tag_ref, f32[4]{0:T(128)S(1)} %copy-done.5, bf16[4,128,1024]{2,1,0:T(8,128)(2,1)S(1)} %get-tuple-element.31.queries_ref, bf16[1024,512]{1,0:T(8,128)(2,1)S(1)} %copy-done.4, bf16[4,128,1024]{2,1,0:T(8,128)(2,1)S(1)} %copy-done.7, ...), custom_call_target="tpu_custom_call" | custom-call | flops 32999999488 | bytes 30000000 | tf_op jit(solution)/shard_map/solve/pallas_call | solution.py:337
  53.2 0.0 collective-permute-done.8.rest_0_
  53.2 0.0 collective-permute-done.9.rest_1_
  53.2 0.0 collective-permute-done.10.rest_2_
  53.2 4.1 %project.1 = bf16[1,1024,2048]{2,1,0:T(8,128)(2,1)} custom-call(s32[1]{0:T(128)} %bitcast.group_ref, bf16[1024,512]{1,0:T(8,128)(2,1)S(1)} %solve.1.readout_ref, bf16[2048,512]{1,0:T(8,128)(2,1)S(1)} %copy-done, bf16[512,512]{1,0:T(8,128)(2,1)S(1)} %collective-permute-done.8.rest_0_, bf16[512,512]{1,0:T(8,128)(2,1)S(1)} %collective-permute-done.9.rest_1_, ...), custom_call_target="tpu_custom_call" | custom-call | flops 5500000256 | bytes 5000000 | tf_op jit(solution)/shard_map/project/pallas_call | solution.py:375
  (6 shorter events, 0.2 us)
Async XLA Ops:
  0.0 12.9 %copy-start = (bf16[2048,512]{1,0:T(8,128)(2,1)S(1)}, bf16[2048,512]{1,0:T(8,128)(2,1)}, u32[]{:S(2)}) copy-start(bf16[2048,512]{1,0:T(8,128)(2,1)} %own_ref.1) | copy-start | bytes 6291460
  0.0 14.6 %copy-start.1 = (bf16[1024,512]{1,0:T(8,128)(2,1)S(1)}, bf16[1024,512]{1,0:T(8,128)(2,1)}, u32[]{:S(2)}) copy-start(bf16[1024,512]{1,0:T(8,128)(2,1)} %values_ref.3) | copy-start | bytes 3145732
  4.1 2.8 %collective-permute-start = (f32[4,128,128]{2,1,0:T(8,128)}, f32[4,128,128]{2,1,0:T(8,128)S(1)}, u32[]{:S(2)}, u32[]{:S(2)}) collective-permute-start(f32[4,128,128]{2,1,0:T(8,128)} %get-tuple-element.26), channel_id=1, source_target_pairs={{0,4},{4,0},{8,12},{12,8},{16,20},{20,16},{24,28},{28,24},{32,36},... | collective-permute-start | bytes 786440 | tf_op jit(solution)/shard_map/ppermute | solution.py:260
  7.9 12.3 %collective-permute-start.1 = (f16[4,128,128]{2,1,0:T(8,128)(2,1)S(1)}, f16[4,128,128]{2,1,0:T(8,128)(2,1)S(1)}, u32[]{:S(2)}, u32[]{:S(2)}) collective-permute-start(f16[4,128,128]{2,1,0:T(8,128)(2,1)S(1)} %add_convert_fusion), channel_id=1, source_target_pairs={{0,8},{4,12},{8,16},{12,20},{16,24},{20,28},{24,0},{28,4},{32,40},... | collective-permute-start | bytes 393224 | tf_op jit(solution)/shard_map/ppermute | solution.py:260
  9.3 10.9 %collective-permute-start.2 = (f16[4,128,128]{2,1,0:T(8,128)(2,1)S(1)}, f16[4,128,128]{2,1,0:T(8,128)(2,1)S(1)}, u32[]{:S(2)}, u32[]{:S(2)}) collective-permute-start(f16[4,128,128]{2,1,0:T(8,128)(2,1)S(1)} %add_convert_fusion), channel_id=1, source_target_pairs={{0,16},{4,20},{8,24},{12,28},{16,0},{20,4},{24,8},{28,12},{32,48},... | collective-permute-start | bytes 393224 | tf_op jit(solution)/shard_map/ppermute | solution.py:260
  11.7 8.5 %collective-permute-start.3 = (f16[4,128,128]{2,1,0:T(8,128)(2,1)S(1)}, f16[4,128,128]{2,1,0:T(8,128)(2,1)S(1)}, u32[]{:S(2)}, u32[]{:S(2)}) collective-permute-start(f16[4,128,128]{2,1,0:T(8,128)(2,1)S(1)} %add_convert_fusion), channel_id=1, source_target_pairs={{0,24},{4,28},{8,0},{12,4},{16,8},{20,12},{24,16},{28,20},{32,56},... | collective-permute-start | bytes 393224 | tf_op jit(solution)/shard_map/ppermute | solution.py:260
  12.9 40.3 %collective-permute-start.8 = (bf16[512,512]{1,0:T(8,128)(2,1)S(1)}, bf16[512,512]{1,0:T(8,128)(2,1)S(1)}, u32[]{:S(2)}, u32[]{:S(2)}) collective-permute-start(bf16[512,512]{1,0:T(8,128)(2,1)S(1)} %constant_dynamic-slice_fusion.2), channel_id=1, source_target_pairs={{0,1},{1,2},{2,3},{3,0},{4,5},{5,6},{6,7},{7,4},{8,9},{9,10},{10,1... | collective-permute-start | bytes 1572872 | tf_op jit(solution)/shard_map/ppermute | solution.py:264
  14.6 1.2 %copy-start.3 = (bf16[1024,512]{1,0:T(8,128)(2,1)S(1)}, bf16[1024,512]{1,0:T(8,128)(2,1)}, u32[]{:S(2)}) copy-start(bf16[1024,512]{1,0:T(8,128)(2,1)} %keys_ref.5) | copy-start | bytes 3145732
  15.9 1.2 %copy-start.6 = (bf16[4,128,1024]{2,1,0:T(8,128)(2,1)S(1)}, bf16[4,128,1024]{2,1,0:T(8,128)(2,1)}, u32[]{:S(2)}) copy-start(bf16[4,128,1024]{2,1,0:T(8,128)(2,1)} %get-tuple-element.32.turned_ref) | copy-start | bytes 3145732
  17.1 0.8 %copy-start.8 = (f32[4,2,1024]{2,1,0:T(2,128)S(1)}, f32[4,2,1024]{2,1,0:T(2,128)}, u32[]{:S(2)}) copy-start(f32[4,2,1024]{2,1,0:T(2,128)} %get-tuple-element.30.factors_ref) | copy-start | bytes 98308
  17.9 7.5 %copy-start.2 = (bf16[1024,512]{1,0:T(8,128)(2,1)S(1)}, bf16[1024,512]{1,0:T(8,128)(2,1)}, u32[]{:S(2)}) copy-start(bf16[1024,512]{1,0:T(8,128)(2,1)} %queries_ref) | copy-start | bytes 3145732
  20.3 9.5 %copy-start.9 = (f32[4,128,128]{2,1,0:T(8,128)S(1)}, f32[4,128,128]{2,1,0:T(8,128)}, u32[]{:S(2)}) copy-start(f32[4,128,128]{2,1,0:T(8,128)} %get-tuple-element.25) | copy-start | bytes 786436
  20.3 9.5 %collective-permute-start.4 = (f16[4,128,128]{2,1,0:T(8,128)(2,1)S(1)}, f16[4,128,128]{2,1,0:T(8,128)(2,1)S(1)}, u32[]{:S(2)}, u32[]{:S(2)}) collective-permute-start(f16[4,128,128]{2,1,0:T(8,128)(2,1)S(1)} %fusion.4), channel_id=1, source_target_pairs={{0,32},{4,36},{8,40},{12,44},{16,48},{20,52},{24,56},{28,60},{32,6... | collective-permute-start | bytes 393224 | tf_op jit(solution)/shard_map/ppermute | solution.py:260
  21.7 8.1 %collective-permute-start.5 = (f16[4,128,128]{2,1,0:T(8,128)(2,1)S(1)}, f16[4,128,128]{2,1,0:T(8,128)(2,1)S(1)}, u32[]{:S(2)}, u32[]{:S(2)}) collective-permute-start(f16[4,128,128]{2,1,0:T(8,128)(2,1)S(1)} %fusion.4), channel_id=1, source_target_pairs={{0,64},{4,68},{8,72},{12,76},{16,80},{20,84},{24,88},{28,92},{32,9... | collective-permute-start | bytes 393224 | tf_op jit(solution)/shard_map/ppermute | solution.py:260
  24.3 5.5 %collective-permute-start.6 = (f16[4,128,128]{2,1,0:T(8,128)(2,1)S(1)}, f16[4,128,128]{2,1,0:T(8,128)(2,1)S(1)}, u32[]{:S(2)}, u32[]{:S(2)}) collective-permute-start(f16[4,128,128]{2,1,0:T(8,128)(2,1)S(1)} %fusion.4), channel_id=1, source_target_pairs={{0,96},{4,100},{8,104},{12,108},{16,112},{20,116},{24,120},{28,124... | collective-permute-start | bytes 393224 | tf_op jit(solution)/shard_map/ppermute | solution.py:260
  26.3 8.0 %copy-start.4 = (bf16[1024,512]{1,0:T(8,128)(2,1)S(1)}, bf16[1024,512]{1,0:T(8,128)(2,1)}, u32[]{:S(2)}) copy-start(bf16[1024,512]{1,0:T(8,128)(2,1)} %keys_ref.5) | copy-start | bytes 3145732
  26.3 8.0 %copy-start.5 = (f32[4]{0:T(128)S(1)}, f32[4]{0:T(128)}, u32[]{:S(2)}) copy-start(f32[4]{0:T(128)} %ridge_ref.1) | copy-start | bytes 52
  26.4 8.0 %copy-start.7 = (bf16[4,128,1024]{2,1,0:T(8,128)(2,1)S(1)}, bf16[4,128,1024]{2,1,0:T(8,128)(2,1)}, u32[]{:S(2)}) copy-start(bf16[4,128,1024]{2,1,0:T(8,128)(2,1)} %get-tuple-element.32.turned_ref) | copy-start | bytes 3145732
  26.4 26.8 %collective-permute-start.9 = (bf16[512,512]{1,0:T(8,128)(2,1)S(1)}, bf16[512,512]{1,0:T(8,128)(2,1)S(1)}, u32[]{:S(2)}, u32[]{:S(2)}) collective-permute-start(bf16[512,512]{1,0:T(8,128)(2,1)S(1)} %constant_dynamic-slice_fusion.1), channel_id=1, source_target_pairs={{0,2},{1,3},{2,0},{3,1},{4,6},{5,7},{6,4},{7,5},{8,10},{9,11},{10,... | collective-permute-start | bytes 1572872 | tf_op jit(solution)/shard_map/ppermute | solution.py:264
  30.0 4.3 %collective-permute-start.7 = (f32[4,128,128]{2,1,0:T(8,128)S(1)}, f32[4,128,128]{2,1,0:T(8,128)S(1)}, u32[]{:S(2)}, u32[]{:S(2)}) collective-permute-start(f32[4,128,128]{2,1,0:T(8,128)S(1)} %get-tuple-element.45), channel_id=1, source_target_pairs={{0,4},{4,0},{8,12},{12,8},{16,20},{20,16},{24,28},{28,24},{32,36},... | collective-permute-start | bytes 786440 | tf_op jit(solution)/shard_map/ppermute | solution.py:260
  32.7 20.5 %collective-permute-start.10 = (bf16[512,512]{1,0:T(8,128)(2,1)S(1)}, bf16[512,512]{1,0:T(8,128)(2,1)S(1)}, u32[]{:S(2)}, u32[]{:S(2)}) collective-permute-start(bf16[512,512]{1,0:T(8,128)(2,1)S(1)} %constant_dynamic-slice_fusion), channel_id=1, source_target_pairs={{0,3},{1,0},{2,1},{3,2},{4,7},{5,4},{6,5},{7,6},{8,11},{9,8},{10,9... | collective-permute-start | bytes 1572872 | tf_op jit(solution)/shard_map/ppermute | solution.py:264

commit v6 on v5

--- a/solution.py
+++ b/solution.py
@@ -62,14 +62,14 @@
             theirs_ref[at] = value
 
 
-def local_kernel(blocks, tag_ref, turned_ref, factors_ref, keys_ref, values_ref, gram_ref, moment_ref, values_turned_ref):
+def local_kernel(blocks, tag_ref, factors_ref, keys_ref, values_ref, gram_ref, moment_ref, values_turned_ref):
     values_turned_ref[0] = values_ref[...].T
     gram_ref[0, 0] = jnp.zeros((HD, HD), F32)
     moment_ref[0, 0] = jnp.zeros((HD, HD), F32)
     grams, moments = [], []
     for block in range(blocks - 1):
         span = slice(block * SPAN, (block + 1) * SPAN)
-        keys = turned_ref[0, :, span].astype(F32)
+        keys = keys_ref[span, :].T.astype(F32)
         left = jnp.concatenate(two_terms(keys * factors_ref[0, :1, span]), axis=0)
         grams.append(dot(left, keys_ref[span, :]))
         left = jnp.concatenate(two_terms(keys * factors_ref[0, 1:, span]), axis=0)
@@ -299,13 +299,13 @@
     local_gram, local_moment, values_turned = pl.pallas_call(
         functools.partial(local_kernel, blocks),
         grid=(heads,),
-        in_specs=[smem, head_turned, rows, by_head, by_head],
+        in_specs=[smem, rows, by_head, by_head],
         out_specs=[head_blocks, head_blocks, head_turned],
         out_shape=[block_shape, block_shape, turned_shape],
         compiler_params=params(16),
         cost_estimate=cost(5),
         name="local",
-    )(tag, keys_turned, factors, keys, values)
+    )(tag, factors, keys, values)
 
     row_total = (chip.astype(F32) + sum(part.astype(F32) for part in along)).astype(F16)
     row_total, queries_later, weight = lax.optimization_barrier((row_total, queries, weight))

time: 57.6 us -> 56.8 us (0.986)
  local copies, waits for them, and re-layouts: 3.35 us -> 2.13 us
    unnamed x20 -> x18, local copies, waits for them, and re-layouts: 3.24 us -> 2.02 us
where the time goes in v6:
time: 56.8 us; the launch traced here: 56.5 us
  Pallas kernels  30.5 us (54%)
  starting transfers between devices  21 us (37%)
  local copies, waits for them, and re-layouts  2.13 us (4%)
  waiting for transfers between devices  1.4 us (2%)
  other arithmetic  1.28 us (2%)
    pallas_call x1, Pallas kernels, shards(): pl.pallas_call(functools.partial(solve_kernel, heads, step_blocks, blocks...  18.8 us
    ppermute x8, starting transfers between devices, send(): return lax.ppermute(array, 'seq', perm)  14.1 us
    ppermute x3, starting transfers between devices, rows_from(): lax.ppermute(piece, 'head', [(i, (i + shift) % groups) for i in range(gro...  6.87 us
    pallas_call x1, Pallas kernels, shards(): pl.pallas_call(functools.partial(totals_kernel, half), grid=(2,), in_spec...  4.13 us
    pallas_call x1, Pallas kernels, shards(): pl.pallas_call(functools.partial(project_kernel, groups), grid_spec=pltpu...  4.12 us
    pallas_call x1, Pallas kernels, shards(): pl.pallas_call(functools.partial(local_kernel, blocks), grid=(heads,), in...  2.51 us
    unnamed x18, local copies, waits for them, and re-layouts  2.02 us
    ppermute x8, waiting for transfers between devices, send(): return lax.ppermute(array, 'seq', perm)  1.39 us
  transfers between devices with their start and end apart: 11, of which 1 were waited for; matrix products, arithmetic and copies ran while one was open for 1% of the time, Pallas kernels for 39%

profile of v6, /device:TPU:1, one launch (start us, length us, event | category | flops | bytes accessed | tf_op | source)
XLA Modules:
  0.0 56.5 jit_solution(8991956109416637035)
XLA Ops:
  0.0 0.0 copy-start
  0.0 0.0 copy-start.1
  0.0 4.1 %totals.1 = (f32[4,128,128]{2,1,0:T(8,128)}, f32[4,128,128]{2,1,0:T(8,128)}, bf16[4,128,1024]{2,1,0:T(8,128)(2,1)}, f32[4,2,1024]{2,1,0:T(2,128)}) custom-call(s32[1]{0:T(128)} %bitcast.1.core_ref.tag_ref, bf16[1024,512]{1,0:T(8,128)(2,1)} %keys_ref.5, bf16[1024,512]{1,0:T(8,128)(2,1)} %values_ref.3, f32[4,1024]{1,0:T(4,128)} %bitcast.3), custom_call_target="tpu_custom_call" | custom-call | flops 5500000256 | bytes 5000000 | tf_op jit(solution)/shard_map/totals/pallas_call | solution.py:275
  4.1 1.4 %collective-permute-start = (f32[4,128,128]{2,1,0:T(8,128)}, f32[4,128,128]{2,1,0:T(8,128)S(1)}, u32[]{:S(2)}, u32[]{:S(2)}) collective-permute-start(f32[4,128,128]{2,1,0:T(8,128)} %get-tuple-element.26), channel_id=1, source_target_pairs={{0,4},{4,0},{8,12},{12,8},{16,20},{20,16},{24,28},{28,24},{32,36},... | collective-permute-start | bytes 786440 | tf_op jit(solution)/shard_map/ppermute | solution.py:260
  5.6 1.4 %collective-permute-done = f32[4,128,128]{2,1,0:T(8,128)S(1)} collective-permute-done((f32[4,128,128]{2,1,0:T(8,128)}, f32[4,128,128]{2,1,0:T(8,128)S(1)}, u32[]{:S(2)}, u32[]{:S(2)}) %collective-permute-start) | collective-permute-done | bytes 262176 | tf_op jit(solution)/shard_map/ppermute | solution.py:260
  6.9 1.0 %add_convert_fusion = f16[4,128,128]{2,1,0:T(8,128)(2,1)S(1)} fusion(f32[4,128,128]{2,1,0:T(8,128)} %get-tuple-element.25, f32[4,128,128]{2,1,0:T(8,128)S(1)} %collective-permute-done), kind=kLoop, calls=%fused_computation.12 | loop fusion | flops 131072 | bytes 655360 | tf_op jit(solution)/shard_map/convert_element_type | solution.py:295
  7.9 1.4 %collective-permute-start.1 = (f16[4,128,128]{2,1,0:T(8,128)(2,1)S(1)}, f16[4,128,128]{2,1,0:T(8,128)(2,1)S(1)}, u32[]{:S(2)}, u32[]{:S(2)}) collective-permute-start(f16[4,128,128]{2,1,0:T(8,128)(2,1)S(1)} %add_convert_fusion), channel_id=1, source_target_pairs={{0,8},{4,12},{8,16},{12,20},{16,24},{20,28},{24,0},{28,4},{32,40},... | collective-permute-start | bytes 393224 | tf_op jit(solution)/shard_map/ppermute | solution.py:260
  9.3 2.5 %collective-permute-start.2 = (f16[4,128,128]{2,1,0:T(8,128)(2,1)S(1)}, f16[4,128,128]{2,1,0:T(8,128)(2,1)S(1)}, u32[]{:S(2)}, u32[]{:S(2)}) collective-permute-start(f16[4,128,128]{2,1,0:T(8,128)(2,1)S(1)} %add_convert_fusion), channel_id=1, source_target_pairs={{0,16},{4,20},{8,24},{12,28},{16,0},{20,4},{24,8},{28,12},{32,48},... | collective-permute-start | bytes 393224 | tf_op jit(solution)/shard_map/ppermute | solution.py:260
  11.7 1.1 %collective-permute-start.3 = (f16[4,128,128]{2,1,0:T(8,128)(2,1)S(1)}, f16[4,128,128]{2,1,0:T(8,128)(2,1)S(1)}, u32[]{:S(2)}, u32[]{:S(2)}) collective-permute-start(f16[4,128,128]{2,1,0:T(8,128)(2,1)S(1)} %add_convert_fusion), channel_id=1, source_target_pairs={{0,24},{4,28},{8,0},{12,4},{16,8},{20,12},{24,16},{28,20},{32,56},... | collective-permute-start | bytes 393224 | tf_op jit(solution)/shard_map/ppermute | solution.py:260
  12.9 0.0 copy-done
  12.9 1.7 %collective-permute-start.8 = (bf16[512,512]{1,0:T(8,128)(2,1)S(1)}, bf16[512,512]{1,0:T(8,128)(2,1)S(1)}, u32[]{:S(2)}, u32[]{:S(2)}) collective-permute-start(bf16[512,512]{1,0:T(8,128)(2,1)S(1)} %constant_dynamic-slice_fusion.2), channel_id=1, source_target_pairs={{0,1},{1,2},{2,3},{3,0},{4,5},{5,6},{6,7},{7,4},{8,9},{9,10},{10,1... | collective-permute-start | bytes 1572872 | tf_op jit(solution)/shard_map/ppermute | solution.py:264
  14.6 0.0 copy-done.1
  14.6 0.0 copy-start.3
  14.6 1.2 %copy-done.3 = bf16[1024,512]{1,0:T(8,128)(2,1)S(1)} copy-done((bf16[1024,512]{1,0:T(8,128)(2,1)S(1)}, bf16[1024,512]{1,0:T(8,128)(2,1)}, u32[]{:S(2)}) %copy-start.3) | copy-done | bytes 1048600
  15.9 0.0 copy-start.7
  15.9 0.8 %copy-done.7 = f32[4,2,1024]{2,1,0:T(2,128)S(1)} copy-done((f32[4,2,1024]{2,1,0:T(2,128)S(1)}, f32[4,2,1024]{2,1,0:T(2,128)}, u32[]{:S(2)}) %copy-start.7) | copy-done | bytes 32792
  16.6 0.0 copy-start.2
  16.6 2.5 %local.1 = (f32[4,8,128,128]{3,2,1,0:T(8,128)S(1)}, f32[4,8,128,128]{3,2,1,0:T(8,128)S(1)}, bf16[4,128,1024]{2,1,0:T(8,128)(2,1)S(1)}) custom-call(s32[1]{0:T(128)} %bitcast.1.core_ref.tag_ref, f32[4,2,1024]{2,1,0:T(2,128)S(1)} %copy-done.7, bf16[1024,512]{1,0:T(8,128)(2,1)S(1)} %copy-done.3, bf16[1024,512]{1,0:T(8,128)(2,1)S(1)} %copy-done.1), custom_call_target="tpu_custom_call" | custom-call | flops 5500000256 | bytes 5000000 | tf_op jit(solution)/shard_map/local/pallas_call | solution.py:299
  19.2 0.0 collective-permute-done.1
  19.2 0.0 collective-permute-done.2
  19.2 0.0 collective-permute-done.3
  19.2 0.1 fusion.4
  19.3 0.0 copy-start.8
  19.3 1.4 %collective-permute-start.4 = (f16[4,128,128]{2,1,0:T(8,128)(2,1)S(1)}, f16[4,128,128]{2,1,0:T(8,128)(2,1)S(1)}, u32[]{:S(2)}, u32[]{:S(2)}) collective-permute-start(f16[4,128,128]{2,1,0:T(8,128)(2,1)S(1)} %fusion.4), channel_id=1, source_target_pairs={{0,32},{4,36},{8,40},{12,44},{16,48},{20,52},{24,56},{28,60},{32,6... | collective-permute-start | bytes 393224 | tf_op jit(solution)/shard_map/ppermute | solution.py:260
  20.6 2.6 %collective-permute-start.5 = (f16[4,128,128]{2,1,0:T(8,128)(2,1)S(1)}, f16[4,128,128]{2,1,0:T(8,128)(2,1)S(1)}, u32[]{:S(2)}, u32[]{:S(2)}) collective-permute-start(f16[4,128,128]{2,1,0:T(8,128)(2,1)S(1)} %fusion.4), channel_id=1, source_target_pairs={{0,64},{4,68},{8,72},{12,76},{16,80},{20,84},{24,88},{28,92},{32,9... | collective-permute-start | bytes 393224 | tf_op jit(solution)/shard_map/ppermute | solution.py:260
  23.3 1.1 %collective-permute-start.6 = (f16[4,128,128]{2,1,0:T(8,128)(2,1)S(1)}, f16[4,128,128]{2,1,0:T(8,128)(2,1)S(1)}, u32[]{:S(2)}, u32[]{:S(2)}) collective-permute-start(f16[4,128,128]{2,1,0:T(8,128)(2,1)S(1)} %fusion.4), channel_id=1, source_target_pairs={{0,96},{4,100},{8,104},{12,108},{16,112},{20,116},{24,120},{28,124... | collective-permute-start | bytes 393224 | tf_op jit(solution)/shard_map/ppermute | solution.py:260
  24.3 0.0 copy-done.2
  24.3 0.9 %columns.1 = (bf16[4,128,1024]{2,1,0:T(8,128)(2,1)S(1)}, f32[4,128,128]{2,1,0:T(8,128)S(1)}, f32[4,128,128]{2,1,0:T(8,128)S(1)}) custom-call(bf16[1024,512]{1,0:T(8,128)(2,1)S(1)} %copy-done.2, f32[4,2,1024]{2,1,0:T(2,128)S(1)} %copy-done.7), custom_call_target="tpu_custom_call" | custom-call | flops 3300000000 | bytes 3000000 | tf_op jit(solution)/shard_map/columns/pallas_call | solution.py:316
  25.3 0.0 copy-start.4
  25.3 0.0 copy-start.5
  25.3 0.0 copy-start.6
  25.4 3.4 %collective-permute-start.9 = (bf16[512,512]{1,0:T(8,128)(2,1)S(1)}, bf16[512,512]{1,0:T(8,128)(2,1)S(1)}, u32[]{:S(2)}, u32[]{:S(2)}) collective-permute-start(bf16[512,512]{1,0:T(8,128)(2,1)S(1)} %constant_dynamic-slice_fusion.1), channel_id=1, source_target_pairs={{0,2},{1,3},{2,0},{3,1},{4,6},{5,7},{6,4},{7,5},{8,10},{9,11},{10,... | collective-permute-start | bytes 1572872 | tf_op jit(solution)/shard_map/ppermute | solution.py:264
  28.7 0.0 collective-permute-done.4
  28.7 0.0 collective-permute-done.5
  28.7 0.0 collective-permute-done.6
  28.8 0.0 copy-done.8
  28.8 0.2 select_add_fusion
  28.9 2.7 %collective-permute-start.7 = (f32[4,128,128]{2,1,0:T(8,128)S(1)}, f32[4,128,128]{2,1,0:T(8,128)S(1)}, u32[]{:S(2)}, u32[]{:S(2)}) collective-permute-start(f32[4,128,128]{2,1,0:T(8,128)S(1)} %get-tuple-element.45), channel_id=1, source_target_pairs={{0,4},{4,0},{8,12},{12,8},{16,20},{20,16},{24,28},{28,24},{32,36},... | collective-permute-start | bytes 786440 | tf_op jit(solution)/shard_map/ppermute | solution.py:260
  31.7 1.8 %collective-permute-start.10 = (bf16[512,512]{1,0:T(8,128)(2,1)S(1)}, bf16[512,512]{1,0:T(8,128)(2,1)S(1)}, u32[]{:S(2)}, u32[]{:S(2)}) collective-permute-start(bf16[512,512]{1,0:T(8,128)(2,1)S(1)} %constant_dynamic-slice_fusion), channel_id=1, source_target_pairs={{0,3},{1,0},{2,1},{3,2},{4,7},{5,4},{6,5},{7,6},{8,11},{9,8},{10,9... | collective-permute-start | bytes 1572872 | tf_op jit(solution)/shard_map/ppermute | solution.py:264
  33.5 0.0 collective-permute-done.7.got_ref
  33.5 0.0 copy-done.4
  33.5 0.0 copy-done.5
  33.5 0.0 copy-done.6
  33.5 18.8 %solve.1.readout_ref = bf16[1024,512]{1,0:T(8,128)(2,1)S(1)} custom-call(s32[1]{0:T(128)} %bitcast.1.core_ref.tag_ref, f32[4]{0:T(128)S(1)} %copy-done.5, bf16[4,128,1024]{2,1,0:T(8,128)(2,1)S(1)} %get-tuple-element.31.queries_ref, bf16[1024,512]{1,0:T(8,128)(2,1)S(1)} %copy-done.4, bf16[4,128,1024]{2,1,0:T(8,128)(2,1)S(1)} %copy-done.6, ...), custom_call_target="tpu_custom_call" | custom-call | flops 32999999488 | bytes 30000000 | tf_op jit(solution)/shard_map/solve/pallas_call | solution.py:337
  52.4 0.0 collective-permute-done.8.rest_0_
  52.4 0.0 collective-permute-done.9.rest_1_
  52.4 0.0 collective-permute-done.10.rest_2_
  52.4 4.1 %project.1 = bf16[1,1024,2048]{2,1,0:T(8,128)(2,1)} custom-call(s32[1]{0:T(128)} %bitcast.group_ref, bf16[1024,512]{1,0:T(8,128)(2,1)S(1)} %solve.1.readout_ref, bf16[2048,512]{1,0:T(8,128)(2,1)S(1)} %copy-done, bf16[512,512]{1,0:T(8,128)(2,1)S(1)} %collective-permute-done.8.rest_0_, bf16[512,512]{1,0:T(8,128)(2,1)S(1)} %collective-permute-done.9.rest_1_, ...), custom_call_target="tpu_custom_call" | custom-call | flops 5500000256 | bytes 5000000 | tf_op jit(solution)/shard_map/project/pallas_call | solution.py:375
  (4 shorter events, 0.1 us)
Async XLA Ops:
  0.0 12.9 %copy-start = (bf16[2048,512]{1,0:T(8,128)(2,1)S(1)}, bf16[2048,512]{1,0:T(8,128)(2,1)}, u32[]{:S(2)}) copy-start(bf16[2048,512]{1,0:T(8,128)(2,1)} %own_ref.1) | copy-start | bytes 6291460
  0.0 14.6 %copy-start.1 = (bf16[1024,512]{1,0:T(8,128)(2,1)S(1)}, bf16[1024,512]{1,0:T(8,128)(2,1)}, u32[]{:S(2)}) copy-start(bf16[1024,512]{1,0:T(8,128)(2,1)} %values_ref.3) | copy-start | bytes 3145732
  4.1 2.8 %collective-permute-start = (f32[4,128,128]{2,1,0:T(8,128)}, f32[4,128,128]{2,1,0:T(8,128)S(1)}, u32[]{:S(2)}, u32[]{:S(2)}) collective-permute-start(f32[4,128,128]{2,1,0:T(8,128)} %get-tuple-element.26), channel_id=1, source_target_pairs={{0,4},{4,0},{8,12},{12,8},{16,20},{20,16},{24,28},{28,24},{32,36},... | collective-permute-start | bytes 786440 | tf_op jit(solution)/shard_map/ppermute | solution.py:260
  7.9 11.2 %collective-permute-start.1 = (f16[4,128,128]{2,1,0:T(8,128)(2,1)S(1)}, f16[4,128,128]{2,1,0:T(8,128)(2,1)S(1)}, u32[]{:S(2)}, u32[]{:S(2)}) collective-permute-start(f16[4,128,128]{2,1,0:T(8,128)(2,1)S(1)} %add_convert_fusion), channel_id=1, source_target_pairs={{0,8},{4,12},{8,16},{12,20},{16,24},{20,28},{24,0},{28,4},{32,40},... | collective-permute-start | bytes 393224 | tf_op jit(solution)/shard_map/ppermute | solution.py:260
  9.3 9.9 %collective-permute-start.2 = (f16[4,128,128]{2,1,0:T(8,128)(2,1)S(1)}, f16[4,128,128]{2,1,0:T(8,128)(2,1)S(1)}, u32[]{:S(2)}, u32[]{:S(2)}) collective-permute-start(f16[4,128,128]{2,1,0:T(8,128)(2,1)S(1)} %add_convert_fusion), channel_id=1, source_target_pairs={{0,16},{4,20},{8,24},{12,28},{16,0},{20,4},{24,8},{28,12},{32,48},... | collective-permute-start | bytes 393224 | tf_op jit(solution)/shard_map/ppermute | solution.py:260
  11.7 7.4 %collective-permute-start.3 = (f16[4,128,128]{2,1,0:T(8,128)(2,1)S(1)}, f16[4,128,128]{2,1,0:T(8,128)(2,1)S(1)}, u32[]{:S(2)}, u32[]{:S(2)}) collective-permute-start(f16[4,128,128]{2,1,0:T(8,128)(2,1)S(1)} %add_convert_fusion), channel_id=1, source_target_pairs={{0,24},{4,28},{8,0},{12,4},{16,8},{20,12},{24,16},{28,20},{32,56},... | collective-permute-start | bytes 393224 | tf_op jit(solution)/shard_map/ppermute | solution.py:260
  12.9 39.4 %collective-permute-start.8 = (bf16[512,512]{1,0:T(8,128)(2,1)S(1)}, bf16[512,512]{1,0:T(8,128)(2,1)S(1)}, u32[]{:S(2)}, u32[]{:S(2)}) collective-permute-start(bf16[512,512]{1,0:T(8,128)(2,1)S(1)} %constant_dynamic-slice_fusion.2), channel_id=1, source_target_pairs={{0,1},{1,2},{2,3},{3,0},{4,5},{5,6},{6,7},{7,4},{8,9},{9,10},{10,1... | collective-permute-start | bytes 1572872 | tf_op jit(solution)/shard_map/ppermute | solution.py:264
  14.6 1.2 %copy-start.3 = (bf16[1024,512]{1,0:T(8,128)(2,1)S(1)}, bf16[1024,512]{1,0:T(8,128)(2,1)}, u32[]{:S(2)}) copy-start(bf16[1024,512]{1,0:T(8,128)(2,1)} %keys_ref.5) | copy-start | bytes 3145732
  15.9 0.8 %copy-start.7 = (f32[4,2,1024]{2,1,0:T(2,128)S(1)}, f32[4,2,1024]{2,1,0:T(2,128)}, u32[]{:S(2)}) copy-start(f32[4,2,1024]{2,1,0:T(2,128)} %get-tuple-element.30.factors_ref) | copy-start | bytes 98308
  16.6 7.7 %copy-start.2 = (bf16[1024,512]{1,0:T(8,128)(2,1)S(1)}, bf16[1024,512]{1,0:T(8,128)(2,1)}, u32[]{:S(2)}) copy-start(bf16[1024,512]{1,0:T(8,128)(2,1)} %queries_ref) | copy-start | bytes 3145732
  19.3 9.5 %copy-start.8 = (f32[4,128,128]{2,1,0:T(8,128)S(1)}, f32[4,128,128]{2,1,0:T(8,128)}, u32[]{:S(2)}) copy-start(f32[4,128,128]{2,1,0:T(8,128)} %get-tuple-element.25) | copy-start | bytes 786436
  19.3 9.5 %collective-permute-start.4 = (f16[4,128,128]{2,1,0:T(8,128)(2,1)S(1)}, f16[4,128,128]{2,1,0:T(8,128)(2,1)S(1)}, u32[]{:S(2)}, u32[]{:S(2)}) collective-permute-start(f16[4,128,128]{2,1,0:T(8,128)(2,1)S(1)} %fusion.4), channel_id=1, source_target_pairs={{0,32},{4,36},{8,40},{12,44},{16,48},{20,52},{24,56},{28,60},{32,6... | collective-permute-start | bytes 393224 | tf_op jit(solution)/shard_map/ppermute | solution.py:260
  20.6 8.1 %collective-permute-start.5 = (f16[4,128,128]{2,1,0:T(8,128)(2,1)S(1)}, f16[4,128,128]{2,1,0:T(8,128)(2,1)S(1)}, u32[]{:S(2)}, u32[]{:S(2)}) collective-permute-start(f16[4,128,128]{2,1,0:T(8,128)(2,1)S(1)} %fusion.4), channel_id=1, source_target_pairs={{0,64},{4,68},{8,72},{12,76},{16,80},{20,84},{24,88},{28,92},{32,9... | collective-permute-start | bytes 393224 | tf_op jit(solution)/shard_map/ppermute | solution.py:260
  23.3 5.5 %collective-permute-start.6 = (f16[4,128,128]{2,1,0:T(8,128)(2,1)S(1)}, f16[4,128,128]{2,1,0:T(8,128)(2,1)S(1)}, u32[]{:S(2)}, u32[]{:S(2)}) collective-permute-start(f16[4,128,128]{2,1,0:T(8,128)(2,1)S(1)} %fusion.4), channel_id=1, source_target_pairs={{0,96},{4,100},{8,104},{12,108},{16,112},{20,116},{24,120},{28,124... | collective-permute-start | bytes 393224 | tf_op jit(solution)/shard_map/ppermute | solution.py:260
  25.3 8.2 %copy-start.4 = (bf16[1024,512]{1,0:T(8,128)(2,1)S(1)}, bf16[1024,512]{1,0:T(8,128)(2,1)}, u32[]{:S(2)}) copy-start(bf16[1024,512]{1,0:T(8,128)(2,1)} %keys_ref.5) | copy-start | bytes 3145732
  25.3 8.2 %copy-start.5 = (f32[4]{0:T(128)S(1)}, f32[4]{0:T(128)}, u32[]{:S(2)}) copy-start(f32[4]{0:T(128)} %ridge_ref.1) | copy-start | bytes 52
  25.3 8.2 %copy-start.6 = (bf16[4,128,1024]{2,1,0:T(8,128)(2,1)S(1)}, bf16[4,128,1024]{2,1,0:T(8,128)(2,1)}, u32[]{:S(2)}) copy-start(bf16[4,128,1024]{2,1,0:T(8,128)(2,1)} %get-tuple-element.32.turned_ref) | copy-start | bytes 3145732
  25.4 27.0 %collective-permute-start.9 = (bf16[512,512]{1,0:T(8,128)(2,1)S(1)}, bf16[512,512]{1,0:T(8,128)(2,1)S(1)}, u32[]{:S(2)}, u32[]{:S(2)}) collective-permute-start(bf16[512,512]{1,0:T(8,128)(2,1)S(1)} %constant_dynamic-slice_fusion.1), channel_id=1, source_target_pairs={{0,2},{1,3},{2,0},{3,1},{4,6},{5,7},{6,4},{7,5},{8,10},{9,11},{10,... | collective-permute-start | bytes 1572872 | tf_op jit(solution)/shard_map/ppermute | solution.py:264
  28.9 4.5 %collective-permute-start.7 = (f32[4,128,128]{2,1,0:T(8,128)S(1)}, f32[4,128,128]{2,1,0:T(8,128)S(1)}, u32[]{:S(2)}, u32[]{:S(2)}) collective-permute-start(f32[4,128,128]{2,1,0:T(8,128)S(1)} %get-tuple-element.45), channel_id=1, source_target_pairs={{0,4},{4,0},{8,12},{12,8},{16,20},{20,16},{24,28},{28,24},{32,36},... | collective-permute-start | bytes 786440 | tf_op jit(solution)/shard_map/ppermute | solution.py:260
  31.7 20.7 %collective-permute-start.10 = (bf16[512,512]{1,0:T(8,128)(2,1)S(1)}, bf16[512,512]{1,0:T(8,128)(2,1)S(1)}, u32[]{:S(2)}, u32[]{:S(2)}) collective-permute-start(bf16[512,512]{1,0:T(8,128)(2,1)S(1)} %constant_dynamic-slice_fusion), channel_id=1, source_target_pairs={{0,3},{1,0},{2,1},{3,2},{4,7},{5,4},{6,5},{7,6},{8,11},{9,8},{10,9... | collective-permute-start | bytes 1572872 | tf_op jit(solution)/shard_map/ppermute | solution.py:264
